TPU v7x, 32 devices: a whole 2x2x4 slice. The times are simulated.
32 devices in a mesh: grp: 2 (over x), gx: 8 (over z, y), gy: 2 (over core).
Axes of the slice: x: 2, y: 2, z: 4, core: 2. Of those that a mesh axis runs over, the one named last changes fastest.
Arguments:
- mode_shapes: float32 [36, 64, 32, 256], P('grp', 'gx', 'gy'), parts along dimension 0, may hold values from -2.5 to 2.5
- eigenvalues: float32 [12], P('grp'), parts along dimension 0, may hold values from 2 to 20
- density: float32 [128, 32, 256], P(('grp', 'gx'), 'gy'), parts along dimension 0, may hold values from 0.1 to 1
- filter_mass: float32 [128, 32, 256], P(('grp', 'gx'), 'gy'), parts along dimension 0, may hold values from 0.5 to 4
- passive: int32 [128, 32, 256], P(('grp', 'gx'), 'gy'), parts along dimension 0, may hold values 0 or 1
Outputs:
- filtered: float32 [12, 64, 32, 256], P('grp', 'gx', 'gy'), parts along dimension 0
There are 2 independent parts, one for each index of `grp`. A program takes and returns all parts, laid end to end along the dimension named above; each array names one. Nothing has to cross between parts.
All inputs are finite; a program needn't handle non-finite values. No bound on the sum of `passive` on one device may be relied on, other than what follows from the above.
Results may differ from a plain program's by a relative error of at most 0.0001.
Values sent between devices are 32-bit elements; how exact they have to be, the bound alone decides.
No kernel may reach another device: no remote copies, remote signals or barrier semaphores. Data moves between devices by JAX's collectives and lax.ppermute only.
A program may use at most 128 MiB of HBM per device.

v0:
```python
import math
from functools import partial

import jax
import jax.numpy as jnp
import numpy as np
from jax import lax
from jax.experimental import pallas as pl
from jax.experimental.pallas import tpu as pltpu
from jax.sharding import PartitionSpec as P

ITERS = 3
RMIN = 4
RADIUS_SQ = RMIN * RMIN / 12.0
DOWN = 3
UP = 2


void_floor = 0.001


def element_table():
    poisson = 0.3
    lame_first = poisson / ((1.0 + poisson) * (1.0 - 2.0 * poisson))
    shear_mod = 1.0 / (2.0 * (1.0 + poisson))
    elastic = np.zeros((6, 6))
    elastic[:3, :3] = lame_first
    for entry in range(3):
        elastic[entry, entry] += 2.0 * shear_mod
        elastic[entry + 3, entry + 3] = shear_mod
    offset = 1.0 / math.sqrt(3.0)
    gauss_points = [(1.0 - offset) / 2.0, (1.0 + offset) / 2.0]
    stiffness = np.zeros((24, 24))
    inertia = np.zeros((24, 24))
    for point_x in gauss_points:
        for point_y in gauss_points:
            for point_z in gauss_points:
                coords = [point_x, point_y, point_z]
                values = np.zeros(8)
                gradient = np.zeros((8, 3))
                for corner in range(8):
                    corner_bits = [corner % 2, corner // 2 % 2, corner // 4]
                    factors = [
                        coords[dimen] if corner_bits[dimen] else 1.0 - coords[dimen]
                        for dimen in range(3)
                    ]
                    sign_list = [1.0 if corner_bits[dimen] else -1.0 for dimen in range(3)]
                    values[corner] = factors[0] * factors[1] * factors[2]
                    for dimen in range(3):
                        others = [
                            factors[other_dim] for other_dim in range(3) if other_dim != dimen
                        ]
                        gradient[corner, dimen] = sign_list[dimen] * others[0] * others[1]
                strain = np.zeros((6, 24))
                for corner in range(8):
                    column = 3 * corner
                    grad_x, grad_y, grad_z = gradient[corner]
                    strain[0, column] = grad_x
                    strain[1, column + 1] = grad_y
                    strain[2, column + 2] = grad_z
                    strain[3, column] = grad_y
                    strain[3, column + 1] = grad_x
                    strain[4, column + 1] = grad_z
                    strain[4, column + 2] = grad_y
                    strain[5, column] = grad_z
                    strain[5, column + 2] = grad_x
                stiffness += 0.125 * strain.T @ elastic @ strain
                shape_matrix = np.kron(values[None, :], np.eye(3))
                inertia += 0.125 * shape_matrix.T @ shape_matrix
    return stiffness, inertia


def energy_classes():
    stiffness, inertia = element_table()
    pair = np.array([[1.0, 1.0], [-1.0, 1.0]])
    basis = np.kron(np.kron(np.kron(pair, pair), pair), np.eye(3))
    stiffness = basis @ stiffness @ basis.T / 64.0
    inertia = basis @ inertia @ basis.T / 64.0
    squares, products = {}, {}
    for i in range(24):
        key = (round(stiffness[i, i], 9), round(inertia[i, i], 9))
        squares.setdefault(key, []).append(i)
        for j in range(i + 1, 24):
            if abs(stiffness[i, j]) > 1e-9:
                products.setdefault(round(stiffness[i, j], 9), []).append((i, j))
    squares = [
        (float(stiffness[v[0], v[0]]) if abs(k[0]) > 1e-9 else 0.0, float(inertia[v[0], v[0]]), v)
        for k, v in squares.items()
    ]
    products = [(2.0 * float(stiffness[v[0]]), v) for v in products.values()]
    return squares, products


def element_energies(entries, squares, products):
    stiff, inert = None, {}
    for weight, mass, members in squares:
        total = entries[members[0]] * entries[members[0]]
        for i in members[1:]:
            total = total + entries[i] * entries[i]
        if weight:
            stiff = total * weight if stiff is None else stiff + total * weight
        inert[mass] = inert[mass] + total if mass in inert else total
    for weight, members in products:
        total = entries[members[0][0]] * entries[members[0][1]]
        for i, j in members[1:]:
            total = total + entries[i] * entries[j]
        stiff = stiff + weight * total
    return stiff, sum(total * mass for mass, total in inert.items())


def shifted(value, step, dim):
    size = value.shape[dim]
    index = lax.broadcasted_iota(jnp.int32, value.shape, dim)
    edge = size - 1 if step > 0 else 0
    return jnp.where(index == edge, 0.0, pltpu.roll(value, (-step) % size, dim))


def missing_plane(shape):
    count = jnp.zeros(shape, jnp.float32)
    for dim in (0, 1):
        index = lax.broadcasted_iota(jnp.int32, shape, dim)
        count += (index == 0).astype(jnp.float32) + (index == shape[dim] - 1).astype(jnp.float32)
    return count


def scalar(flag):
    return jnp.where(flag, 1.0, 0.0).astype(jnp.float32)


def neighbour_count(missing, x, layers, first, last):
    count = 6.0 - missing
    if x == 0:
        count -= scalar(first)
    if x == layers - 1:
        count -= scalar(last)
    return count


def halves(core, half):
    return pl.multiple_of(core * half, half), pl.multiple_of((1 - core) * half, half)


def pack_kernel(place, modes, density, mass, passive, straight, crossed, swap, field, sems):
    group, layers = modes.shape[0] // 2, modes.shape[1]
    core = place[0]
    mine, theirs = core * group, (1 - core) * group
    copies = [
        pltpu.make_async_copy(modes.at[pl.ds(mine, group), 0], straight.at[pl.ds(0, group)], sems.at[0]),
        pltpu.make_async_copy(modes.at[pl.ds(theirs, group), 0], crossed.at[pl.ds(0, group)], sems.at[1]),
    ]
    copies += [
        pltpu.make_async_copy(modes.at[theirs + i], swap.at[pl.ds(i * layers, layers)], sems.at[2 + i])
        for i in range(group)
    ]
    for copy in copies:
        copy.start()
    base = group * layers
    for x in range(layers):
        rho, weight = density[x], mass[x]
        design = (1 - passive[x]).astype(jnp.float32)
        slope = 3.0 * (1.0 - void_floor) * rho * rho * design
        for k, value in enumerate((slope, weight, design)):
            swap[base + k * layers + x] = value
            field[k * layers + x] = value
        if x < 2:
            straight[group + x] = weight
            crossed[group + x] = weight
    for copy in copies:
        copy.wait()


def energy_kernel(low, high, end, *refs):
    place, eig, modes, swap, field = refs[:5]
    refs = refs[5:]
    if end:
        (halo, halo_swap, _, z_out, mass_out, ghost_mass), refs = refs[:6], refs[6:]
    else:
        (_, z_out, mass_out), refs = refs[:3], refs[3:]
    nodes, fields, sums, sems = refs
    layers, half, depth = modes.shape[1:]
    group = modes.shape[0] // 2
    width, count = 2 * half, high - low
    core, first, last = place[0], place[1], place[2]
    mine, other = halves(core, half)
    start = core * group
    copies = []

    def move(source, target):
        copy = pltpu.make_async_copy(source, target, sems.at[len(copies)])
        copy.start()
        copies.append(copy)

    base = group * layers
    for k in range(3):
        move(field.at[pl.ds(k * layers + low, count)], fields.at[k, :, pl.ds(mine, half), :])
        move(swap.at[pl.ds(base + k * layers + low, count)], fields.at[k, :, pl.ds(other, half), :])
    held = count if end else count + 1
    move(modes.at[pl.ds(start, group), pl.ds(low, held)], nodes.at[:, pl.ds(0, held), pl.ds(mine, half), :])
    for i in range(group):
        move(swap.at[pl.ds(i * layers + low, held)], nodes.at[i, pl.ds(0, held), pl.ds(other, half), :])
    if end:
        move(halo.at[pl.ds(0, group)], nodes.at[:, count, pl.ds(mine, half), :])
        move(halo_swap.at[pl.ds(0, group)], nodes.at[:, count, pl.ds(other, half), :])
        move(halo.at[pl.ds(group, 2)], ghost_mass.at[:, pl.ds(mine, half), :])
        move(halo_swap.at[pl.ds(group, 2)], ghost_mass.at[:, pl.ds(other, half), :])
    for copy in copies:
        copy.wait()

    squares, products = energy_classes()
    missing = missing_plane((width, depth))
    for i in range(count):
        mass = fields[1, i]
        mass_out[i] = mass
        inverse = 1.0 / (mass + RADIUS_SQ * neighbour_count(missing, low + i, layers, first, last))
        fields[0, i] = fields[0, i] * inverse
        fields[2, i] = fields[2, i] * inverse
    if end:
        z_out[z_out.shape[0] - 1] = fields[1, count - 1]

    def transform(mode, i):
        for comp in range(3):
            here = nodes[3 * mode + comp, i]
            above = shifted(here, 1, 1)
            for z, value in ((0, here + above), (1, above - here)):
                beside = shifted(value, 1, 0)
                sums[i % 3, 4 * comp + 2 * z] = value + beside
                sums[i % 3, 4 * comp + 2 * z + 1] = beside - value

    def energies(mode, value, i):
        for row in range(0, width, 8):
            for lane in range(0, depth, 128):
                span = (pl.ds(row, 8), pl.ds(lane, 128))
                entries = [None] * 24
                for comp in range(3):
                    for z in (0, 1):
                        for y in (0, 1):
                            near = sums[(i % 3, 4 * comp + 2 * z + y) + span]
                            far = sums[((i + 1) % 3, 4 * comp + 2 * z + y) + span]
                            entries[3 * (2 * y + 4 * z) + comp] = near + far
                            entries[3 * (2 * y + 4 * z + 1) + comp] = far - near
                stiff, inert = element_energies(entries, squares, products)
                result = fields[(0, i) + span] * stiff - (value * fields[(2, i) + span]) * inert
                z_out[(mode * count + i,) + span] = result

    def one_mode(mode, carry):
        value = eig[core * (group // 3) + mode]
        transform(mode, 0)
        transform(mode, 1)
        for i in range(count):
            if i + 2 <= count:
                transform(mode, i + 2)
            energies(mode, value, i)
        return carry

    lax.fori_loop(0, group // 3, one_mode, 0)


class Layers:
    def __init__(self, *parts):
        self.where = {}
        for low, count, ref, offset, stride in parts:
            for i in range(count):
                self.where[low + i] = (ref, offset + i, stride)

    def __call__(self, mode, x):
        ref, offset, stride = self.where[x]
        return ref[mode * stride + offset]


def krylov_step(place, layers, modes, mass, zeroth, first_in, second_in, first_out, second_out, plan, moments, scratch):
    first, last = place[1], place[2]
    ones, twos, in_0, in_1, in_3, inner, ahead_of = plan
    width, depth = moments.shape[2], None
    inverse, count_of = scratch
    shape = inverse.shape[1:]
    width, depth = shape
    missing = missing_plane(shape)
    slot = {x: i for i, x in enumerate(sorted(set(ones) | set(twos) | set(in_0)))}
    for x, i in slot.items():
        count = neighbour_count(missing, x, layers, first, last)
        count_of[i] = count
        value = 1.0 / (mass(0, x) + RADIUS_SQ * count)
        if x < 0:
            value = value * (1.0 - scalar(first))
        if x >= layers:
            value = value * (1.0 - scalar(last))
        inverse[i] = value

    def apply(field, mode, x):
        here = field(mode, x)
        beside = field(mode, x - 1) + field(mode, x + 1)
        beside += shifted(here, 1, 1) + shifted(here, -1, 1)
        beside += shifted(here, 1, 0) + shifted(here, -1, 0)
        return mass(0, x) * here + RADIUS_SQ * (count_of[slot[x]] * here - beside)

    def fold(value):
        total = None
        for row in range(0, width, 8):
            for lane in range(0, depth, 128):
                piece = value[row : row + 8, lane : lane + 128]
                total = piece if total is None else total + piece
        return total

    row = lax.broadcasted_iota(jnp.int32, shape, 0)
    lane = lax.broadcasted_iota(jnp.int32, shape, 1)

    def one_mode(mode, carry):
        sums = [None] * 6

        def add(k, value):
            sums[k] = fold(value) if sums[k] is None else sums[k] + fold(value)

        for x in in_0:
            here = zeroth(mode, x)
            add(0, here * ((mass(0, x) + RADIUS_SQ * count_of[slot[x]]) * here))
        for x in ones:
            image = apply(zeroth, mode, x)
            one = image * inverse[slot[x]]
            first_out[mode * len(ones) + x - ones[0]] = one
            if x in in_1:
                add(1, zeroth(mode, x) * image)
                add(2, one * image)
        for x in twos:
            image = apply(first_in, mode, x)
            two = image * inverse[slot[x]]
            second_out[mode * len(twos) + x - twos[0]] = two
            if x in in_3:
                add(3, first_in(mode, x) * image)
                add(4, two * image)
        for x in inner:
            here = second_in(mode, x)
            add(5, mass(0, x) * here * here)
            aside = jnp.where(row == width - 1, 0.0, pltpu.roll(here, width - 1, 0) - here)
            above = jnp.where(lane == depth - 1, 0.0, pltpu.roll(here, depth - 1, 1) - here)
            add(5, RADIUS_SQ * (aside * aside + above * above))
        for x in ahead_of:
            edge = second_in(mode, x + 1) - second_in(mode, x)
            if x == layers - 1:
                edge = edge * (1.0 - scalar(last))
            add(5, RADIUS_SQ * (edge * edge))
        for k in range(6):
            if sums[k] is not None:
                moments[mode * 6 + k] = moments[mode * 6 + k] + sums[k]
        return carry

    lax.fori_loop(0, modes, one_mode, 0)


def send_halves(target, core, half, modes, fields):
    _, other = halves(core, half)
    total = target.shape[0] // modes

    def one_mode(mode, carry):
        for i, (field, x) in enumerate(fields):
            ref, offset, stride = field.where[x]
            target[mode * total + i] = ref[mode * stride + offset, pl.ds(other, half), :]
        return carry

    lax.fori_loop(0, modes, one_mode, 0)


def plans(layers):
    inner_ones, inner_twos = list(range(1, layers - 1)), list(range(2, layers - 2))
    inner = (inner_ones, inner_twos, list(range(layers)), inner_ones, inner_twos, inner_twos, inner_twos[:-1])
    right_ones, right_twos = [layers - 1, layers, layers + 1], [layers - 2, layers - 1, layers]
    right = (right_ones, right_twos, [], [layers - 1], right_twos[:2], right_twos[:2], [layers - 3] + right_twos[:2])
    left = ([-1, 0], [0, 1], [], [0], [0, 1], [0, 1], [0, 1])
    return inner, right, left


def inner_kernel(modes, layers, cuts, place, za, zb, zc, ma, mb, mc, ones, twos, send, moments, inverse, counts):
    plan = plans(layers)[0]
    zeroth, mass = z0_layers(cuts, layers, za, zb, zc), mass_layers(cuts, layers, ma, mb, mc)
    first = Layers((1, layers - 2, ones, 0, layers - 2))
    second = Layers((2, layers - 4, twos, 0, layers - 4))
    moments[...] = jnp.zeros(moments.shape, jnp.float32)
    krylov_step(place, layers, modes, mass, zeroth, first, second, ones, twos, plan, moments, (inverse, counts))
    fields = [(zeroth, x) for x in range(layers)] + [(first, x) for x in plan[0]] + [(second, x) for x in plan[1]]
    send_halves(send, place[0], za.shape[1] // 2, modes, fields)


def z0_layers(cuts, layers, za, zb, zc):
    a, b = cuts
    return Layers((0, a, za, 0, a), (a, b - a, zb, 0, b - a), (b, layers - b, zc, 0, layers - b))


def mass_layers(cuts, layers, ma, mb, mc):
    a, b = cuts
    return Layers((0, a, ma, 0, 0), (a, b - a, mb, 0, 0), (b, layers - b, mc, 0, 0))


def right_kernel(modes, layers, cuts, place, zc, mc, down, ghost_mass, ones_in, twos_in, moments_in,
                 ones, twos, send, moments, inverse, counts):
    plan = plans(layers)[1]
    tail = layers - cuts[1]
    zeroth = Layers((cuts[1], tail, zc, 0, tail), (layers, DOWN, down, 0, DOWN))
    mass = Layers((cuts[1], tail, mc, 0, 0), (layers, 2, ghost_mass, 0, 0))
    first = Layers((1, layers - 2, ones_in, 0, layers - 2), (layers - 1, 3, ones, 0, 3))
    second = Layers((2, layers - 4, twos_in, 0, layers - 4), (layers - 2, 3, twos, 0, 3))
    moments[...] = moments_in[...]
    krylov_step(place, layers, modes, mass, zeroth, first, second, ones, twos, plan, moments, (inverse, counts))
    fields = [(first, layers - 1), (second, layers - 2), (second, layers - 1)]
    send_halves(send, place[0], zc.shape[1] // 2, modes, fields)


def left_kernel(modes, layers, cuts, place, za, ma, up, ones_in, twos_in, moments_in,
                ones, twos, send, parts, inverse, counts, moments):
    plan = plans(layers)[2]
    zeroth = Layers((-UP, UP, up, 0, UP), (0, cuts[0], za, 0, cuts[0]))
    mass = Layers((-1, 1, up, UP * modes, 0), (0, cuts[0], ma, 0, 0))
    first = Layers((-1, 2, ones, 0, 2), (1, layers - 2, ones_in, 0, layers - 2))
    second = Layers((0, 2, twos, 0, 2), (2, layers - 4, twos_in, 0, layers - 4))
    moments[...] = moments_in[...]
    krylov_step(place, layers, modes, mass, zeroth, first, second, ones, twos, plan, moments, (inverse, counts))
    fields = [(first, 0), (second, 0), (second, 1)]
    send_halves(send, place[0], za.shape[1] // 2, modes, fields)
    row = lax.broadcasted_iota(jnp.int32, (8, 128), 0)
    lane = lax.broadcasted_iota(jnp.int32, (8, 128), 1)
    block = jnp.zeros((8, 128), jnp.float32)
    for mode in range(modes):
        for k in range(6):
            line = jnp.sum(moments[mode * 6 + k], axis=0, keepdims=True)
            total = jnp.sum(line, axis=1, keepdims=True)
            block = jnp.where((row == mode) & (lane == k), total, block)
    for i in range(parts.shape[0]):
        parts[i] = block


def combine_kernel(modes, layers, cuts, place, parts, za, zb, zc, ones_in, twos_in, ones_right, twos_right,
                   ones_left, twos_left, swap, swap_right, swap_left, out):
    core = place[0]
    half, depth = out.shape[2:]
    mine, _ = halves(core, half)
    shape = (8, 128)
    lane = lax.broadcasted_iota(jnp.int32, shape, 1)
    factors = []
    for c in (0, 1):
        block = parts[c]
        for i in range(2 + c, parts.shape[0], 2):
            block = block + parts[i]
        m = [jnp.sum(jnp.where(lane == k, block, 0.0), axis=1, keepdims=True) for k in range(6)]
        one, two = m[2] / m[1], m[3] / m[1]
        pivot = m[3] - one * m[2]
        cross = m[4] - two * m[2]
        slope = cross / pivot
        rest = m[5] - two * m[3] - slope * cross
        right_1 = m[1] - one * m[0]
        right_2 = m[2] - two * m[0] - slope * right_1
        c2 = right_2 / rest
        c1 = (right_1 - cross * c2) / pivot
        c0 = (m[0] - m[2] * c1 - m[3] * c2) / m[1]
        factors.append([jnp.broadcast_to(c, (8, depth)) for c in (c0, c1, c2)])

    zeroth = z0_layers(cuts, layers, za, zb, zc)
    first = Layers((0, 1, ones_left, 1, 2), (1, layers - 2, ones_in, 0, layers - 2), (layers - 1, 1, ones_right, 0, 3))
    second = Layers((0, 2, twos_left, 0, 2), (2, layers - 4, twos_in, 0, layers - 4), (layers - 2, 2, twos_right, 0, 3))
    total = swap.shape[0] // modes
    theirs = [
        Layers((0, layers, swap, 0, total)),
        Layers((0, 1, swap_left, 0, 3), (1, layers - 2, swap, layers, total), (layers - 1, 1, swap_right, 0, 3)),
        Layers((0, 2, swap_left, 1, 3), (2, layers - 4, swap, 2 * layers - 2, total), (layers - 2, 2, swap_right, 1, 3)),
    ]

    for slot in (0, 1):
        for mode in range(modes):
            target = slot * modes + mode
            a, b, c = (f[mode : mode + 1] for f in factors[slot])

            @pl.when(core == slot)
            def _():
                for x in range(layers):
                    planes = []
                    for field in (zeroth, first, second):
                        ref, offset, stride = field.where[x]
                        planes.append(ref[mode * stride + offset, pl.ds(mine, half), :])
                    out[target, x] = a * planes[0] + b * planes[1] + c * planes[2]

            @pl.when(core != slot)
            def _():
                for x in range(layers):
                    planes = [field(mode, x) for field in theirs]
                    out[target, x] = a * planes[0] + b * planes[1] + c * planes[2]


def local(mode_shapes, eigenvalues, density, filter_mass, passive):
    f32 = jnp.float32
    layers, half, depth = density.shape
    group = mode_shapes.shape[0] // 2
    modes = group // 3
    width = 2 * half
    core, at = lax.axis_index("gy"), lax.axis_index("gx")
    count = lax.axis_size("gx")
    place = jnp.stack([core, (at == 0).astype(jnp.int32), (at == count - 1).astype(jnp.int32)]).astype(jnp.int32)
    across = [(0, 1), (1, 0)]
    straight = [(2 * i + c, 2 * i - 2 + c) for i in range(1, count) for c in (0, 1)]
    crossed = [(2 * i + c, 2 * i - 1 - c) for i in range(1, count) for c in (0, 1)]
    both = ("gx", "gy")
    smem = pl.BlockSpec(memory_space=pltpu.SMEM)
    vmem = pl.BlockSpec(memory_space=pltpu.VMEM)
    anywhere = pl.BlockSpec(memory_space=pl.ANY)

    def planes(n, rows=width):
        return jax.ShapeDtypeStruct((n, rows, depth), f32)

    def kernel(name, body, outs, in_specs, scratch, limit, work):
        return pl.pallas_call(
            body,
            out_shape=outs,
            in_specs=in_specs,
            out_specs=jax.tree.map(lambda _: vmem, outs),
            scratch_shapes=scratch,
            compiler_params=pltpu.CompilerParams(vmem_limit_bytes=limit * 2**20),
            cost_estimate=pl.CostEstimate(flops=work * 2**20, bytes_accessed=2**20, transcendentals=0),
            name=name,
        )

    first_node, first_cross, swap, field = kernel(
        "pack",
        pack_kernel,
        (planes(group + 2, half), planes(group + 2, half), planes((group + 3) * layers, half), planes(3 * layers, half)),
        [smem, anywhere, vmem, vmem, vmem],
        [pltpu.SemaphoreType.DMA((2 + group,))],
        8,
        1,
    )(place, mode_shapes, density, filter_mass, passive)
    swap = lax.ppermute(swap, "gy", across)
    halo = lax.ppermute(first_node, both, straight)
    halo_swap = lax.ppermute(first_cross, both, crossed)

    cuts = (DOWN, layers - UP)

    def energies(name, low, high, *extra):
        end = high == layers
        n = high - low
        outs = (planes(modes * n + end), planes(n))
        return kernel(
            name,
            partial(energy_kernel, low, high, end),
            outs + (planes(2),) if end else outs,
            [smem, smem] + [anywhere] * (3 + len(extra)),
            [
                pltpu.VMEM((group, n + 1, width, depth), f32),
                pltpu.VMEM((3, n, width, depth), f32),
                pltpu.VMEM((3, 12, width, depth), f32),
                pltpu.SemaphoreType.DMA((group + 11,)),
            ],
            12,
            n * 200,
        )(place, eigenvalues, mode_shapes, swap, field, *extra)

    za, ma = energies("energies_first", 0, cuts[0], eigenvalues)
    down = lax.ppermute(za, "gx", [(i, i - 1) for i in range(1, count)])
    zb, mb = energies("energies_inner", cuts[0], cuts[1], ma)
    zc, mc, ghost_mass = energies("energies_last", cuts[1], layers, halo, halo_swap, mb)
    up = lax.ppermute(zc, "gx", [(i, i + 1) for i in range(count - 1)])

    tables = [pltpu.VMEM((layers, width, depth), f32)] * 2
    sums = jax.ShapeDtypeStruct((6 * modes, 8, 128), f32)
    ones_in, twos_in, send, moments = kernel(
        "krylov_inner",
        partial(inner_kernel, modes, layers, cuts),
        (planes(modes * (layers - 2)), planes(modes * (layers - 4)), planes(modes * (3 * layers - 6), half), sums),
        [smem] + [vmem] * 6,
        tables,
        12,
        400,
    )(place, za, zb, zc, ma, mb, mc)
    swap_in = lax.ppermute(send, "gy", across)
    ones_right, twos_right, send, moments = kernel(
        "krylov_right",
        partial(right_kernel, modes, layers, cuts),
        (planes(3 * modes), planes(3 * modes), planes(3 * modes, half), sums),
        [smem] + [vmem] * 7,
        tables,
        12,
        200,
    )(place, zc, mc, down, ghost_mass, ones_in, twos_in, moments)
    swap_right = lax.ppermute(send, "gy", across)
    ones_left, twos_left, send, parts = kernel(
        "krylov_left",
        partial(left_kernel, modes, layers, cuts),
        (planes(2 * modes), planes(2 * modes), planes(3 * modes, half), jax.ShapeDtypeStruct((2 * count, 8, 128), f32)),
        [smem] + [vmem] * 6,
        tables + [pltpu.VMEM((6 * modes, 8, 128), f32)],
        12,
        200,
    )(place, za, ma, up, ones_in, twos_in, moments)
    swap_left = lax.ppermute(send, "gy", across)
    parts = lax.all_to_all(parts, both, 0, 0, tiled=True)

    return kernel(
        "combine",
        partial(combine_kernel, modes, layers, cuts),
        jax.ShapeDtypeStruct((2 * modes, layers, half, depth), f32),
        [smem] + [vmem] * 13,
        [],
        12,
        100,
    )(place, parts, za, zb, zc, ones_in, twos_in, ones_right, twos_right, ones_left, twos_left, swap_in, swap_right, swap_left)


def solution(mesh):
    in_specs = (
        P("grp", "gx", "gy", None),
        P("grp"),
        P(("grp", "gx"), "gy", None),
        P(("grp", "gx"), "gy", None),
        P(("grp", "gx"), "gy", None),
    )
    out_specs = P("grp", "gx", "gy", None)
    return jax.shard_map(local, mesh=mesh, in_specs=in_specs, out_specs=out_specs, check_vma=False)
```

profile of v0, /device:TPU:0, one launch (start us, length us, event | category | flops | bytes accessed | tf_op | source)
XLA Modules:
  0.0 58.3 jit_solution(3819919830974736944)
XLA Ops:
  0.0 0.1 pad_add_fusion.place.refs_0_
  0.1 1.7 %copy-done = f32[18,8,16,256]{3,2,1,0:T(8,128)S(1)} copy-done((f32[18,8,16,256]{3,2,1,0:T(8,128)S(1)}, f32[18,8,16,256]{3,2,1,0:T(8,128)}, u32[]{:S(2)}) %copy-start) | copy-done | bytes 2359320
  1.7 0.9 %copy-done.2 = f32[8,16,256]{2,1,0:T(8,128)S(1)} copy-done((f32[8,16,256]{2,1,0:T(8,128)S(1)}, f32[8,16,256]{2,1,0:T(8,128)}, u32[]{:S(2)}) %copy-start.2) | copy-done | bytes 131096
  2.7 0.9 %copy-done.3 = f32[8,16,256]{2,1,0:T(8,128)S(1)} copy-done((f32[8,16,256]{2,1,0:T(8,128)S(1)}, f32[8,16,256]{2,1,0:T(8,128)}, u32[]{:S(2)}) %copy-start.3) | copy-done | bytes 131096
  3.6 0.9 %copy-done.4 = s32[8,16,256]{2,1,0:T(8,128)S(1)} copy-done((s32[8,16,256]{2,1,0:T(8,128)S(1)}, s32[8,16,256]{2,1,0:T(8,128)}, u32[]{:S(2)}) %copy-start.4) | copy-done | bytes 131096
  4.5 2.3 %pack.1 = (f32[11,16,256]{2,1,0:T(8,128)S(1)}, f32[11,16,256]{2,1,0:T(8,128)S(1)}, f32[96,16,256]{2,1,0:T(8,128)S(1)}, f32[24,16,256]{2,1,0:T(8,128)S(1)}) custom-call(s32[3]{0:T(128)S(1)} %pad_add_fusion.place.refs_0_, f32[18,8,16,256]{3,2,1,0:T(8,128)S(1)} %copy-done, f32[8,16,256]{2,1,0:T(8,128)S(1)} %copy-done.2, f32[8,16,256]{2,1,0:T(8,128)S(1)} %copy-done.3, ...), custom_call_target="tpu_custom_call" | custom-call | flops 1048576 | bytes 1048576 | tf_op jit(solution)/shard_map/pack/pallas_call | solution.py:517
  6.8 0.5 collective-permute-start
  7.3 1.3 %collective-permute-start.1 = (f32[11,16,256]{2,1,0:T(8,128)S(1)}, f32[11,16,256]{2,1,0:T(8,128)S(1)}, u32[]{:S(2)}, u32[]{:S(2)}) collective-permute-start(f32[11,16,256]{2,1,0:T(8,128)S(1)} %get-tuple-element.32), channel_id=1, source_target_pairs={{2,0},{3,1},{4,2},{5,3},{6,4},{7,5},{8,6},{9,7},{10,8},{11,9},{12,... | collective-permute-start | bytes 540680 | tf_op jit(solution)/shard_map/ppermute | solution.py:527
  8.6 1.3 %collective-permute-start.2 = (f32[11,16,256]{2,1,0:T(8,128)S(1)}, f32[11,16,256]{2,1,0:T(8,128)S(1)}, u32[]{:S(2)}, u32[]{:S(2)}) collective-permute-start(f32[11,16,256]{2,1,0:T(8,128)S(1)} %get-tuple-element.33), channel_id=1, source_target_pairs={{2,1},{3,0},{4,3},{5,2},{6,5},{7,4},{8,7},{9,6},{10,9},{11,8},{12,... | collective-permute-start | bytes 540680 | tf_op jit(solution)/shard_map/ppermute | solution.py:528
  9.9 0.4 collective-permute-done.refs_3_
  10.3 0.0 copy-done.5
  10.3 0.0 copy-done.1
  10.3 3.1 %energies_first.1 = (f32[9,32,256]{2,1,0:T(8,128)S(1)}, f32[3,32,256]{2,1,0:T(8,128)S(1)}) custom-call(s32[3]{0:T(128)S(1)} %pad_add_fusion.place.refs_0_, f32[6]{0:T(128)S(1)} %copy-done.5, f32[18,8,16,256]{3,2,1,0:T(8,128)S(1)} %copy-done.1, f32[96,16,256]{2,1,0:T(8,128)S(1)} %collective-permute-done.refs_3_, ...), custom_call_target="tpu_custom_call" | custom-call | flops 629145600 | bytes 1048576 | tf_op jit(solution)/shard_map/energies_first/pallas_call | solution.py:536
  13.5 3.1 %energies_inner.1 = (f32[9,32,256]{2,1,0:T(8,128)S(1)}, f32[3,32,256]{2,1,0:T(8,128)S(1)}) custom-call(s32[3]{0:T(128)S(1)} %pad_add_fusion.place.refs_0_, f32[6]{0:T(128)S(1)} %copy-done.5, f32[18,8,16,256]{3,2,1,0:T(8,128)S(1)} %copy-done.1, f32[96,16,256]{2,1,0:T(8,128)S(1)} %collective-permute-done.refs_3_, ...), custom_call_target="tpu_custom_call" | custom-call | flops 629145600 | bytes 1048576 | tf_op jit(solution)/shard_map/energies_inner/pallas_call | solution.py:536
  16.6 0.5 collective-permute-done.1.refs_5_
  17.1 3.5 %collective-permute-done.2.refs_6_ = f32[11,16,256]{2,1,0:T(8,128)S(1)} collective-permute-done((f32[11,16,256]{2,1,0:T(8,128)S(1)}, f32[11,16,256]{2,1,0:T(8,128)S(1)}, u32[]{:S(2)}, u32[]{:S(2)}) %collective-permute-start.2) | collective-permute-done | bytes 180256 | tf_op jit(solution)/shard_map/ppermute | solution.py:528
  20.6 2.7 %energies_last.1 = (f32[7,32,256]{2,1,0:T(8,128)S(1)}, f32[2,32,256]{2,1,0:T(8,128)S(1)}, f32[2,32,256]{2,1,0:T(8,128)S(1)}) custom-call(s32[3]{0:T(128)S(1)} %pad_add_fusion.place.refs_0_, f32[6]{0:T(128)S(1)} %copy-done.5, f32[18,8,16,256]{3,2,1,0:T(8,128)S(1)} %copy-done.1, f32[96,16,256]{2,1,0:T(8,128)S(1)} %collective-permute-done.refs_3_, ...), custom_call_target="tpu_custom_call" | custom-call | flops 419430400 | bytes 1048576 | tf_op jit(solution)/shard_map/energies_last/pallas_call | solution.py:536
  23.2 1.9 %krylov_inner.1 = (f32[18,32,256]{2,1,0:T(8,128)S(1)}, f32[12,32,256]{2,1,0:T(8,128)S(1)}, f32[54,16,256]{2,1,0:T(8,128)S(1)}, f32[18,8,128]{2,1,0:T(8,128)S(1)}) custom-call(s32[3]{0:T(128)S(1)} %pad_add_fusion.place.refs_0_, f32[9,32,256]{2,1,0:T(8,128)S(1)} %get-tuple-element.30.za, f32[9,32,256]{2,1,0:T(8,128)S(1)} %get-tuple-element.36.zb, ...), custom_call_target="tpu_custom_call" | custom-call | flops 419430400 | bytes 1048576 | tf_op jit(solution)/shard_map/krylov_inner/pallas_call | solution.py:559
  25.1 0.2 collective-permute-start.5
  25.3 1.3 %collective-permute-start.4 = (f32[9,32,256]{2,1,0:T(8,128)S(1)}, f32[9,32,256]{2,1,0:T(8,128)S(1)}, u32[]{:S(2)}, u32[]{:S(2)}) collective-permute-start(f32[9,32,256]{2,1,0:T(8,128)S(1)} %get-tuple-element.30.za), channel_id=1, source_target_pairs={{2,0},{4,2},{6,4},{8,6},{10,8},{12,10},{14,12},{3,1},{5,3},{7,5},{... | collective-permute-start | bytes 884744 | tf_op jit(solution)/shard_map/ppermute | solution.py:552
  26.6 5.1 %collective-permute-start.3 = (f32[7,32,256]{2,1,0:T(8,128)S(1)}, f32[7,32,256]{2,1,0:T(8,128)S(1)}, u32[]{:S(2)}, u32[]{:S(2)}) collective-permute-start(f32[7,32,256]{2,1,0:T(8,128)S(1)} %get-tuple-element.35.zc), channel_id=1, source_target_pairs={{0,2},{2,4},{4,6},{6,8},{8,10},{10,12},{12,14},{1,3},{3,5},{5,7},{... | collective-permute-start | bytes 688136 | tf_op jit(solution)/shard_map/ppermute | solution.py:555
  31.7 5.5 %collective-permute-done.4.down = f32[9,32,256]{2,1,0:T(8,128)S(1)} collective-permute-done((f32[9,32,256]{2,1,0:T(8,128)S(1)}, f32[9,32,256]{2,1,0:T(8,128)S(1)}, u32[]{:S(2)}, u32[]{:S(2)}) %collective-permute-start.4) | collective-permute-done | bytes 294944 | tf_op jit(solution)/shard_map/ppermute | solution.py:552
  37.2 1.4 %krylov_right.1 = (f32[9,32,256]{2,1,0:T(8,128)S(1)}, f32[9,32,256]{2,1,0:T(8,128)S(1)}, f32[9,16,256]{2,1,0:T(8,128)S(1)}, f32[18,8,128]{2,1,0:T(8,128)S(1)}) custom-call(s32[3]{0:T(128)S(1)} %pad_add_fusion.place.refs_0_, f32[7,32,256]{2,1,0:T(8,128)S(1)} %get-tuple-element.35.zc, f32[2,32,256]{2,1,0:T(8,128)S(1)} %get-tuple-element.37.mc, ...), custom_call_target="tpu_custom_call" | custom-call | flops 209715200 | bytes 1048576 | tf_op jit(solution)/shard_map/krylov_right/pallas_call | solution.py:569
  38.6 0.1 collective-permute-start.6
  38.7 3.6 %collective-permute-done.3.up = f32[7,32,256]{2,1,0:T(8,128)S(1)} collective-permute-done((f32[7,32,256]{2,1,0:T(8,128)S(1)}, f32[7,32,256]{2,1,0:T(8,128)S(1)}, u32[]{:S(2)}, u32[]{:S(2)}) %collective-permute-start.3) | collective-permute-done | bytes 229408 | tf_op jit(solution)/shard_map/ppermute | solution.py:555
  42.3 1.5 %krylov_left.1 = (f32[6,32,256]{2,1,0:T(8,128)S(1)}, f32[6,32,256]{2,1,0:T(8,128)S(1)}, f32[9,16,256]{2,1,0:T(8,128)S(1)}, f32[16,8,128]{2,1,0:T(8,128)S(1)}) custom-call(s32[3]{0:T(128)S(1)} %pad_add_fusion.place.refs_0_, f32[9,32,256]{2,1,0:T(8,128)S(1)} %get-tuple-element.30.za, f32[3,32,256]{2,1,0:T(8,128)S(1)} %get-tuple-element.31.refs_5_.ma, ...), custom_call_target="tpu_custom_call" | custom-call | flops 209715200 | bytes 1048576 | tf_op jit(solution)/shard_map/krylov_left/pallas_call | solution.py:579
  43.7 0.1 collective-permute-start.7
  43.9 12.7 %all_to_all.5.parts = f32[16,8,128]{2,1,0:T(8,128)S(1)} all-to-all(f32[16,8,128]{2,1,0:T(8,128)S(1)} %get-tuple-element.43), channel_id=1, replica_groups=mesh['grp'=2,'gx'=8,'gy'=2] {'gx','gy'}, dimensions={0} | all-to-all | bytes 131072 | tf_op jit(solution)/shard_map/all_to_all | solution.py:589
  56.6 0.0 collective-permute-done.6.swap_right
  56.6 0.0 collective-permute-done.7.swap_left
  56.6 0.0 collective-permute-done.5.swap
  56.6 1.7 %combine.1 = f32[6,8,16,256]{3,2,1,0:T(8,128)} custom-call(s32[3]{0:T(128)S(1)} %pad_add_fusion.place.refs_0_, f32[16,8,128]{2,1,0:T(8,128)S(1)} %all_to_all.5.parts, f32[9,32,256]{2,1,0:T(8,128)S(1)} %get-tuple-element.30.za, f32[9,32,256]{2,1,0:T(8,128)S(1)} %get-tuple-element.36.zb, f32[7,32,256]{2,1,0:T(8,128)S(1)} %get-tuple-element.35.zc, ...), custom_call_target="tpu_custom_call" | custom-call | flops 104857600 | bytes 1048576 | tf_op jit(solution)/shard_map/combine/pallas_call | solution.py:591
  (6 shorter events, 0.0 us)
Async XLA Ops:
  0.0 10.3 %copy-start.5 = (f32[6]{0:T(128)S(1)}, f32[6]{0:T(128)}, u32[]{:S(2)}) copy-start(f32[6]{0:T(128)} %refs_1_.5) | copy-start | bytes 76
  0.1 1.7 %copy-start = (f32[18,8,16,256]{3,2,1,0:T(8,128)S(1)}, f32[18,8,16,256]{3,2,1,0:T(8,128)}, u32[]{:S(2)}) copy-start(f32[18,8,16,256]{3,2,1,0:T(8,128)} %refs_2_.5) | copy-start | bytes 7077892
  1.7 0.9 %copy-start.2 = (f32[8,16,256]{2,1,0:T(8,128)S(1)}, f32[8,16,256]{2,1,0:T(8,128)}, u32[]{:S(2)}) copy-start(f32[8,16,256]{2,1,0:T(8,128)} %density.1) | copy-start | bytes 393220
  2.7 0.9 %copy-start.3 = (f32[8,16,256]{2,1,0:T(8,128)S(1)}, f32[8,16,256]{2,1,0:T(8,128)}, u32[]{:S(2)}) copy-start(f32[8,16,256]{2,1,0:T(8,128)} %mass.1) | copy-start | bytes 393220
  3.6 0.9 %copy-start.4 = (s32[8,16,256]{2,1,0:T(8,128)S(1)}, s32[8,16,256]{2,1,0:T(8,128)}, u32[]{:S(2)}) copy-start(s32[8,16,256]{2,1,0:T(8,128)} %passive.1) | copy-start | bytes 393220
  4.5 5.9 %copy-start.1 = (f32[18,8,16,256]{3,2,1,0:T(8,128)S(1)}, f32[18,8,16,256]{3,2,1,0:T(8,128)}, u32[]{:S(2)}) copy-start(f32[18,8,16,256]{3,2,1,0:T(8,128)} %refs_2_.5) | copy-start | bytes 7077892
  6.8 3.6 %collective-permute-start = (f32[96,16,256]{2,1,0:T(8,128)S(1)}, f32[96,16,256]{2,1,0:T(8,128)S(1)}, u32[]{:S(2)}, u32[]{:S(2)}) collective-permute-start(f32[96,16,256]{2,1,0:T(8,128)S(1)} %get-tuple-element.28), channel_id=1, source_target_pairs={{0,1},{1,0},{2,3},{3,2},{4,5},{5,4},{6,7},{7,6},{8,9},{9,8},{10,11... | collective-permute-start | bytes 4718600 | tf_op jit(solution)/shard_map/ppermute | solution.py:526
  7.3 9.8 %collective-permute-start.1 = (f32[11,16,256]{2,1,0:T(8,128)S(1)}, f32[11,16,256]{2,1,0:T(8,128)S(1)}, u32[]{:S(2)}, u32[]{:S(2)}) collective-permute-start(f32[11,16,256]{2,1,0:T(8,128)S(1)} %get-tuple-element.32), channel_id=1, source_target_pairs={{2,0},{3,1},{4,2},{5,3},{6,4},{7,5},{8,6},{9,7},{10,8},{11,9},{12,... | collective-permute-start | bytes 540680 | tf_op jit(solution)/shard_map/ppermute | solution.py:527
  8.6 12.0 %collective-permute-start.2 = (f32[11,16,256]{2,1,0:T(8,128)S(1)}, f32[11,16,256]{2,1,0:T(8,128)S(1)}, u32[]{:S(2)}, u32[]{:S(2)}) collective-permute-start(f32[11,16,256]{2,1,0:T(8,128)S(1)} %get-tuple-element.33), channel_id=1, source_target_pairs={{2,1},{3,0},{4,3},{5,2},{6,5},{7,4},{8,7},{9,6},{10,9},{11,8},{12,... | collective-permute-start | bytes 540680 | tf_op jit(solution)/shard_map/ppermute | solution.py:528
  25.1 31.5 %collective-permute-start.5 = (f32[54,16,256]{2,1,0:T(8,128)S(1)}, f32[54,16,256]{2,1,0:T(8,128)S(1)}, u32[]{:S(2)}, u32[]{:S(2)}) collective-permute-start(f32[54,16,256]{2,1,0:T(8,128)S(1)} %get-tuple-element.48), channel_id=1, source_target_pairs={{0,1},{1,0},{2,3},{3,2},{4,5},{5,4},{6,7},{7,6},{8,9},{9,8},{10,11... | collective-permute-start | bytes 2654216 | tf_op jit(solution)/shard_map/ppermute | solution.py:568
  25.3 11.9 %collective-permute-start.4 = (f32[9,32,256]{2,1,0:T(8,128)S(1)}, f32[9,32,256]{2,1,0:T(8,128)S(1)}, u32[]{:S(2)}, u32[]{:S(2)}) collective-permute-start(f32[9,32,256]{2,1,0:T(8,128)S(1)} %get-tuple-element.30.za), channel_id=1, source_target_pairs={{2,0},{4,2},{6,4},{8,6},{10,8},{12,10},{14,12},{3,1},{5,3},{7,5},{... | collective-permute-start | bytes 884744 | tf_op jit(solution)/shard_map/ppermute | solution.py:552
  26.6 15.7 %collective-permute-start.3 = (f32[7,32,256]{2,1,0:T(8,128)S(1)}, f32[7,32,256]{2,1,0:T(8,128)S(1)}, u32[]{:S(2)}, u32[]{:S(2)}) collective-permute-start(f32[7,32,256]{2,1,0:T(8,128)S(1)} %get-tuple-element.35.zc), channel_id=1, source_target_pairs={{0,2},{2,4},{4,6},{6,8},{8,10},{10,12},{12,14},{1,3},{3,5},{5,7},{... | collective-permute-start | bytes 688136 | tf_op jit(solution)/shard_map/ppermute | solution.py:555
  38.6 18.0 %collective-permute-start.6 = (f32[9,16,256]{2,1,0:T(8,128)S(1)}, f32[9,16,256]{2,1,0:T(8,128)S(1)}, u32[]{:S(2)}, u32[]{:S(2)}) collective-permute-start(f32[9,16,256]{2,1,0:T(8,128)S(1)} %get-tuple-element.49), channel_id=1, source_target_pairs={{0,1},{1,0},{2,3},{3,2},{4,5},{5,4},{6,7},{7,6},{8,9},{9,8},{10,11... | collective-permute-start | bytes 442376 | tf_op jit(solution)/shard_map/ppermute | solution.py:578
  43.7 12.8 %collective-permute-start.7 = (f32[9,16,256]{2,1,0:T(8,128)S(1)}, f32[9,16,256]{2,1,0:T(8,128)S(1)}, u32[]{:S(2)}, u32[]{:S(2)}) collective-permute-start(f32[9,16,256]{2,1,0:T(8,128)S(1)} %get-tuple-element.50), channel_id=1, source_target_pairs={{0,1},{1,0},{2,3},{3,2},{4,5},{5,4},{6,7},{7,6},{8,9},{9,8},{10,11... | collective-permute-start | bytes 442376 | tf_op jit(solution)/shard_map/ppermute | solution.py:588
where the time goes:
time: 58.6 us; the launch traced here: 58.3 us
  Pallas kernels  17.7 us (30%)
  waiting for transfers between devices  13.5 us (23%)
  blocking collectives  12.7 us (22%)
  starting transfers between devices  9.82 us (17%)
  local copies, waits for them, and re-layouts  4.38 us (7%)
    all_to_all x1, blocking collectives, local(): parts = lax.all_to_all(parts, both, 0, 0, tiled=True)  12.7 us
    pallas_call x3, Pallas kernels, energies(): kernel(name, partial(energy_kernel, low, high, end), outs + (planes(2),)...  8.94 us
    ppermute x1, waiting for transfers between devices, local(): down = lax.ppermute(za, 'gx', [(i, i - 1) for i in range(1, count)])  5.5 us
    ppermute x1, starting transfers between devices, local(): up = lax.ppermute(zc, 'gx', [(i, i + 1) for i in range(count - 1)])  5.09 us
    unnamed x12, local copies, waits for them, and re-layouts  4.38 us
    ppermute x1, waiting for transfers between devices, local(): up = lax.ppermute(zc, 'gx', [(i, i + 1) for i in range(count - 1)])  3.63 us
    ppermute x1, waiting for transfers between devices, local(): halo_swap = lax.ppermute(first_cross, both, crossed)  3.45 us
    pallas_call x1, Pallas kernels, local(): kernel('pack', pack_kernel, (planes(group + 2, half), planes(group + 2, h...  2.28 us
  transfers between devices with their start and end apart: 8, of which 5 were waited for; matrix products, arithmetic and copies ran while one was open for 0% of the time, Pallas kernels for 16%

commit v1 on v0

--- a/solution.py
+++ b/solution.py
@@ -140,7 +140,7 @@
     return pl.multiple_of(core * half, half), pl.multiple_of((1 - core) * half, half)
 
 
-def pack_kernel(place, modes, density, mass, passive, straight, crossed, swap, field, sems):
+def pack_kernel(place, modes, density, mass, passive, straight, crossed, swap, field, floats, flags, sems):
     group, layers = modes.shape[0] // 2, modes.shape[1]
     core = place[0]
     mine, theirs = core * group, (1 - core) * group
@@ -152,12 +152,18 @@
         pltpu.make_async_copy(modes.at[theirs + i], swap.at[pl.ds(i * layers, layers)], sems.at[2 + i])
         for i in range(group)
     ]
-    for copy in copies:
+    inputs = [
+        pltpu.make_async_copy(source, target, sems.at[2 + group + i])
+        for i, (source, target) in enumerate(((density, floats.at[0]), (mass, floats.at[1]), (passive, flags)))
+    ]
+    for copy in inputs + copies:
         copy.start()
+    for copy in inputs:
+        copy.wait()
     base = group * layers
     for x in range(layers):
-        rho, weight = density[x], mass[x]
-        design = (1 - passive[x]).astype(jnp.float32)
+        rho, weight = floats[0, x], floats[1, x]
+        design = (1 - flags[x]).astype(jnp.float32)
         slope = 3.0 * (1.0 - void_floor) * rho * rho * design
         for k, value in enumerate((slope, weight, design)):
             swap[base + k * layers + x] = value
@@ -175,7 +181,8 @@
     if end:
         (halo, halo_swap, _, z_out, mass_out, ghost_mass), refs = refs[:6], refs[6:]
     else:
-        (_, z_out, mass_out), refs = refs[:3], refs[3:]
+        *_, z_out, mass_out = refs[:-4]
+        refs = refs[-4:]
     nodes, fields, sums, sems = refs
     layers, half, depth = modes.shape[1:]
     group = modes.shape[0] // 2
@@ -346,17 +353,19 @@
     lax.fori_loop(0, modes, one_mode, 0)
 
 
-def send_halves(target, core, half, modes, fields):
+def send_halves(target, core, half, modes, parts, sems):
     _, other = halves(core, half)
     total = target.shape[0] // modes
-
-    def one_mode(mode, carry):
-        for i, (field, x) in enumerate(fields):
-            ref, offset, stride = field.where[x]
-            target[mode * total + i] = ref[mode * stride + offset, pl.ds(other, half), :]
-        return carry
-
-    lax.fori_loop(0, modes, one_mode, 0)
+    copies = []
+    for mode in range(modes):
+        at = mode * total
+        for ref, offset, stride, count in parts:
+            source = ref.at[pl.ds(mode * stride + offset, count), pl.ds(other, half), :]
+            copies.append(pltpu.make_async_copy(source, target.at[pl.ds(at, count)], sems.at[len(copies)]))
+            at += count
+    for copy in copies:
+        copy.start()
+    return copies
 
 
 def plans(layers):
@@ -368,15 +377,13 @@
     return inner, right, left
 
 
-def inner_kernel(modes, layers, cuts, place, za, zb, zc, ma, mb, mc, ones, twos, send, moments, inverse, counts):
+def inner_kernel(modes, layers, cuts, place, za, zb, zc, ma, mb, mc, ones, twos, moments, inverse, counts):
     plan = plans(layers)[0]
     zeroth, mass = z0_layers(cuts, layers, za, zb, zc), mass_layers(cuts, layers, ma, mb, mc)
     first = Layers((1, layers - 2, ones, 0, layers - 2))
     second = Layers((2, layers - 4, twos, 0, layers - 4))
     moments[...] = jnp.zeros(moments.shape, jnp.float32)
     krylov_step(place, layers, modes, mass, zeroth, first, second, ones, twos, plan, moments, (inverse, counts))
-    fields = [(zeroth, x) for x in range(layers)] + [(first, x) for x in plan[0]] + [(second, x) for x in plan[1]]
-    send_halves(send, place[0], za.shape[1] // 2, modes, fields)
 
 
 def z0_layers(cuts, layers, za, zb, zc):
@@ -390,7 +397,7 @@
 
 
 def right_kernel(modes, layers, cuts, place, zc, mc, down, ghost_mass, ones_in, twos_in, moments_in,
-                 ones, twos, send, moments, inverse, counts):
+                 ones, twos, moments, inverse, counts):
     plan = plans(layers)[1]
     tail = layers - cuts[1]
     zeroth = Layers((cuts[1], tail, zc, 0, tail), (layers, DOWN, down, 0, DOWN))
@@ -399,21 +406,30 @@
     second = Layers((2, layers - 4, twos_in, 0, layers - 4), (layers - 2, 3, twos, 0, 3))
     moments[...] = moments_in[...]
     krylov_step(place, layers, modes, mass, zeroth, first, second, ones, twos, plan, moments, (inverse, counts))
-    fields = [(first, layers - 1), (second, layers - 2), (second, layers - 1)]
-    send_halves(send, place[0], zc.shape[1] // 2, modes, fields)
-
-
-def left_kernel(modes, layers, cuts, place, za, ma, up, ones_in, twos_in, moments_in,
-                ones, twos, send, parts, inverse, counts, moments):
+
+
+def left_kernel(modes, layers, cuts, place, za, zb, zc, ma, up, ones_in, twos_in, ones_right, twos_right, moments_in,
+                ones, twos, send, parts, inverse, counts, moments, sems):
     plan = plans(layers)[2]
+    half = za.shape[1] // 2
+    tail = layers - cuts[1]
+    pieces = [(za, 0, cuts[0], cuts[0]), (zb, 0, cuts[1] - cuts[0], cuts[1] - cuts[0]), (zc, 0, tail, tail)]
+    pieces += [(ones_in, 0, layers - 2, layers - 2), (ones_right, 0, 3, 1)]
+    pieces += [(twos_in, 0, layers - 4, layers - 4), (twos_right, 0, 3, 2)]
+    copies = send_halves(send, place[0], half, modes, pieces, sems)
     zeroth = Layers((-UP, UP, up, 0, UP), (0, cuts[0], za, 0, cuts[0]))
     mass = Layers((-1, 1, up, UP * modes, 0), (0, cuts[0], ma, 0, 0))
     first = Layers((-1, 2, ones, 0, 2), (1, layers - 2, ones_in, 0, layers - 2))
     second = Layers((0, 2, twos, 0, 2), (2, layers - 4, twos_in, 0, layers - 4))
     moments[...] = moments_in[...]
     krylov_step(place, layers, modes, mass, zeroth, first, second, ones, twos, plan, moments, (inverse, counts))
-    fields = [(first, 0), (second, 0), (second, 1)]
-    send_halves(send, place[0], za.shape[1] // 2, modes, fields)
+    _, other = halves(place[0], half)
+    total = send.shape[0] // modes
+    for mode in range(modes):
+        at = (mode + 1) * total - 3
+        send[at] = ones[2 * mode + 1, pl.ds(other, half), :]
+        send[at + 1] = twos[2 * mode, pl.ds(other, half), :]
+        send[at + 2] = twos[2 * mode + 1, pl.ds(other, half), :]
     row = lax.broadcasted_iota(jnp.int32, (8, 128), 0)
     lane = lax.broadcasted_iota(jnp.int32, (8, 128), 1)
     block = jnp.zeros((8, 128), jnp.float32)
@@ -424,10 +440,12 @@
             block = jnp.where((row == mode) & (lane == k), total, block)
     for i in range(parts.shape[0]):
         parts[i] = block
+    for copy in copies:
+        copy.wait()
 
 
 def combine_kernel(modes, layers, cuts, place, parts, za, zb, zc, ones_in, twos_in, ones_right, twos_right,
-                   ones_left, twos_left, swap, swap_right, swap_left, out):
+                   ones_left, twos_left, swap, out):
     core = place[0]
     half, depth = out.shape[2:]
     mine, _ = halves(core, half)
@@ -457,8 +475,8 @@
     total = swap.shape[0] // modes
     theirs = [
         Layers((0, layers, swap, 0, total)),
-        Layers((0, 1, swap_left, 0, 3), (1, layers - 2, swap, layers, total), (layers - 1, 1, swap_right, 0, 3)),
-        Layers((0, 2, swap_left, 1, 3), (2, layers - 4, swap, 2 * layers - 2, total), (layers - 2, 2, swap_right, 1, 3)),
+        Layers((0, 1, swap, 3 * layers - 3, total), (1, layers - 1, swap, layers, total)),
+        Layers((0, 2, swap, 3 * layers - 2, total), (2, layers - 2, swap, 2 * layers - 1, total)),
     ]
 
     for slot in (0, 1):
@@ -497,6 +515,7 @@
     both = ("gx", "gy")
     smem = pl.BlockSpec(memory_space=pltpu.SMEM)
     vmem = pl.BlockSpec(memory_space=pltpu.VMEM)
+    hbm = pl.BlockSpec(memory_space=pltpu.HBM)
     anywhere = pl.BlockSpec(memory_space=pl.ANY)
 
     def planes(n, rows=width):
@@ -518,11 +537,15 @@
         "pack",
         pack_kernel,
         (planes(group + 2, half), planes(group + 2, half), planes((group + 3) * layers, half), planes(3 * layers, half)),
-        [smem, anywhere, vmem, vmem, vmem],
-        [pltpu.SemaphoreType.DMA((2 + group,))],
+        [smem] + [hbm] * 4,
+        [
+            pltpu.VMEM((2, layers, half, depth), f32),
+            pltpu.VMEM((layers, half, depth), jnp.int32),
+            pltpu.SemaphoreType.DMA((5 + group,)),
+        ],
         8,
         1,
-    )(place, mode_shapes, density, filter_mass, passive)
+    )(place, *(pltpu.with_memory_space_constraint(x, pltpu.HBM) for x in (mode_shapes, density, filter_mass, passive)))
     swap = lax.ppermute(swap, "gy", across)
     halo = lax.ppermute(first_node, both, straight)
     halo_swap = lax.ppermute(first_cross, both, crossed)
@@ -548,7 +571,7 @@
             n * 200,
         )(place, eigenvalues, mode_shapes, swap, field, *extra)
 
-    za, ma = energies("energies_first", 0, cuts[0], eigenvalues)
+    za, ma = energies("energies_first", 0, cuts[0])
     down = lax.ppermute(za, "gx", [(i, i - 1) for i in range(1, count)])
     zb, mb = energies("energies_inner", cuts[0], cuts[1], ma)
     zc, mc, ghost_mass = energies("energies_last", cuts[1], layers, halo, halo_swap, mb)
@@ -556,47 +579,50 @@
 
     tables = [pltpu.VMEM((layers, width, depth), f32)] * 2
     sums = jax.ShapeDtypeStruct((6 * modes, 8, 128), f32)
-    ones_in, twos_in, send, moments = kernel(
+    ones_in, twos_in, moments = kernel(
         "krylov_inner",
         partial(inner_kernel, modes, layers, cuts),
-        (planes(modes * (layers - 2)), planes(modes * (layers - 4)), planes(modes * (3 * layers - 6), half), sums),
+        (planes(modes * (layers - 2)), planes(modes * (layers - 4)), sums),
         [smem] + [vmem] * 6,
         tables,
         12,
         400,
     )(place, za, zb, zc, ma, mb, mc)
-    swap_in = lax.ppermute(send, "gy", across)
-    ones_right, twos_right, send, moments = kernel(
+    ones_right, twos_right, moments = kernel(
         "krylov_right",
         partial(right_kernel, modes, layers, cuts),
-        (planes(3 * modes), planes(3 * modes), planes(3 * modes, half), sums),
+        (planes(3 * modes), planes(3 * modes), sums),
         [smem] + [vmem] * 7,
         tables,
         12,
         200,
     )(place, zc, mc, down, ghost_mass, ones_in, twos_in, moments)
-    swap_right = lax.ppermute(send, "gy", across)
     ones_left, twos_left, send, parts = kernel(
         "krylov_left",
         partial(left_kernel, modes, layers, cuts),
-        (planes(2 * modes), planes(2 * modes), planes(3 * modes, half), jax.ShapeDtypeStruct((2 * count, 8, 128), f32)),
-        [smem] + [vmem] * 6,
-        tables + [pltpu.VMEM((6 * modes, 8, 128), f32)],
+        (
+            planes(2 * modes),
+            planes(2 * modes),
+            planes(modes * 3 * layers, half),
+            jax.ShapeDtypeStruct((2 * count, 8, 128), f32),
+        ),
+        [smem] + [vmem] * 10,
+        tables + [pltpu.VMEM((6 * modes, 8, 128), f32), pltpu.SemaphoreType.DMA((7 * modes,))],
         12,
         200,
-    )(place, za, ma, up, ones_in, twos_in, moments)
-    swap_left = lax.ppermute(send, "gy", across)
+    )(place, za, zb, zc, ma, up, ones_in, twos_in, ones_right, twos_right, moments)
+    swap_in = lax.ppermute(send, "gy", across)
     parts = lax.all_to_all(parts, both, 0, 0, tiled=True)
 
     return kernel(
         "combine",
         partial(combine_kernel, modes, layers, cuts),
         jax.ShapeDtypeStruct((2 * modes, layers, half, depth), f32),
-        [smem] + [vmem] * 13,
+        [smem] + [vmem] * 11,
         [],
         12,
         100,
-    )(place, parts, za, zb, zc, ones_in, twos_in, ones_right, twos_right, ones_left, twos_left, swap_in, swap_right, swap_left)
+    )(place, parts, za, zb, zc, ones_in, twos_in, ones_right, twos_right, ones_left, twos_left, swap_in)
 
 
 def solution(mesh):

time: 58.6 us -> 48 us (0.82)
  waiting for transfers between devices: 13.5 us -> 5.48 us
  local copies, waits for them, and re-layouts: 4.38 us -> 0.01 us
  blocking collectives: 12.7 us -> 15.1 us
  starting transfers between devices: 9.82 us -> 8.8 us
  Pallas kernels: 17.7 us -> 18.3 us
    ppermute x1, waiting for transfers between devices: 5.5 us -> 0.01 us  [local(): down = lax.ppermute(za, 'gx', [(i, i - 1) for i in range(1, count)])]
    unnamed x12 -> x4, local copies, waits for them, and re-layouts: 4.38 us -> 0.01 us
    all_to_all x1, blocking collectives: 12.7 us -> 15.1 us  [local(): parts = lax.all_to_all(parts, both, 0, 0, tiled=True)]
    ppermute x1, waiting for transfers between devices: 3.63 us -> 2.4 us  [local(): up = lax.ppermute(zc, 'gx', [(i, i + 1) for i in range(count - 1)])]
    ppermute x1, waiting for transfers between devices: 3.45 us -> 2.63 us  [local(): halo_swap = lax.ppermute(first_cross, both, crossed)]
    ppermute x1, starting transfers between devices: 5.09 us -> 4.35 us  [local(): up = lax.ppermute(zc, 'gx', [(i, i + 1) for i in range(count - 1)])]
    pallas_call x1, Pallas kernels: 1.46 us -> 2.12 us  [local(): kernel('krylov_left', partial(left_kernel, modes, layers, cuts), (planes(...]
  transfers between devices with their start and end apart: 8 -> 6, of which waited for: 5 -> 3; matrix products, arithmetic and copies ran while one was open for 0% -> 0% of each run, Pallas kernels for 16% -> 25%
where the time goes in v1:
time: 48 us; the launch traced here: 47.8 us
  Pallas kernels  18.3 us (38%)
  blocking collectives  15.1 us (31%)
  starting transfers between devices  8.8 us (18%)
  waiting for transfers between devices  5.48 us (11%)
    all_to_all x1, blocking collectives, local(): parts = lax.all_to_all(parts, both, 0, 0, tiled=True)  15.1 us
    pallas_call x3, Pallas kernels, energies(): kernel(name, partial(energy_kernel, low, high, end), outs + (planes(2),)...  8.94 us
    ppermute x1, starting transfers between devices, local(): up = lax.ppermute(zc, 'gx', [(i, i + 1) for i in range(count - 1)])  4.35 us
    ppermute x1, waiting for transfers between devices, local(): halo_swap = lax.ppermute(first_cross, both, crossed)  2.63 us
    ppermute x1, waiting for transfers between devices, local(): up = lax.ppermute(zc, 'gx', [(i, i + 1) for i in range(count - 1)])  2.4 us
    pallas_call x1, Pallas kernels, local(): kernel('pack', pack_kernel, (planes(group + 2, half), planes(group + 2, h...  2.29 us
    pallas_call x1, Pallas kernels, local(): kernel('krylov_left', partial(left_kernel, modes, layers, cuts), (planes(...  2.12 us
    pallas_call x1, Pallas kernels, local(): kernel('krylov_inner', partial(inner_kernel, modes, layers, cuts), (plane...  1.86 us
  transfers between devices with their start and end apart: 6, of which 3 were waited for; matrix products, arithmetic and copies ran while one was open for 0% of the time, Pallas kernels for 25%

profile of v1, /device:TPU:0, one launch (start us, length us, event | category | flops | bytes accessed | tf_op | source)
XLA Modules:
  0.0 47.8 jit_solution(7588529181403932041)
XLA Ops:
  0.0 0.0 copy-start
  0.0 0.0 copy-start.1
  0.0 0.1 pad_add_fusion.place.refs_0_
  0.1 2.3 %pack.1 = (f32[11,16,256]{2,1,0:T(8,128)S(1)}, f32[11,16,256]{2,1,0:T(8,128)S(1)}, f32[96,16,256]{2,1,0:T(8,128)S(1)}, f32[24,16,256]{2,1,0:T(8,128)S(1)}) custom-call(s32[3]{0:T(128)S(1)} %pad_add_fusion.place.refs_0_, f32[18,8,16,256]{3,2,1,0:T(8,128)} %refs_2_.5, f32[8,16,256]{2,1,0:T(8,128)} %density.1, f32[8,16,256]{2,1,0:T(8,128)} %mass.1, ...), custom_call_target="tpu_custom_call" | custom-call | flops 1048576 | bytes 1048576 | tf_op jit(solution)/shard_map/pack/pallas_call | solution.py:536
  2.4 0.5 %collective-permute-start = (f32[96,16,256]{2,1,0:T(8,128)S(1)}, f32[96,16,256]{2,1,0:T(8,128)S(1)}, u32[]{:S(2)}, u32[]{:S(2)}) collective-permute-start(f32[96,16,256]{2,1,0:T(8,128)S(1)} %get-tuple-element.26), channel_id=1, source_target_pairs={{0,1},{1,0},{2,3},{3,2},{4,5},{5,4},{6,7},{7,6},{8,9},{9,8},{10,11... | collective-permute-start | bytes 4718600 | tf_op jit(solution)/shard_map/ppermute | solution.py:549
  2.9 1.3 %collective-permute-start.1 = (f32[11,16,256]{2,1,0:T(8,128)S(1)}, f32[11,16,256]{2,1,0:T(8,128)S(1)}, u32[]{:S(2)}, u32[]{:S(2)}) collective-permute-start(f32[11,16,256]{2,1,0:T(8,128)S(1)} %get-tuple-element.31), channel_id=1, source_target_pairs={{2,0},{3,1},{4,2},{5,3},{6,4},{7,5},{8,6},{9,7},{10,8},{11,9},{12,... | collective-permute-start | bytes 540680 | tf_op jit(solution)/shard_map/ppermute | solution.py:550
  4.2 1.3 %collective-permute-start.2 = (f32[11,16,256]{2,1,0:T(8,128)S(1)}, f32[11,16,256]{2,1,0:T(8,128)S(1)}, u32[]{:S(2)}, u32[]{:S(2)}) collective-permute-start(f32[11,16,256]{2,1,0:T(8,128)S(1)} %get-tuple-element.32), channel_id=1, source_target_pairs={{2,1},{3,0},{4,3},{5,2},{6,5},{7,4},{8,7},{9,6},{10,9},{11,8},{12,... | collective-permute-start | bytes 540680 | tf_op jit(solution)/shard_map/ppermute | solution.py:551
  5.5 0.4 collective-permute-done.refs_3_
  5.9 0.0 copy-done
  5.9 0.0 copy-done.1
  5.9 3.1 %energies_first.1 = (f32[9,32,256]{2,1,0:T(8,128)S(1)}, f32[3,32,256]{2,1,0:T(8,128)S(1)}) custom-call(s32[3]{0:T(128)S(1)} %pad_add_fusion.place.refs_0_, f32[6]{0:T(128)S(1)} %copy-done.1, f32[18,8,16,256]{3,2,1,0:T(8,128)S(1)} %copy-done, f32[96,16,256]{2,1,0:T(8,128)S(1)} %collective-permute-done.refs_3_, f32[24,16,256]{2,1,0:T(8,128)S(1)} %get-tuple-element.27.refs_4_), custom_call_target="tpu_custom_call" | custom-call | flops 629145600 | bytes 1048576 | tf_op jit(solution)/shard_map/energies_first/pallas_call | solution.py:559
  9.1 1.3 %collective-permute-start.4 = (f32[9,32,256]{2,1,0:T(8,128)S(1)}, f32[9,32,256]{2,1,0:T(8,128)S(1)}, u32[]{:S(2)}, u32[]{:S(2)}) collective-permute-start(f32[9,32,256]{2,1,0:T(8,128)S(1)} %get-tuple-element.28.za), channel_id=1, source_target_pairs={{2,0},{4,2},{6,4},{8,6},{10,8},{12,10},{14,12},{3,1},{5,3},{7,5},{... | collective-permute-start | bytes 884744 | tf_op jit(solution)/shard_map/ppermute | solution.py:575
  10.4 3.1 %energies_inner.1 = (f32[9,32,256]{2,1,0:T(8,128)S(1)}, f32[3,32,256]{2,1,0:T(8,128)S(1)}) custom-call(s32[3]{0:T(128)S(1)} %pad_add_fusion.place.refs_0_, f32[6]{0:T(128)S(1)} %copy-done.1, f32[18,8,16,256]{3,2,1,0:T(8,128)S(1)} %copy-done, f32[96,16,256]{2,1,0:T(8,128)S(1)} %collective-permute-done.refs_3_, f32[24,16,256]{2,1,0:T(8,128)S(1)} %get-tuple-element.27.refs_4_, ...), custom_call_target="tpu_custom_call" | custom-call | flops 629145600 | bytes 1048576 | tf_op jit(solution)/shard_map/energies_inner/pallas_call | solution.py:559
  13.5 0.0 collective-permute-done.1.refs_5_
  13.5 2.6 %collective-permute-done.2.refs_6_ = f32[11,16,256]{2,1,0:T(8,128)S(1)} collective-permute-done((f32[11,16,256]{2,1,0:T(8,128)S(1)}, f32[11,16,256]{2,1,0:T(8,128)S(1)}, u32[]{:S(2)}, u32[]{:S(2)}) %collective-permute-start.2) | collective-permute-done | bytes 180256 | tf_op jit(solution)/shard_map/ppermute | solution.py:551
  16.2 2.7 %energies_last.1 = (f32[7,32,256]{2,1,0:T(8,128)S(1)}, f32[2,32,256]{2,1,0:T(8,128)S(1)}, f32[2,32,256]{2,1,0:T(8,128)S(1)}) custom-call(s32[3]{0:T(128)S(1)} %pad_add_fusion.place.refs_0_, f32[6]{0:T(128)S(1)} %copy-done.1, f32[18,8,16,256]{3,2,1,0:T(8,128)S(1)} %copy-done, f32[96,16,256]{2,1,0:T(8,128)S(1)} %collective-permute-done.refs_3_, ...), custom_call_target="tpu_custom_call" | custom-call | flops 419430400 | bytes 1048576 | tf_op jit(solution)/shard_map/energies_last/pallas_call | solution.py:559
  18.8 4.3 %collective-permute-start.3 = (f32[7,32,256]{2,1,0:T(8,128)S(1)}, f32[7,32,256]{2,1,0:T(8,128)S(1)}, u32[]{:S(2)}, u32[]{:S(2)}) collective-permute-start(f32[7,32,256]{2,1,0:T(8,128)S(1)} %get-tuple-element.34.zc), channel_id=1, source_target_pairs={{0,2},{2,4},{4,6},{6,8},{8,10},{10,12},{12,14},{1,3},{3,5},{5,7},{... | collective-permute-start | bytes 688136 | tf_op jit(solution)/shard_map/ppermute | solution.py:578
  23.2 1.9 %krylov_inner.1 = (f32[18,32,256]{2,1,0:T(8,128)S(1)}, f32[12,32,256]{2,1,0:T(8,128)S(1)}, f32[18,8,128]{2,1,0:T(8,128)S(1)}) custom-call(s32[3]{0:T(128)S(1)} %pad_add_fusion.place.refs_0_, f32[9,32,256]{2,1,0:T(8,128)S(1)} %get-tuple-element.28.za, f32[9,32,256]{2,1,0:T(8,128)S(1)} %get-tuple-element.30.zb, f32[7,32,256]{2,1,0:T(8,128)S(1)} %get-tuple-element.34.zc, ...), custom_call_target="tpu_custom_call" | custom-call | flops 419430400 | bytes 1048576 | tf_op jit(solution)/shard_map/krylov_inner/pallas_call | solution.py:582
  25.1 0.0 collective-permute-done.4.down
  25.1 1.4 %krylov_right.1 = (f32[9,32,256]{2,1,0:T(8,128)S(1)}, f32[9,32,256]{2,1,0:T(8,128)S(1)}, f32[18,8,128]{2,1,0:T(8,128)S(1)}) custom-call(s32[3]{0:T(128)S(1)} %pad_add_fusion.place.refs_0_, f32[7,32,256]{2,1,0:T(8,128)S(1)} %get-tuple-element.34.zc, f32[2,32,256]{2,1,0:T(8,128)S(1)} %get-tuple-element.35.mc, f32[9,32,256]{2,1,0:T(8,128)S(1)} %collective-permute-done.4.down, ...), custom_call_target="tpu_custom_call" | custom-call | flops 209715200 | bytes 1048576 | tf_op jit(solution)/shard_map/krylov_right/pallas_call | solution.py:591
  26.4 2.4 %collective-permute-done.3.up = f32[7,32,256]{2,1,0:T(8,128)S(1)} collective-permute-done((f32[7,32,256]{2,1,0:T(8,128)S(1)}, f32[7,32,256]{2,1,0:T(8,128)S(1)}, u32[]{:S(2)}, u32[]{:S(2)}) %collective-permute-start.3) | collective-permute-done | bytes 229408 | tf_op jit(solution)/shard_map/ppermute | solution.py:578
  28.8 2.1 %krylov_left.1 = (f32[6,32,256]{2,1,0:T(8,128)S(1)}, f32[6,32,256]{2,1,0:T(8,128)S(1)}, f32[72,16,256]{2,1,0:T(8,128)S(1)}, f32[16,8,128]{2,1,0:T(8,128)S(1)}) custom-call(s32[3]{0:T(128)S(1)} %pad_add_fusion.place.refs_0_, f32[9,32,256]{2,1,0:T(8,128)S(1)} %get-tuple-element.28.za, f32[9,32,256]{2,1,0:T(8,128)S(1)} %get-tuple-element.30.zb, ...), custom_call_target="tpu_custom_call" | custom-call | flops 209715200 | bytes 1048576 | tf_op jit(solution)/shard_map/krylov_left/pallas_call | solution.py:600
  31.0 0.1 collective-permute-start.5
  31.0 15.1 %all_to_all.5.parts = f32[16,8,128]{2,1,0:T(8,128)S(1)} all-to-all(f32[16,8,128]{2,1,0:T(8,128)S(1)} %get-tuple-element.43), channel_id=1, replica_groups=mesh['grp'=2,'gx'=8,'gy'=2] {'gx','gy'}, dimensions={0} | all-to-all | bytes 131072 | tf_op jit(solution)/shard_map/all_to_all | solution.py:615
  46.1 0.0 collective-permute-done.5.swap
  46.1 1.7 %combine.1 = f32[6,8,16,256]{3,2,1,0:T(8,128)} custom-call(s32[3]{0:T(128)S(1)} %pad_add_fusion.place.refs_0_, f32[16,8,128]{2,1,0:T(8,128)S(1)} %all_to_all.5.parts, f32[9,32,256]{2,1,0:T(8,128)S(1)} %get-tuple-element.28.za, f32[9,32,256]{2,1,0:T(8,128)S(1)} %get-tuple-element.30.zb, f32[7,32,256]{2,1,0:T(8,128)S(1)} %get-tuple-element.34.zc, ...), custom_call_target="tpu_custom_call" | custom-call | flops 104857600 | bytes 1048576 | tf_op jit(solution)/shard_map/combine/pallas_call | solution.py:617
Async XLA Ops:
  0.0 5.9 %copy-start = (f32[18,8,16,256]{3,2,1,0:T(8,128)S(1)}, f32[18,8,16,256]{3,2,1,0:T(8,128)}, u32[]{:S(2)}) copy-start(f32[18,8,16,256]{3,2,1,0:T(8,128)} %refs_2_.5) | copy-start | bytes 7077892
  0.0 5.9 %copy-start.1 = (f32[6]{0:T(128)S(1)}, f32[6]{0:T(128)}, u32[]{:S(2)}) copy-start(f32[6]{0:T(128)} %refs_1_.5) | copy-start | bytes 76
  2.4 3.6 %collective-permute-start = (f32[96,16,256]{2,1,0:T(8,128)S(1)}, f32[96,16,256]{2,1,0:T(8,128)S(1)}, u32[]{:S(2)}, u32[]{:S(2)}) collective-permute-start(f32[96,16,256]{2,1,0:T(8,128)S(1)} %get-tuple-element.26), channel_id=1, source_target_pairs={{0,1},{1,0},{2,3},{3,2},{4,5},{5,4},{6,7},{7,6},{8,9},{9,8},{10,11... | collective-permute-start | bytes 4718600 | tf_op jit(solution)/shard_map/ppermute | solution.py:549
  2.9 10.6 %collective-permute-start.1 = (f32[11,16,256]{2,1,0:T(8,128)S(1)}, f32[11,16,256]{2,1,0:T(8,128)S(1)}, u32[]{:S(2)}, u32[]{:S(2)}) collective-permute-start(f32[11,16,256]{2,1,0:T(8,128)S(1)} %get-tuple-element.31), channel_id=1, source_target_pairs={{2,0},{3,1},{4,2},{5,3},{6,4},{7,5},{8,6},{9,7},{10,8},{11,9},{12,... | collective-permute-start | bytes 540680 | tf_op jit(solution)/shard_map/ppermute | solution.py:550
  4.2 12.0 %collective-permute-start.2 = (f32[11,16,256]{2,1,0:T(8,128)S(1)}, f32[11,16,256]{2,1,0:T(8,128)S(1)}, u32[]{:S(2)}, u32[]{:S(2)}) collective-permute-start(f32[11,16,256]{2,1,0:T(8,128)S(1)} %get-tuple-element.32), channel_id=1, source_target_pairs={{2,1},{3,0},{4,3},{5,2},{6,5},{7,4},{8,7},{9,6},{10,9},{11,8},{12,... | collective-permute-start | bytes 540680 | tf_op jit(solution)/shard_map/ppermute | solution.py:551
  9.1 16.0 %collective-permute-start.4 = (f32[9,32,256]{2,1,0:T(8,128)S(1)}, f32[9,32,256]{2,1,0:T(8,128)S(1)}, u32[]{:S(2)}, u32[]{:S(2)}) collective-permute-start(f32[9,32,256]{2,1,0:T(8,128)S(1)} %get-tuple-element.28.za), channel_id=1, source_target_pairs={{2,0},{4,2},{6,4},{8,6},{10,8},{12,10},{14,12},{3,1},{5,3},{7,5},{... | collective-permute-start | bytes 884744 | tf_op jit(solution)/shard_map/ppermute | solution.py:575
  18.8 10.0 %collective-permute-start.3 = (f32[7,32,256]{2,1,0:T(8,128)S(1)}, f32[7,32,256]{2,1,0:T(8,128)S(1)}, u32[]{:S(2)}, u32[]{:S(2)}) collective-permute-start(f32[7,32,256]{2,1,0:T(8,128)S(1)} %get-tuple-element.34.zc), channel_id=1, source_target_pairs={{0,2},{2,4},{4,6},{6,8},{8,10},{10,12},{12,14},{1,3},{3,5},{5,7},{... | collective-permute-start | bytes 688136 | tf_op jit(solution)/shard_map/ppermute | solution.py:578
  31.0 15.1 %collective-permute-start.5 = (f32[72,16,256]{2,1,0:T(8,128)S(1)}, f32[72,16,256]{2,1,0:T(8,128)S(1)}, u32[]{:S(2)}, u32[]{:S(2)}) collective-permute-start(f32[72,16,256]{2,1,0:T(8,128)S(1)} %get-tuple-element.46), channel_id=1, source_target_pairs={{0,1},{1,0},{2,3},{3,2},{4,5},{5,4},{6,7},{7,6},{8,9},{9,8},{10,11... | collective-permute-start | bytes 3538952 | tf_op jit(solution)/shard_map/ppermute | solution.py:614

commit v2 on v1

--- a/solution.py
+++ b/solution.py
@@ -224,16 +224,20 @@
     if end:
         z_out[z_out.shape[0] - 1] = fields[1, count - 1]
 
-    def transform(mode, i):
+    ring = sums.shape[0]
+
+    def transform(step):
+        mode, i = divmod(step, count + 1)
         for comp in range(3):
             here = nodes[3 * mode + comp, i]
             above = shifted(here, 1, 1)
             for z, value in ((0, here + above), (1, above - here)):
                 beside = shifted(value, 1, 0)
-                sums[i % 3, 4 * comp + 2 * z] = value + beside
-                sums[i % 3, 4 * comp + 2 * z + 1] = beside - value
-
-    def energies(mode, value, i):
+                sums[step % ring, 4 * comp + 2 * z] = value + beside
+                sums[step % ring, 4 * comp + 2 * z + 1] = beside - value
+
+    def energies(step, value):
+        mode, i = divmod(step, count + 1)
         for row in range(0, width, 8):
             for lane in range(0, depth, 128):
                 span = (pl.ds(row, 8), pl.ds(lane, 128))
@@ -241,25 +245,23 @@
                 for comp in range(3):
                     for z in (0, 1):
                         for y in (0, 1):
-                            near = sums[(i % 3, 4 * comp + 2 * z + y) + span]
-                            far = sums[((i + 1) % 3, 4 * comp + 2 * z + y) + span]
+                            near = sums[(step % ring, 4 * comp + 2 * z + y) + span]
+                            far = sums[((step + 1) % ring, 4 * comp + 2 * z + y) + span]
                             entries[3 * (2 * y + 4 * z) + comp] = near + far
                             entries[3 * (2 * y + 4 * z + 1) + comp] = far - near
                 stiff, inert = element_energies(entries, squares, products)
                 result = fields[(0, i) + span] * stiff - (value * fields[(2, i) + span]) * inert
                 z_out[(mode * count + i,) + span] = result
 
-    def one_mode(mode, carry):
-        value = eig[core * (group // 3) + mode]
-        transform(mode, 0)
-        transform(mode, 1)
-        for i in range(count):
-            if i + 2 <= count:
-                transform(mode, i + 2)
-            energies(mode, value, i)
-        return carry
-
-    lax.fori_loop(0, group // 3, one_mode, 0)
+    total = group // 3 * (count + 1)
+    values = [eig[core * (group // 3) + mode] for mode in range(group // 3)]
+    transform(0)
+    transform(1)
+    for step in range(total):
+        if step + 2 < total:
+            transform(step + 2)
+        if step % (count + 1) < count:
+            energies(step, values[step // (count + 1)])
 
 
 class Layers:
@@ -564,7 +566,7 @@
             [
                 pltpu.VMEM((group, n + 1, width, depth), f32),
                 pltpu.VMEM((3, n, width, depth), f32),
-                pltpu.VMEM((3, 12, width, depth), f32),
+                pltpu.VMEM((4, 12, width, depth), f32),
                 pltpu.SemaphoreType.DMA((group + 11,)),
             ],
             12,
@@ -572,10 +574,11 @@
         )(place, eigenvalues, mode_shapes, swap, field, *extra)
 
     za, ma = energies("energies_first", 0, cuts[0])
-    down = lax.ppermute(za, "gx", [(i, i - 1) for i in range(1, count)])
-    zb, mb = energies("energies_inner", cuts[0], cuts[1], ma)
-    zc, mc, ghost_mass = energies("energies_last", cuts[1], layers, halo, halo_swap, mb)
+    down, halo, halo_swap = lax.optimization_barrier((za, halo, halo_swap))
+    down = lax.ppermute(down, "gx", [(i, i - 1) for i in range(1, count)])
+    zc, mc, ghost_mass = energies("energies_last", cuts[1], layers, halo, halo_swap, ma)
     up = lax.ppermute(zc, "gx", [(i, i + 1) for i in range(count - 1)])
+    zb, mb = energies("energies_inner", cuts[0], cuts[1], mc)
 
     tables = [pltpu.VMEM((layers, width, depth), f32)] * 2
     sums = jax.ShapeDtypeStruct((6 * modes, 8, 128), f32)

time: 48 us -> 49.8 us (1.037)
  waiting for transfers between devices: 5.48 us -> 9.46 us
  blocking collectives: 15.1 us -> 12.6 us
  starting transfers between devices: 8.8 us -> 9.46 us
  Pallas kernels: 18.3 us -> 17.8 us
    ppermute x1, waiting for transfers between devices: 0.01 us -> 3.79 us  [local(): halo = lax.ppermute(first_node, both, straight)]
    all_to_all x1, blocking collectives: 15.1 us -> 12.6 us  [local(): parts = lax.all_to_all(parts, both, 0, 0, tiled=True)]
    ppermute x1, waiting for transfers between devices: 2.63 us -> 3.45 us  [local(): halo_swap = lax.ppermute(first_cross, both, crossed)]
    ppermute x1, starting transfers between devices: 4.35 us -> 4.98 us  [local(): up = lax.ppermute(zc, 'gx', [(i, i + 1) for i in range(count - 1)])]
    ppermute x1, waiting for transfers between devices: 2.4 us -> 1.77 us  [local(): up = lax.ppermute(zc, 'gx', [(i, i + 1) for i in range(count - 1)])]
  transfers between devices with their start and end apart: 6 -> 6, of which waited for: 3 -> 4; matrix products, arithmetic and copies ran while one was open for 0% -> 0% of each run, Pallas kernels for 25% -> 24%
where the time goes in v2:
time: 49.8 us; the launch traced here: 49.6 us
  Pallas kernels  17.8 us (36%)
  blocking collectives  12.6 us (25%)
  starting transfers between devices  9.46 us (19%)
  waiting for transfers between devices  9.46 us (19%)
    all_to_all x1, blocking collectives, local(): parts = lax.all_to_all(parts, both, 0, 0, tiled=True)  12.6 us
    pallas_call x3, Pallas kernels, energies(): kernel(name, partial(energy_kernel, low, high, end), outs + (planes(2),)...  8.49 us
    ppermute x1, starting transfers between devices, local(): up = lax.ppermute(zc, 'gx', [(i, i + 1) for i in range(count - 1)])  4.98 us
    ppermute x1, waiting for transfers between devices, local(): halo = lax.ppermute(first_node, both, straight)  3.79 us
    ppermute x1, waiting for transfers between devices, local(): halo_swap = lax.ppermute(first_cross, both, crossed)  3.45 us
    pallas_call x1, Pallas kernels, local(): kernel('pack', pack_kernel, (planes(group + 2, half), planes(group + 2, h...  2.29 us
    pallas_call x1, Pallas kernels, local(): kernel('krylov_left', partial(left_kernel, modes, layers, cuts), (planes(...  2.12 us
    pallas_call x1, Pallas kernels, local(): kernel('krylov_inner', partial(inner_kernel, modes, layers, cuts), (plane...  1.86 us
  transfers between devices with their start and end apart: 6, of which 4 were waited for; matrix products, arithmetic and copies ran while one was open for 0% of the time, Pallas kernels for 24%

profile of v2, /device:TPU:0, one launch (start us, length us, event | category | flops | bytes accessed | tf_op | source)
XLA Modules:
  0.0 49.6 jit_solution(4611132393059172100)
XLA Ops:
  0.0 0.0 copy-start
  0.0 0.0 copy-start.1
  0.0 0.1 pad_add_fusion.place.refs_0_
  0.1 2.3 %pack.1 = (f32[11,16,256]{2,1,0:T(8,128)S(1)}, f32[11,16,256]{2,1,0:T(8,128)S(1)}, f32[96,16,256]{2,1,0:T(8,128)S(1)}, f32[24,16,256]{2,1,0:T(8,128)S(1)}) custom-call(s32[3]{0:T(128)S(1)} %pad_add_fusion.place.refs_0_, f32[18,8,16,256]{3,2,1,0:T(8,128)} %refs_2_.5, f32[8,16,256]{2,1,0:T(8,128)} %density.1, f32[8,16,256]{2,1,0:T(8,128)} %mass.1, ...), custom_call_target="tpu_custom_call" | custom-call | flops 1048576 | bytes 1048576 | tf_op jit(solution)/shard_map/pack/pallas_call | solution.py:538
  2.4 0.5 %collective-permute-start = (f32[96,16,256]{2,1,0:T(8,128)S(1)}, f32[96,16,256]{2,1,0:T(8,128)S(1)}, u32[]{:S(2)}, u32[]{:S(2)}) collective-permute-start(f32[96,16,256]{2,1,0:T(8,128)S(1)} %get-tuple-element.29), channel_id=1, source_target_pairs={{0,1},{1,0},{2,3},{3,2},{4,5},{5,4},{6,7},{7,6},{8,9},{9,8},{10,11... | collective-permute-start | bytes 4718600 | tf_op jit(solution)/shard_map/ppermute | solution.py:551
  2.9 1.3 %collective-permute-start.1 = (f32[11,16,256]{2,1,0:T(8,128)S(1)}, f32[11,16,256]{2,1,0:T(8,128)S(1)}, u32[]{:S(2)}, u32[]{:S(2)}) collective-permute-start(f32[11,16,256]{2,1,0:T(8,128)S(1)} %get-tuple-element.32), channel_id=1, source_target_pairs={{2,0},{3,1},{4,2},{5,3},{6,4},{7,5},{8,6},{9,7},{10,8},{11,9},{12,... | collective-permute-start | bytes 540680 | tf_op jit(solution)/shard_map/ppermute | solution.py:552
  4.2 1.3 %collective-permute-start.2 = (f32[11,16,256]{2,1,0:T(8,128)S(1)}, f32[11,16,256]{2,1,0:T(8,128)S(1)}, u32[]{:S(2)}, u32[]{:S(2)}) collective-permute-start(f32[11,16,256]{2,1,0:T(8,128)S(1)} %get-tuple-element.33), channel_id=1, source_target_pairs={{2,1},{3,0},{4,3},{5,2},{6,5},{7,4},{8,7},{9,6},{10,9},{11,8},{12,... | collective-permute-start | bytes 540680 | tf_op jit(solution)/shard_map/ppermute | solution.py:553
  5.5 0.4 collective-permute-done.refs_3_
  5.9 0.0 copy-done
  5.9 0.0 copy-done.1
  5.9 3.0 %energies_first.1 = (f32[9,32,256]{2,1,0:T(8,128)S(1)}, f32[3,32,256]{2,1,0:T(8,128)S(1)}) custom-call(s32[3]{0:T(128)S(1)} %pad_add_fusion.place.refs_0_, f32[6]{0:T(128)S(1)} %copy-done.1, f32[18,8,16,256]{3,2,1,0:T(8,128)S(1)} %copy-done, f32[96,16,256]{2,1,0:T(8,128)S(1)} %collective-permute-done.refs_3_, f32[24,16,256]{2,1,0:T(8,128)S(1)} %get-tuple-element.30.refs_4_), custom_call_target="tpu_custom_call" | custom-call | flops 629145600 | bytes 1048576 | tf_op jit(solution)/shard_map/energies_first/pallas_call | solution.py:561
  8.9 3.8 %collective-permute-done.1.refs_5_ = f32[11,16,256]{2,1,0:T(8,128)S(1)} collective-permute-done((f32[11,16,256]{2,1,0:T(8,128)S(1)}, f32[11,16,256]{2,1,0:T(8,128)S(1)}, u32[]{:S(2)}, u32[]{:S(2)}) %collective-permute-start.1) | collective-permute-done | bytes 180256 | tf_op jit(solution)/shard_map/ppermute | solution.py:552
  12.7 3.5 %collective-permute-done.2.refs_6_ = f32[11,16,256]{2,1,0:T(8,128)S(1)} collective-permute-done((f32[11,16,256]{2,1,0:T(8,128)S(1)}, f32[11,16,256]{2,1,0:T(8,128)S(1)}, u32[]{:S(2)}, u32[]{:S(2)}) %collective-permute-start.2) | collective-permute-done | bytes 180256 | tf_op jit(solution)/shard_map/ppermute | solution.py:553
  16.2 1.3 %collective-permute-start.4 = (f32[9,32,256]{2,1,0:T(8,128)S(1)}, f32[9,32,256]{2,1,0:T(8,128)S(1)}, u32[]{:S(2)}, u32[]{:S(2)}) collective-permute-start(f32[9,32,256]{2,1,0:T(8,128)S(1)} %get-tuple-element.43.za), channel_id=1, source_target_pairs={{2,0},{4,2},{6,4},{8,6},{10,8},{12,10},{14,12},{3,1},{5,3},{7,5},{... | collective-permute-start | bytes 884744 | tf_op jit(solution)/shard_map/ppermute | solution.py:578
  17.5 2.5 %energies_last.1 = (f32[7,32,256]{2,1,0:T(8,128)S(1)}, f32[2,32,256]{2,1,0:T(8,128)S(1)}, f32[2,32,256]{2,1,0:T(8,128)S(1)}) custom-call(s32[3]{0:T(128)S(1)} %pad_add_fusion.place.refs_0_, f32[6]{0:T(128)S(1)} %copy-done.1, f32[18,8,16,256]{3,2,1,0:T(8,128)S(1)} %copy-done, f32[96,16,256]{2,1,0:T(8,128)S(1)} %collective-permute-done.refs_3_, ...), custom_call_target="tpu_custom_call" | custom-call | flops 419430400 | bytes 1048576 | tf_op jit(solution)/shard_map/energies_last/pallas_call | solution.py:561
  20.0 5.0 %collective-permute-start.3 = (f32[7,32,256]{2,1,0:T(8,128)S(1)}, f32[7,32,256]{2,1,0:T(8,128)S(1)}, u32[]{:S(2)}, u32[]{:S(2)}) collective-permute-start(f32[7,32,256]{2,1,0:T(8,128)S(1)} %get-tuple-element.39.zc), channel_id=1, source_target_pairs={{0,2},{2,4},{4,6},{6,8},{8,10},{10,12},{12,14},{1,3},{3,5},{5,7},{... | collective-permute-start | bytes 688136 | tf_op jit(solution)/shard_map/ppermute | solution.py:580
  25.0 3.0 %energies_inner.1 = (f32[9,32,256]{2,1,0:T(8,128)S(1)}, f32[3,32,256]{2,1,0:T(8,128)S(1)}) custom-call(s32[3]{0:T(128)S(1)} %pad_add_fusion.place.refs_0_, f32[6]{0:T(128)S(1)} %copy-done.1, f32[18,8,16,256]{3,2,1,0:T(8,128)S(1)} %copy-done, f32[96,16,256]{2,1,0:T(8,128)S(1)} %collective-permute-done.refs_3_, f32[24,16,256]{2,1,0:T(8,128)S(1)} %get-tuple-element.30.refs_4_, ...), custom_call_target="tpu_custom_call" | custom-call | flops 629145600 | bytes 1048576 | tf_op jit(solution)/shard_map/energies_inner/pallas_call | solution.py:561
  28.0 1.9 %krylov_inner.1 = (f32[18,32,256]{2,1,0:T(8,128)S(1)}, f32[12,32,256]{2,1,0:T(8,128)S(1)}, f32[18,8,128]{2,1,0:T(8,128)S(1)}) custom-call(s32[3]{0:T(128)S(1)} %pad_add_fusion.place.refs_0_, f32[9,32,256]{2,1,0:T(8,128)S(1)} %get-tuple-element.43.za, f32[9,32,256]{2,1,0:T(8,128)S(1)} %get-tuple-element.38.zb, f32[7,32,256]{2,1,0:T(8,128)S(1)} %get-tuple-element.39.zc, ...), custom_call_target="tpu_custom_call" | custom-call | flops 419430400 | bytes 1048576 | tf_op jit(solution)/shard_map/krylov_inner/pallas_call | solution.py:585
  29.8 0.0 collective-permute-done.4.down
  29.8 1.4 %krylov_right.1 = (f32[9,32,256]{2,1,0:T(8,128)S(1)}, f32[9,32,256]{2,1,0:T(8,128)S(1)}, f32[18,8,128]{2,1,0:T(8,128)S(1)}) custom-call(s32[3]{0:T(128)S(1)} %pad_add_fusion.place.refs_0_, f32[7,32,256]{2,1,0:T(8,128)S(1)} %get-tuple-element.39.zc, f32[2,32,256]{2,1,0:T(8,128)S(1)} %get-tuple-element.37.refs_5_.mc, ...), custom_call_target="tpu_custom_call" | custom-call | flops 209715200 | bytes 1048576 | tf_op jit(solution)/shard_map/krylov_right/pallas_call | solution.py:594
  31.2 1.8 %collective-permute-done.3.up = f32[7,32,256]{2,1,0:T(8,128)S(1)} collective-permute-done((f32[7,32,256]{2,1,0:T(8,128)S(1)}, f32[7,32,256]{2,1,0:T(8,128)S(1)}, u32[]{:S(2)}, u32[]{:S(2)}) %collective-permute-start.3) | collective-permute-done | bytes 229408 | tf_op jit(solution)/shard_map/ppermute | solution.py:580
  33.0 2.1 %krylov_left.1 = (f32[6,32,256]{2,1,0:T(8,128)S(1)}, f32[6,32,256]{2,1,0:T(8,128)S(1)}, f32[72,16,256]{2,1,0:T(8,128)S(1)}, f32[16,8,128]{2,1,0:T(8,128)S(1)}) custom-call(s32[3]{0:T(128)S(1)} %pad_add_fusion.place.refs_0_, f32[9,32,256]{2,1,0:T(8,128)S(1)} %get-tuple-element.43.za, f32[9,32,256]{2,1,0:T(8,128)S(1)} %get-tuple-element.38.zb, ...), custom_call_target="tpu_custom_call" | custom-call | flops 209715200 | bytes 1048576 | tf_op jit(solution)/shard_map/krylov_left/pallas_call | solution.py:603
  35.1 0.1 collective-permute-start.5
  35.2 12.6 %all_to_all.5.parts = f32[16,8,128]{2,1,0:T(8,128)S(1)} all-to-all(f32[16,8,128]{2,1,0:T(8,128)S(1)} %get-tuple-element.49), channel_id=1, replica_groups=mesh['grp'=2,'gx'=8,'gy'=2] {'gx','gy'}, dimensions={0} | all-to-all | bytes 131072 | tf_op jit(solution)/shard_map/all_to_all | solution.py:618
  47.8 0.0 collective-permute-done.5.swap
  47.9 1.7 %combine.1 = f32[6,8,16,256]{3,2,1,0:T(8,128)} custom-call(s32[3]{0:T(128)S(1)} %pad_add_fusion.place.refs_0_, f32[16,8,128]{2,1,0:T(8,128)S(1)} %all_to_all.5.parts, f32[9,32,256]{2,1,0:T(8,128)S(1)} %get-tuple-element.43.za, f32[9,32,256]{2,1,0:T(8,128)S(1)} %get-tuple-element.38.zb, f32[7,32,256]{2,1,0:T(8,128)S(1)} %get-tuple-element.39.zc, ...), custom_call_target="tpu_custom_call" | custom-call | flops 104857600 | bytes 1048576 | tf_op jit(solution)/shard_map/combine/pallas_call | solution.py:620
Async XLA Ops:
  0.0 5.9 %copy-start = (f32[18,8,16,256]{3,2,1,0:T(8,128)S(1)}, f32[18,8,16,256]{3,2,1,0:T(8,128)}, u32[]{:S(2)}) copy-start(f32[18,8,16,256]{3,2,1,0:T(8,128)} %refs_2_.5) | copy-start | bytes 7077892
  0.0 5.9 %copy-start.1 = (f32[6]{0:T(128)S(1)}, f32[6]{0:T(128)}, u32[]{:S(2)}) copy-start(f32[6]{0:T(128)} %refs_1_.5) | copy-start | bytes 76
  2.4 3.6 %collective-permute-start = (f32[96,16,256]{2,1,0:T(8,128)S(1)}, f32[96,16,256]{2,1,0:T(8,128)S(1)}, u32[]{:S(2)}, u32[]{:S(2)}) collective-permute-start(f32[96,16,256]{2,1,0:T(8,128)S(1)} %get-tuple-element.29), channel_id=1, source_target_pairs={{0,1},{1,0},{2,3},{3,2},{4,5},{5,4},{6,7},{7,6},{8,9},{9,8},{10,11... | collective-permute-start | bytes 4718600 | tf_op jit(solution)/shard_map/ppermute | solution.py:551
  2.9 9.8 %collective-permute-start.1 = (f32[11,16,256]{2,1,0:T(8,128)S(1)}, f32[11,16,256]{2,1,0:T(8,128)S(1)}, u32[]{:S(2)}, u32[]{:S(2)}) collective-permute-start(f32[11,16,256]{2,1,0:T(8,128)S(1)} %get-tuple-element.32), channel_id=1, source_target_pairs={{2,0},{3,1},{4,2},{5,3},{6,4},{7,5},{8,6},{9,7},{10,8},{11,9},{12,... | collective-permute-start | bytes 540680 | tf_op jit(solution)/shard_map/ppermute | solution.py:552
  4.2 12.0 %collective-permute-start.2 = (f32[11,16,256]{2,1,0:T(8,128)S(1)}, f32[11,16,256]{2,1,0:T(8,128)S(1)}, u32[]{:S(2)}, u32[]{:S(2)}) collective-permute-start(f32[11,16,256]{2,1,0:T(8,128)S(1)} %get-tuple-element.33), channel_id=1, source_target_pairs={{2,1},{3,0},{4,3},{5,2},{6,5},{7,4},{8,7},{9,6},{10,9},{11,8},{12,... | collective-permute-start | bytes 540680 | tf_op jit(solution)/shard_map/ppermute | solution.py:553
  16.2 13.7 %collective-permute-start.4 = (f32[9,32,256]{2,1,0:T(8,128)S(1)}, f32[9,32,256]{2,1,0:T(8,128)S(1)}, u32[]{:S(2)}, u32[]{:S(2)}) collective-permute-start(f32[9,32,256]{2,1,0:T(8,128)S(1)} %get-tuple-element.43.za), channel_id=1, source_target_pairs={{2,0},{4,2},{6,4},{8,6},{10,8},{12,10},{14,12},{3,1},{5,3},{7,5},{... | collective-permute-start | bytes 884744 | tf_op jit(solution)/shard_map/ppermute | solution.py:578
  20.0 13.0 %collective-permute-start.3 = (f32[7,32,256]{2,1,0:T(8,128)S(1)}, f32[7,32,256]{2,1,0:T(8,128)S(1)}, u32[]{:S(2)}, u32[]{:S(2)}) collective-permute-start(f32[7,32,256]{2,1,0:T(8,128)S(1)} %get-tuple-element.39.zc), channel_id=1, source_target_pairs={{0,2},{2,4},{4,6},{6,8},{8,10},{10,12},{12,14},{1,3},{3,5},{5,7},{... | collective-permute-start | bytes 688136 | tf_op jit(solution)/shard_map/ppermute | solution.py:580
  35.1 12.8 %collective-permute-start.5 = (f32[72,16,256]{2,1,0:T(8,128)S(1)}, f32[72,16,256]{2,1,0:T(8,128)S(1)}, u32[]{:S(2)}, u32[]{:S(2)}) collective-permute-start(f32[72,16,256]{2,1,0:T(8,128)S(1)} %get-tuple-element.52), channel_id=1, source_target_pairs={{0,1},{1,0},{2,3},{3,2},{4,5},{5,4},{6,7},{7,6},{8,9},{9,8},{10,11... | collective-permute-start | bytes 3538952 | tf_op jit(solution)/shard_map/ppermute | solution.py:617

commit v3 on v2

--- a/solution.py
+++ b/solution.py
@@ -140,50 +140,26 @@
     return pl.multiple_of(core * half, half), pl.multiple_of((1 - core) * half, half)
 
 
-def pack_kernel(place, modes, density, mass, passive, straight, crossed, swap, field, floats, flags, sems):
-    group, layers = modes.shape[0] // 2, modes.shape[1]
+def first_kernel(place, modes, mass, straight, crossed, sems):
+    group = modes.shape[0] // 2
     core = place[0]
-    mine, theirs = core * group, (1 - core) * group
-    copies = [
-        pltpu.make_async_copy(modes.at[pl.ds(mine, group), 0], straight.at[pl.ds(0, group)], sems.at[0]),
-        pltpu.make_async_copy(modes.at[pl.ds(theirs, group), 0], crossed.at[pl.ds(0, group)], sems.at[1]),
-    ]
-    copies += [
-        pltpu.make_async_copy(modes.at[theirs + i], swap.at[pl.ds(i * layers, layers)], sems.at[2 + i])
-        for i in range(group)
-    ]
-    inputs = [
-        pltpu.make_async_copy(source, target, sems.at[2 + group + i])
-        for i, (source, target) in enumerate(((density, floats.at[0]), (mass, floats.at[1]), (passive, flags)))
-    ]
-    for copy in inputs + copies:
+    copies = []
+    for target, start in ((straight, core * group), (crossed, (1 - core) * group)):
+        for source, at, count in ((modes.at[pl.ds(start, group), 0], 0, group), (mass.at[pl.ds(0, 2)], group, 2)):
+            copies.append(pltpu.make_async_copy(source, target.at[pl.ds(at, count)], sems.at[len(copies)]))
+    for copy in copies:
         copy.start()
-    for copy in inputs:
-        copy.wait()
-    base = group * layers
-    for x in range(layers):
-        rho, weight = floats[0, x], floats[1, x]
-        design = (1 - flags[x]).astype(jnp.float32)
-        slope = 3.0 * (1.0 - void_floor) * rho * rho * design
-        for k, value in enumerate((slope, weight, design)):
-            swap[base + k * layers + x] = value
-            field[k * layers + x] = value
-        if x < 2:
-            straight[group + x] = weight
-            crossed[group + x] = weight
     for copy in copies:
         copy.wait()
 
 
 def energy_kernel(low, high, end, *refs):
-    place, eig, modes, swap, field = refs[:5]
-    refs = refs[5:]
+    place, eig, modes, modes_swap, density, density_swap, mass, mass_swap, passive, passive_swap = refs[:10]
     if end:
-        (halo, halo_swap, _, z_out, mass_out, ghost_mass), refs = refs[:6], refs[6:]
+        halo, halo_swap = refs[10:12]
+        z_out, mass_out, ghost_mass, nodes, floats, flags, sums, sems = refs[-8:]
     else:
-        *_, z_out, mass_out = refs[:-4]
-        refs = refs[-4:]
-    nodes, fields, sums, sems = refs
+        z_out, mass_out, nodes, floats, flags, sums, sems = refs[-7:]
     layers, half, depth = modes.shape[1:]
     group = modes.shape[0] // 2
     width, count = 2 * half, high - low
@@ -197,37 +173,49 @@
         copy.start()
         copies.append(copy)
 
-    base = group * layers
-    for k in range(3):
-        move(field.at[pl.ds(k * layers + low, count)], fields.at[k, :, pl.ds(mine, half), :])
-        move(swap.at[pl.ds(base + k * layers + low, count)], fields.at[k, :, pl.ds(other, half), :])
-    held = count if end else count + 1
-    move(modes.at[pl.ds(start, group), pl.ds(low, held)], nodes.at[:, pl.ds(0, held), pl.ds(mine, half), :])
-    for i in range(group):
-        move(swap.at[pl.ds(i * layers + low, held)], nodes.at[i, pl.ds(0, held), pl.ds(other, half), :])
+    span = pl.ds(low, count)
+    for i, (own, theirs) in enumerate(((density, density_swap), (mass, mass_swap))):
+        move(own.at[span], floats.at[i, :, pl.ds(mine, half), :])
+        move(theirs.at[span], floats.at[i, :, pl.ds(other, half), :])
+    move(passive.at[span], flags.at[:, pl.ds(mine, half), :])
+    move(passive_swap.at[span], flags.at[:, pl.ds(other, half), :])
     if end:
-        move(halo.at[pl.ds(0, group)], nodes.at[:, count, pl.ds(mine, half), :])
-        move(halo_swap.at[pl.ds(0, group)], nodes.at[:, count, pl.ds(other, half), :])
         move(halo.at[pl.ds(group, 2)], ghost_mass.at[:, pl.ds(mine, half), :])
         move(halo_swap.at[pl.ds(group, 2)], ghost_mass.at[:, pl.ds(other, half), :])
-    for copy in copies:
+    fields_end = len(copies)
+    held = count if end else count + 1
+    arrivals = []
+    for mode in range(group // 3):
+        before = len(copies)
+        comps, rows = pl.ds(3 * mode, 3), pl.ds(start + 3 * mode, 3)
+        for source, far, at in ((modes, halo if end else None, mine), (modes_swap, halo_swap if end else None, other)):
+            move(source.at[rows, pl.ds(low, held)], nodes.at[comps, pl.ds(0, held), pl.ds(at, half), :])
+            if end:
+                move(far.at[comps], nodes.at[comps, count, pl.ds(at, half), :])
+        arrivals.append(copies[before:])
+    for copy in copies[:fields_end]:
         copy.wait()
 
     squares, products = energy_classes()
     missing = missing_plane((width, depth))
     for i in range(count):
-        mass = fields[1, i]
-        mass_out[i] = mass
-        inverse = 1.0 / (mass + RADIUS_SQ * neighbour_count(missing, low + i, layers, first, last))
-        fields[0, i] = fields[0, i] * inverse
-        fields[2, i] = fields[2, i] * inverse
+        weight = floats[1, i]
+        mass_out[i] = weight
+        inverse = 1.0 / (weight + RADIUS_SQ * neighbour_count(missing, low + i, layers, first, last))
+        design = (1 - flags[i]).astype(jnp.float32) * inverse
+        rho = floats[0, i]
+        floats[0, i] = 3.0 * (1.0 - void_floor) * rho * rho * design
+        floats[1, i] = design
     if end:
-        z_out[z_out.shape[0] - 1] = fields[1, count - 1]
+        z_out[z_out.shape[0] - 1] = mass_out[count - 1]
 
     ring = sums.shape[0]
 
     def transform(step):
         mode, i = divmod(step, count + 1)
+        if i == 0:
+            for copy in arrivals[mode]:
+                copy.wait()
         for comp in range(3):
             here = nodes[3 * mode + comp, i]
             above = shifted(here, 1, 1)
@@ -250,7 +238,7 @@
                             entries[3 * (2 * y + 4 * z) + comp] = near + far
                             entries[3 * (2 * y + 4 * z + 1) + comp] = far - near
                 stiff, inert = element_energies(entries, squares, products)
-                result = fields[(0, i) + span] * stiff - (value * fields[(2, i) + span]) * inert
+                result = floats[(0, i) + span] * stiff - (value * floats[(1, i) + span]) * inert
                 z_out[(mode * count + i,) + span] = result
 
     total = group // 3 * (count + 1)
@@ -512,12 +500,10 @@
     count = lax.axis_size("gx")
     place = jnp.stack([core, (at == 0).astype(jnp.int32), (at == count - 1).astype(jnp.int32)]).astype(jnp.int32)
     across = [(0, 1), (1, 0)]
-    straight = [(2 * i + c, 2 * i - 2 + c) for i in range(1, count) for c in (0, 1)]
-    crossed = [(2 * i + c, 2 * i - 1 - c) for i in range(1, count) for c in (0, 1)]
-    both = ("gx", "gy")
+    downward = [(i, i - 1) for i in range(1, count)]
+    upward = [(i, i + 1) for i in range(count - 1)]
     smem = pl.BlockSpec(memory_space=pltpu.SMEM)
     vmem = pl.BlockSpec(memory_space=pltpu.VMEM)
-    hbm = pl.BlockSpec(memory_space=pltpu.HBM)
     anywhere = pl.BlockSpec(memory_space=pl.ANY)
 
     def planes(n, rows=width):
@@ -535,22 +521,22 @@
             name=name,
         )
 
-    first_node, first_cross, swap, field = kernel(
-        "pack",
-        pack_kernel,
-        (planes(group + 2, half), planes(group + 2, half), planes((group + 3) * layers, half), planes(3 * layers, half)),
-        [smem] + [hbm] * 4,
-        [
-            pltpu.VMEM((2, layers, half, depth), f32),
-            pltpu.VMEM((layers, half, depth), jnp.int32),
-            pltpu.SemaphoreType.DMA((5 + group,)),
-        ],
-        8,
+    operands = []
+    for x in (mode_shapes, density, filter_mass, passive):
+        operands += [pltpu.with_memory_space_constraint(x, pltpu.HBM), lax.ppermute(x, "gy", across)]
+    node, node_crossed = kernel(
+        "first_layer",
+        first_kernel,
+        (planes(group + 2, half), planes(group + 2, half)),
+        [smem] + [anywhere] * 2,
+        [pltpu.SemaphoreType.DMA((4,))],
+        4,
         1,
-    )(place, *(pltpu.with_memory_space_constraint(x, pltpu.HBM) for x in (mode_shapes, density, filter_mass, passive)))
-    swap = lax.ppermute(swap, "gy", across)
-    halo = lax.ppermute(first_node, both, straight)
-    halo_swap = lax.ppermute(first_cross, both, crossed)
+    )(place, operands[0], operands[4])
+    straight = [(2 * i + c, 2 * i - 2 + c) for i in range(1, count) for c in (0, 1)]
+    crossed = [(2 * i + c, 2 * i - 1 - c) for i in range(1, count) for c in (0, 1)]
+    halo = lax.ppermute(node, ("gx", "gy"), straight)
+    halo_swap = lax.ppermute(node_crossed, ("gx", "gy"), crossed)
 
     cuts = (DOWN, layers - UP)
 
@@ -562,23 +548,23 @@
             name,
             partial(energy_kernel, low, high, end),
             outs + (planes(2),) if end else outs,
-            [smem, smem] + [anywhere] * (3 + len(extra)),
+            [smem, smem] + [anywhere] * (8 + len(extra)),
             [
                 pltpu.VMEM((group, n + 1, width, depth), f32),
-                pltpu.VMEM((3, n, width, depth), f32),
+                pltpu.VMEM((2, n, width, depth), f32),
+                pltpu.VMEM((n, width, depth), jnp.int32),
                 pltpu.VMEM((4, 12, width, depth), f32),
-                pltpu.SemaphoreType.DMA((group + 11,)),
+                pltpu.SemaphoreType.DMA((8 + 4 * modes,)),
             ],
             12,
             n * 200,
-        )(place, eigenvalues, mode_shapes, swap, field, *extra)
+        )(place, eigenvalues, *operands, *extra)
 
     za, ma = energies("energies_first", 0, cuts[0])
-    down, halo, halo_swap = lax.optimization_barrier((za, halo, halo_swap))
-    down = lax.ppermute(down, "gx", [(i, i - 1) for i in range(1, count)])
-    zc, mc, ghost_mass = energies("energies_last", cuts[1], layers, halo, halo_swap, ma)
-    up = lax.ppermute(zc, "gx", [(i, i + 1) for i in range(count - 1)])
-    zb, mb = energies("energies_inner", cuts[0], cuts[1], mc)
+    down = lax.ppermute(za, "gx", downward)
+    zb, mb = energies("energies_inner", cuts[0], cuts[1], ma)
+    zc, mc, ghost_mass = energies("energies_last", cuts[1], layers, halo, halo_swap, mb)
+    up = lax.ppermute(zc, "gx", upward)
 
     tables = [pltpu.VMEM((layers, width, depth), f32)] * 2
     sums = jax.ShapeDtypeStruct((6 * modes, 8, 128), f32)
@@ -615,7 +601,7 @@
         200,
     )(place, za, zb, zc, ma, up, ones_in, twos_in, ones_right, twos_right, moments)
     swap_in = lax.ppermute(send, "gy", across)
-    parts = lax.all_to_all(parts, both, 0, 0, tiled=True)
+    parts = lax.all_to_all(parts, ("gx", "gy"), 0, 0, tiled=True)
 
     return kernel(
         "combine",

time: 49.8 us -> 49.6 us (level)
  waiting for transfers between devices: 9.46 us -> 3.74 us
  blocking collectives: 12.6 us -> 16.3 us
  Pallas kernels: 17.8 us -> 18.8 us
  starting transfers between devices: 9.46 us -> 10.2 us
    ppermute x5 -> x8, waiting for transfers between devices: 9.46 us -> 3.74 us  [the longest x1 1.9 us: local(): up = lax.ppermute(zc, 'gx', upward)]
    all_to_all x1, blocking collectives: 12.6 us -> 16.3 us  [local(): parts = lax.all_to_all(parts, ('gx', 'gy'), 0, 0, tiled=True)]
    pallas_call x3, Pallas kernels: 8.49 us -> 10.2 us  [energies(): kernel(name, partial(energy_kernel, low, high, end), outs + (planes(2),)...]
    ppermute x5 -> x8, starting transfers between devices: 9.35 us -> 10.2 us  [the longest x1 5.27 us: local(): up = lax.ppermute(zc, 'gx', upward)]
    pallas_call x1, Pallas kernels: 2.29 us -> 1.58 us  [local(): kernel('first_layer', first_kernel, (planes(group + 2, half), planes(grou...]
  transfers between devices with their start and end apart: 6 -> 9, of which waited for: 4 -> 3; matrix products, arithmetic and copies ran while one was open for 0% -> 0% of each run, Pallas kernels for 24% -> 30%
where the time goes in v3:
time: 49.6 us; the launch traced here: 49.3 us
  Pallas kernels  18.8 us (38%)
  blocking collectives  16.3 us (33%)
  starting transfers between devices  10.2 us (21%)
  waiting for transfers between devices  3.74 us (8%)
    all_to_all x1, blocking collectives, local(): parts = lax.all_to_all(parts, ('gx', 'gy'), 0, 0, tiled=True)  16.3 us
    pallas_call x3, Pallas kernels, energies(): kernel(name, partial(energy_kernel, low, high, end), outs + (planes(2),)...  10.2 us
    ppermute x1, starting transfers between devices, local(): up = lax.ppermute(zc, 'gx', upward)  5.27 us
    pallas_call x1, Pallas kernels, local(): kernel('krylov_left', partial(left_kernel, modes, layers, cuts), (planes(...  2.12 us
    ppermute x1, waiting for transfers between devices, local(): up = lax.ppermute(zc, 'gx', upward)  1.9 us
    pallas_call x1, Pallas kernels, local(): kernel('krylov_inner', partial(inner_kernel, modes, layers, cuts), (plane...  1.85 us
    pallas_call x1, Pallas kernels, local(): kernel('combine', partial(combine_kernel, modes, layers, cuts), jax.Shape...  1.71 us
    pallas_call x1, Pallas kernels, local(): kernel('first_layer', first_kernel, (planes(group + 2, half), planes(grou...  1.58 us
  transfers between devices with their start and end apart: 9, of which 3 were waited for; matrix products, arithmetic and copies ran while one was open for 0% of the time, Pallas kernels for 30%

profile of v3, /device:TPU:0, one launch (start us, length us, event | category | flops | bytes accessed | tf_op | source)
XLA Modules:
  0.0 49.3 jit_solution(11209820341548014781)
XLA Ops:
  0.0 0.0 copy-start
  0.0 0.5 collective-permute-start
  0.5 0.1 collective-permute-start.1
  0.5 0.4 collective-permute-start.3
  1.0 0.1 collective-permute-start.2
  1.0 0.1 pad_add_fusion.refs_0_.place
  1.1 1.6 %first_layer.1 = (f32[11,16,256]{2,1,0:T(8,128)S(1)}, f32[11,16,256]{2,1,0:T(8,128)S(1)}) custom-call(s32[3]{0:T(128)S(1)} %pad_add_fusion.refs_0_.place, f32[18,8,16,256]{3,2,1,0:T(8,128)} %refs_2_.5, f32[8,16,256]{2,1,0:T(8,128)} %refs_6_.5), custom_call_target="tpu_custom_call" | custom-call | flops 1048576 | bytes 1048576 | tf_op jit(solution)/shard_map/first_layer/pallas_call | solution.py:527
  2.7 1.3 %collective-permute-start.4 = (f32[11,16,256]{2,1,0:T(8,128)S(1)}, f32[11,16,256]{2,1,0:T(8,128)S(1)}, u32[]{:S(2)}, u32[]{:S(2)}) collective-permute-start(f32[11,16,256]{2,1,0:T(8,128)S(1)} %get-tuple-element.27), channel_id=1, source_target_pairs={{2,0},{3,1},{4,2},{5,3},{6,4},{7,5},{8,6},{9,7},{10,8},{11,9},{12,... | collective-permute-start | bytes 540680 | tf_op jit(solution)/shard_map/ppermute | solution.py:538
  4.0 1.0 %collective-permute-done.1.refs_5_ = f32[8,16,256]{2,1,0:T(8,128)S(1)} collective-permute-done((f32[8,16,256]{2,1,0:T(8,128)}, f32[8,16,256]{2,1,0:T(8,128)S(1)}, u32[]{:S(2)}, u32[]{:S(2)}) %collective-permute-start.1) | collective-permute-done | bytes 131104 | tf_op jit(solution)/shard_map/ppermute | solution.py:526
  5.0 1.3 %collective-permute-start.5 = (f32[11,16,256]{2,1,0:T(8,128)S(1)}, f32[11,16,256]{2,1,0:T(8,128)S(1)}, u32[]{:S(2)}, u32[]{:S(2)}) collective-permute-start(f32[11,16,256]{2,1,0:T(8,128)S(1)} %get-tuple-element.28), channel_id=1, source_target_pairs={{2,1},{3,0},{4,3},{5,2},{6,5},{7,4},{8,7},{9,6},{10,9},{11,8},{12,... | collective-permute-start | bytes 540680 | tf_op jit(solution)/shard_map/ppermute | solution.py:539
  6.3 0.0 collective-permute-done.3.refs_9_
  6.3 0.0 collective-permute-done.2.refs_7_
  6.3 0.0 collective-permute-done.refs_3_
  6.3 0.0 copy-done
  6.3 3.6 %energies_first.1 = (f32[9,32,256]{2,1,0:T(8,128)S(1)}, f32[3,32,256]{2,1,0:T(8,128)S(1)}) custom-call(s32[3]{0:T(128)S(1)} %pad_add_fusion.refs_0_.place, f32[6]{0:T(128)S(1)} %copy-done, f32[18,8,16,256]{3,2,1,0:T(8,128)} %refs_2_.5, f32[18,8,16,256]{3,2,1,0:T(8,128)S(1)} %collective-permute-done.refs_3_, f32[8,16,256]{2,1,0:T(8,128)} %refs_4_.5, ...), custom_call_target="tpu_custom_call" | custom-call | flops 629145600 | bytes 1048576 | tf_op jit(solution)/shard_map/energies_first/pallas_call | solution.py:547
  9.9 1.3 %collective-permute-start.7 = (f32[9,32,256]{2,1,0:T(8,128)S(1)}, f32[9,32,256]{2,1,0:T(8,128)S(1)}, u32[]{:S(2)}, u32[]{:S(2)}) collective-permute-start(f32[9,32,256]{2,1,0:T(8,128)S(1)} %get-tuple-element.24.za), channel_id=1, source_target_pairs={{2,0},{4,2},{6,4},{8,6},{10,8},{12,10},{14,12},{3,1},{5,3},{7,5},{... | collective-permute-start | bytes 884744 | tf_op jit(solution)/shard_map/ppermute | solution.py:564
  11.2 3.6 %energies_inner.1 = (f32[9,32,256]{2,1,0:T(8,128)S(1)}, f32[3,32,256]{2,1,0:T(8,128)S(1)}) custom-call(s32[3]{0:T(128)S(1)} %pad_add_fusion.refs_0_.place, f32[6]{0:T(128)S(1)} %copy-done, f32[18,8,16,256]{3,2,1,0:T(8,128)} %refs_2_.5, f32[18,8,16,256]{3,2,1,0:T(8,128)S(1)} %collective-permute-done.refs_3_, f32[8,16,256]{2,1,0:T(8,128)} %refs_4_.5, ...), custom_call_target="tpu_custom_call" | custom-call | flops 629145600 | bytes 1048576 | tf_op jit(solution)/shard_map/energies_inner/pallas_call | solution.py:547
  14.8 0.0 collective-permute-done.4.refs_10_
  14.8 0.8 %collective-permute-done.5.refs_11_ = f32[11,16,256]{2,1,0:T(8,128)S(1)} collective-permute-done((f32[11,16,256]{2,1,0:T(8,128)S(1)}, f32[11,16,256]{2,1,0:T(8,128)S(1)}, u32[]{:S(2)}, u32[]{:S(2)}) %collective-permute-start.5) | collective-permute-done | bytes 180256 | tf_op jit(solution)/shard_map/ppermute | solution.py:539
  15.6 3.0 %energies_last.1 = (f32[7,32,256]{2,1,0:T(8,128)S(1)}, f32[2,32,256]{2,1,0:T(8,128)S(1)}, f32[2,32,256]{2,1,0:T(8,128)S(1)}) custom-call(s32[3]{0:T(128)S(1)} %pad_add_fusion.refs_0_.place, f32[6]{0:T(128)S(1)} %copy-done, f32[18,8,16,256]{3,2,1,0:T(8,128)} %refs_2_.5, f32[18,8,16,256]{3,2,1,0:T(8,128)S(1)} %collective-permute-done.refs_3_, ...), custom_call_target="tpu_custom_call" | custom-call | flops 419430400 | bytes 1048576 | tf_op jit(solution)/shard_map/energies_last/pallas_call | solution.py:547
  18.7 5.3 %collective-permute-start.6 = (f32[7,32,256]{2,1,0:T(8,128)S(1)}, f32[7,32,256]{2,1,0:T(8,128)S(1)}, u32[]{:S(2)}, u32[]{:S(2)}) collective-permute-start(f32[7,32,256]{2,1,0:T(8,128)S(1)} %get-tuple-element.30.zc), channel_id=1, source_target_pairs={{0,2},{2,4},{4,6},{6,8},{8,10},{10,12},{12,14},{1,3},{3,5},{5,7},{... | collective-permute-start | bytes 688136 | tf_op jit(solution)/shard_map/ppermute | solution.py:567
  23.9 1.9 %krylov_inner.1 = (f32[18,32,256]{2,1,0:T(8,128)S(1)}, f32[12,32,256]{2,1,0:T(8,128)S(1)}, f32[18,8,128]{2,1,0:T(8,128)S(1)}) custom-call(s32[3]{0:T(128)S(1)} %pad_add_fusion.refs_0_.place, f32[9,32,256]{2,1,0:T(8,128)S(1)} %get-tuple-element.24.za, f32[9,32,256]{2,1,0:T(8,128)S(1)} %get-tuple-element.26.zb, f32[7,32,256]{2,1,0:T(8,128)S(1)} %get-tuple-element.30.zc, ...), custom_call_target="tpu_custom_call" | custom-call | flops 419430400 | bytes 1048576 | tf_op jit(solution)/shard_map/krylov_inner/pallas_call | solution.py:571
  25.8 0.0 collective-permute-done.7.down
  25.8 1.4 %krylov_right.1 = (f32[9,32,256]{2,1,0:T(8,128)S(1)}, f32[9,32,256]{2,1,0:T(8,128)S(1)}, f32[18,8,128]{2,1,0:T(8,128)S(1)}) custom-call(s32[3]{0:T(128)S(1)} %pad_add_fusion.refs_0_.place, f32[7,32,256]{2,1,0:T(8,128)S(1)} %get-tuple-element.30.zc, f32[2,32,256]{2,1,0:T(8,128)S(1)} %get-tuple-element.31.mc, f32[9,32,256]{2,1,0:T(8,128)S(1)} %collective-permute-done.7.down, ...), custom_call_target="tpu_custom_call" | custom-call | flops 209715200 | bytes 1048576 | tf_op jit(solution)/shard_map/krylov_right/pallas_call | solution.py:580
  27.2 1.9 %collective-permute-done.6.up = f32[7,32,256]{2,1,0:T(8,128)S(1)} collective-permute-done((f32[7,32,256]{2,1,0:T(8,128)S(1)}, f32[7,32,256]{2,1,0:T(8,128)S(1)}, u32[]{:S(2)}, u32[]{:S(2)}) %collective-permute-start.6) | collective-permute-done | bytes 229408 | tf_op jit(solution)/shard_map/ppermute | solution.py:567
  29.1 2.1 %krylov_left.1 = (f32[6,32,256]{2,1,0:T(8,128)S(1)}, f32[6,32,256]{2,1,0:T(8,128)S(1)}, f32[72,16,256]{2,1,0:T(8,128)S(1)}, f32[16,8,128]{2,1,0:T(8,128)S(1)}) custom-call(s32[3]{0:T(128)S(1)} %pad_add_fusion.refs_0_.place, f32[9,32,256]{2,1,0:T(8,128)S(1)} %get-tuple-element.24.za, f32[9,32,256]{2,1,0:T(8,128)S(1)} %get-tuple-element.26.zb, ...), custom_call_target="tpu_custom_call" | custom-call | flops 209715200 | bytes 1048576 | tf_op jit(solution)/shard_map/krylov_left/pallas_call | solution.py:589
  31.2 0.1 collective-permute-start.8
  31.3 16.3 %all_to_all.5.parts = f32[16,8,128]{2,1,0:T(8,128)S(1)} all-to-all(f32[16,8,128]{2,1,0:T(8,128)S(1)} %get-tuple-element.39), channel_id=1, replica_groups=mesh['grp'=2,'gx'=8,'gy'=2] {'gx','gy'}, dimensions={0} | all-to-all | bytes 131072 | tf_op jit(solution)/shard_map/all_to_all | solution.py:604
  47.6 0.0 collective-permute-done.8.swap
  47.6 1.7 %combine.1 = f32[6,8,16,256]{3,2,1,0:T(8,128)} custom-call(s32[3]{0:T(128)S(1)} %pad_add_fusion.refs_0_.place, f32[16,8,128]{2,1,0:T(8,128)S(1)} %all_to_all.5.parts, f32[9,32,256]{2,1,0:T(8,128)S(1)} %get-tuple-element.24.za, f32[9,32,256]{2,1,0:T(8,128)S(1)} %get-tuple-element.26.zb, f32[7,32,256]{2,1,0:T(8,128)S(1)} %get-tuple-element.30.zc, ...), custom_call_target="tpu_custom_call" | custom-call | flops 104857600 | bytes 1048576 | tf_op jit(solution)/shard_map/combine/pallas_call | solution.py:606
Async XLA Ops:
  0.0 6.3 %copy-start = (f32[6]{0:T(128)S(1)}, f32[6]{0:T(128)}, u32[]{:S(2)}) copy-start(f32[6]{0:T(128)} %refs_1_.5) | copy-start | bytes 76
  0.0 6.3 %collective-permute-start = (f32[18,8,16,256]{3,2,1,0:T(8,128)}, f32[18,8,16,256]{3,2,1,0:T(8,128)S(1)}, u32[]{:S(2)}, u32[]{:S(2)}) collective-permute-start(f32[18,8,16,256]{3,2,1,0:T(8,128)} %refs_2_.5), channel_id=1, source_target_pairs={{0,1},{1,0},{2,3},{3,2},{4,5},{5,4},{6,7},{7,6},{8,9},{9,8},{10,11... | collective-permute-start | bytes 7077896 | tf_op jit(solution)/shard_map/ppermute | solution.py:526
  0.5 4.6 %collective-permute-start.1 = (f32[8,16,256]{2,1,0:T(8,128)}, f32[8,16,256]{2,1,0:T(8,128)S(1)}, u32[]{:S(2)}, u32[]{:S(2)}) collective-permute-start(f32[8,16,256]{2,1,0:T(8,128)} %refs_4_.5), channel_id=1, source_target_pairs={{0,1},{1,0},{2,3},{3,2},{4,5},{5,4},{6,7},{7,6},{8,9},{9,8},{10,11... | collective-permute-start | bytes 393224 | tf_op jit(solution)/shard_map/ppermute | solution.py:526
  0.5 5.8 %collective-permute-start.3 = (s32[8,16,256]{2,1,0:T(8,128)}, s32[8,16,256]{2,1,0:T(8,128)S(1)}, u32[]{:S(2)}, u32[]{:S(2)}) collective-permute-start(s32[8,16,256]{2,1,0:T(8,128)} %refs_8_.5), channel_id=1, source_target_pairs={{0,1},{1,0},{2,3},{3,2},{4,5},{5,4},{6,7},{7,6},{8,9},{9,8},{10,11... | collective-permute-start | bytes 393224 | tf_op jit(solution)/shard_map/ppermute | solution.py:526
  1.0 5.3 %collective-permute-start.2 = (f32[8,16,256]{2,1,0:T(8,128)}, f32[8,16,256]{2,1,0:T(8,128)S(1)}, u32[]{:S(2)}, u32[]{:S(2)}) collective-permute-start(f32[8,16,256]{2,1,0:T(8,128)} %refs_6_.5), channel_id=1, source_target_pairs={{0,1},{1,0},{2,3},{3,2},{4,5},{5,4},{6,7},{7,6},{8,9},{9,8},{10,11... | collective-permute-start | bytes 393224 | tf_op jit(solution)/shard_map/ppermute | solution.py:526
  2.7 12.1 %collective-permute-start.4 = (f32[11,16,256]{2,1,0:T(8,128)S(1)}, f32[11,16,256]{2,1,0:T(8,128)S(1)}, u32[]{:S(2)}, u32[]{:S(2)}) collective-permute-start(f32[11,16,256]{2,1,0:T(8,128)S(1)} %get-tuple-element.27), channel_id=1, source_target_pairs={{2,0},{3,1},{4,2},{5,3},{6,4},{7,5},{8,6},{9,7},{10,8},{11,9},{12,... | collective-permute-start | bytes 540680 | tf_op jit(solution)/shard_map/ppermute | solution.py:538
  5.0 10.6 %collective-permute-start.5 = (f32[11,16,256]{2,1,0:T(8,128)S(1)}, f32[11,16,256]{2,1,0:T(8,128)S(1)}, u32[]{:S(2)}, u32[]{:S(2)}) collective-permute-start(f32[11,16,256]{2,1,0:T(8,128)S(1)} %get-tuple-element.28), channel_id=1, source_target_pairs={{2,1},{3,0},{4,3},{5,2},{6,5},{7,4},{8,7},{9,6},{10,9},{11,8},{12,... | collective-permute-start | bytes 540680 | tf_op jit(solution)/shard_map/ppermute | solution.py:539
  9.9 15.9 %collective-permute-start.7 = (f32[9,32,256]{2,1,0:T(8,128)S(1)}, f32[9,32,256]{2,1,0:T(8,128)S(1)}, u32[]{:S(2)}, u32[]{:S(2)}) collective-permute-start(f32[9,32,256]{2,1,0:T(8,128)S(1)} %get-tuple-element.24.za), channel_id=1, source_target_pairs={{2,0},{4,2},{6,4},{8,6},{10,8},{12,10},{14,12},{3,1},{5,3},{7,5},{... | collective-permute-start | bytes 884744 | tf_op jit(solution)/shard_map/ppermute | solution.py:564
  18.7 10.4 %collective-permute-start.6 = (f32[7,32,256]{2,1,0:T(8,128)S(1)}, f32[7,32,256]{2,1,0:T(8,128)S(1)}, u32[]{:S(2)}, u32[]{:S(2)}) collective-permute-start(f32[7,32,256]{2,1,0:T(8,128)S(1)} %get-tuple-element.30.zc), channel_id=1, source_target_pairs={{0,2},{2,4},{4,6},{6,8},{8,10},{10,12},{12,14},{1,3},{3,5},{5,7},{... | collective-permute-start | bytes 688136 | tf_op jit(solution)/shard_map/ppermute | solution.py:567
  31.2 16.4 %collective-permute-start.8 = (f32[72,16,256]{2,1,0:T(8,128)S(1)}, f32[72,16,256]{2,1,0:T(8,128)S(1)}, u32[]{:S(2)}, u32[]{:S(2)}) collective-permute-start(f32[72,16,256]{2,1,0:T(8,128)S(1)} %get-tuple-element.42), channel_id=1, source_target_pairs={{0,1},{1,0},{2,3},{3,2},{4,5},{5,4},{6,7},{7,6},{8,9},{9,8},{10,11... | collective-permute-start | bytes 3538952 | tf_op jit(solution)/shard_map/ppermute | solution.py:603

commit v4 on v3

--- a/solution.py
+++ b/solution.py
@@ -140,13 +140,20 @@
     return pl.multiple_of(core * half, half), pl.multiple_of((1 - core) * half, half)
 
 
-def first_kernel(place, modes, mass, straight, crossed, sems):
+def first_kernel(place, modes, density, mass, passive, straight, crossed, own, own_density, own_mass, own_passive, sems):
     group = modes.shape[0] // 2
-    core = place[0]
-    copies = []
-    for target, start in ((straight, core * group), (crossed, (1 - core) * group)):
-        for source, at, count in ((modes.at[pl.ds(start, group), 0], 0, group), (mass.at[pl.ds(0, 2)], group, 2)):
-            copies.append(pltpu.make_async_copy(source, target.at[pl.ds(at, count)], sems.at[len(copies)]))
+    mine, theirs = pl.ds(place[0] * group, group), pl.ds((1 - place[0]) * group, group)
+    moves = [
+        (modes.at[mine, 0], straight.at[pl.ds(0, group)]),
+        (mass.at[pl.ds(0, 2)], straight.at[pl.ds(group, 2)]),
+        (modes.at[theirs, 0], crossed.at[pl.ds(0, group)]),
+        (mass.at[pl.ds(0, 2)], crossed.at[pl.ds(group, 2)]),
+        (modes.at[mine], own),
+        (density, own_density),
+        (mass, own_mass),
+        (passive, own_passive),
+    ]
+    copies = [pltpu.make_async_copy(*move, sems.at[i]) for i, move in enumerate(moves)]
     for copy in copies:
         copy.start()
     for copy in copies:
@@ -157,67 +164,45 @@
     place, eig, modes, modes_swap, density, density_swap, mass, mass_swap, passive, passive_swap = refs[:10]
     if end:
         halo, halo_swap = refs[10:12]
-        z_out, mass_out, ghost_mass, nodes, floats, flags, sums, sems = refs[-8:]
+        z_out, mass_out, ghost_mass, floats, sums = refs[-5:]
     else:
-        z_out, mass_out, nodes, floats, flags, sums, sems = refs[-7:]
-    layers, half, depth = modes.shape[1:]
-    group = modes.shape[0] // 2
+        z_out, mass_out, floats, sums = refs[-4:]
+    group, layers, half, depth = modes.shape
     width, count = 2 * half, high - low
     core, first, last = place[0], place[1], place[2]
-    mine, other = halves(core, half)
     start = core * group
-    copies = []
-
-    def move(source, target):
-        copy = pltpu.make_async_copy(source, target, sems.at[len(copies)])
-        copy.start()
-        copies.append(copy)
-
-    span = pl.ds(low, count)
-    for i, (own, theirs) in enumerate(((density, density_swap), (mass, mass_swap))):
-        move(own.at[span], floats.at[i, :, pl.ds(mine, half), :])
-        move(theirs.at[span], floats.at[i, :, pl.ds(other, half), :])
-    move(passive.at[span], flags.at[:, pl.ds(mine, half), :])
-    move(passive_swap.at[span], flags.at[:, pl.ds(other, half), :])
-    if end:
-        move(halo.at[pl.ds(group, 2)], ghost_mass.at[:, pl.ds(mine, half), :])
-        move(halo_swap.at[pl.ds(group, 2)], ghost_mass.at[:, pl.ds(other, half), :])
-    fields_end = len(copies)
-    held = count if end else count + 1
-    arrivals = []
-    for mode in range(group // 3):
-        before = len(copies)
-        comps, rows = pl.ds(3 * mode, 3), pl.ds(start + 3 * mode, 3)
-        for source, far, at in ((modes, halo if end else None, mine), (modes_swap, halo_swap if end else None, other)):
-            move(source.at[rows, pl.ds(low, held)], nodes.at[comps, pl.ds(0, held), pl.ds(at, half), :])
-            if end:
-                move(far.at[comps], nodes.at[comps, count, pl.ds(at, half), :])
-        arrivals.append(copies[before:])
-    for copy in copies[:fields_end]:
-        copy.wait()
+    lower = core == 0
+
+    def whole(own, other):
+        return jnp.concatenate([jnp.where(lower, own, other), jnp.where(lower, other, own)], axis=0)
 
     squares, products = energy_classes()
     missing = missing_plane((width, depth))
     for i in range(count):
-        weight = floats[1, i]
+        x = low + i
+        weight = whole(mass[x], mass_swap[x])
         mass_out[i] = weight
-        inverse = 1.0 / (weight + RADIUS_SQ * neighbour_count(missing, low + i, layers, first, last))
-        design = (1 - flags[i]).astype(jnp.float32) * inverse
-        rho = floats[0, i]
+        inverse = 1.0 / (weight + RADIUS_SQ * neighbour_count(missing, x, layers, first, last))
+        design = (1 - whole(passive[x], passive_swap[x])).astype(jnp.float32) * inverse
+        rho = whole(density[x], density_swap[x])
         floats[0, i] = 3.0 * (1.0 - void_floor) * rho * rho * design
         floats[1, i] = design
     if end:
         z_out[z_out.shape[0] - 1] = mass_out[count - 1]
+        for i in (0, 1):
+            ghost_mass[i] = whole(halo[group + i], halo_swap[group + i])
+
+    def node(row, x):
+        if x == layers:
+            return whole(halo[row], halo_swap[row])
+        return whole(modes[row, x], modes_swap[start + row, x])
 
     ring = sums.shape[0]
 
     def transform(step):
         mode, i = divmod(step, count + 1)
-        if i == 0:
-            for copy in arrivals[mode]:
-                copy.wait()
         for comp in range(3):
-            here = nodes[3 * mode + comp, i]
+            here = node(3 * mode + comp, low + i)
             above = shifted(here, 1, 1)
             for z, value in ((0, here + above), (1, above - here)):
                 beside = shifted(value, 1, 0)
@@ -359,19 +344,21 @@
 
 
 def plans(layers):
-    inner_ones, inner_twos = list(range(1, layers - 1)), list(range(2, layers - 2))
-    inner = (inner_ones, inner_twos, list(range(layers)), inner_ones, inner_twos, inner_twos, inner_twos[:-1])
-    right_ones, right_twos = [layers - 1, layers, layers + 1], [layers - 2, layers - 1, layers]
-    right = (right_ones, right_twos, [], [layers - 1], right_twos[:2], right_twos[:2], [layers - 3] + right_twos[:2])
+    ones, twos = list(range(1, layers + 2)), list(range(2, layers + 1))
+    inner = twos[:-1]
+    main = (ones, twos, list(range(layers)), list(range(1, layers)), inner, inner, inner)
     left = ([-1, 0], [0, 1], [], [0], [0, 1], [0, 1], [0, 1])
-    return inner, right, left
-
-
-def inner_kernel(modes, layers, cuts, place, za, zb, zc, ma, mb, mc, ones, twos, moments, inverse, counts):
+    return main, left
+
+
+def main_kernel(modes, layers, cuts, place, za, zb, zc, ma, mb, mc, down, ghost_mass, ones, twos, moments, inverse, counts):
     plan = plans(layers)[0]
-    zeroth, mass = z0_layers(cuts, layers, za, zb, zc), mass_layers(cuts, layers, ma, mb, mc)
-    first = Layers((1, layers - 2, ones, 0, layers - 2))
-    second = Layers((2, layers - 4, twos, 0, layers - 4))
+    zeroth = z0_layers(cuts, layers, za, zb, zc)
+    zeroth.where.update(Layers((layers, DOWN, down, 0, DOWN)).where)
+    mass = mass_layers(cuts, layers, ma, mb, mc)
+    mass.where.update(Layers((layers, 2, ghost_mass, 0, 0)).where)
+    first = Layers((1, layers + 1, ones, 0, layers + 1))
+    second = Layers((2, layers - 1, twos, 0, layers - 1))
     moments[...] = jnp.zeros(moments.shape, jnp.float32)
     krylov_step(place, layers, modes, mass, zeroth, first, second, ones, twos, plan, moments, (inverse, counts))
 
@@ -386,31 +373,18 @@
     return Layers((0, a, ma, 0, 0), (a, b - a, mb, 0, 0), (b, layers - b, mc, 0, 0))
 
 
-def right_kernel(modes, layers, cuts, place, zc, mc, down, ghost_mass, ones_in, twos_in, moments_in,
-                 ones, twos, moments, inverse, counts):
+def left_kernel(modes, layers, cuts, place, za, zb, zc, ma, up, ones_in, twos_in, moments_in,
+                ones, twos, send, parts, inverse, counts, moments, sems):
     plan = plans(layers)[1]
-    tail = layers - cuts[1]
-    zeroth = Layers((cuts[1], tail, zc, 0, tail), (layers, DOWN, down, 0, DOWN))
-    mass = Layers((cuts[1], tail, mc, 0, 0), (layers, 2, ghost_mass, 0, 0))
-    first = Layers((1, layers - 2, ones_in, 0, layers - 2), (layers - 1, 3, ones, 0, 3))
-    second = Layers((2, layers - 4, twos_in, 0, layers - 4), (layers - 2, 3, twos, 0, 3))
-    moments[...] = moments_in[...]
-    krylov_step(place, layers, modes, mass, zeroth, first, second, ones, twos, plan, moments, (inverse, counts))
-
-
-def left_kernel(modes, layers, cuts, place, za, zb, zc, ma, up, ones_in, twos_in, ones_right, twos_right, moments_in,
-                ones, twos, send, parts, inverse, counts, moments, sems):
-    plan = plans(layers)[2]
     half = za.shape[1] // 2
     tail = layers - cuts[1]
     pieces = [(za, 0, cuts[0], cuts[0]), (zb, 0, cuts[1] - cuts[0], cuts[1] - cuts[0]), (zc, 0, tail, tail)]
-    pieces += [(ones_in, 0, layers - 2, layers - 2), (ones_right, 0, 3, 1)]
-    pieces += [(twos_in, 0, layers - 4, layers - 4), (twos_right, 0, 3, 2)]
+    pieces += [(ones_in, 0, layers + 1, layers - 1), (twos_in, 0, layers - 1, layers - 2)]
     copies = send_halves(send, place[0], half, modes, pieces, sems)
     zeroth = Layers((-UP, UP, up, 0, UP), (0, cuts[0], za, 0, cuts[0]))
     mass = Layers((-1, 1, up, UP * modes, 0), (0, cuts[0], ma, 0, 0))
-    first = Layers((-1, 2, ones, 0, 2), (1, layers - 2, ones_in, 0, layers - 2))
-    second = Layers((0, 2, twos, 0, 2), (2, layers - 4, twos_in, 0, layers - 4))
+    first = Layers((-1, 2, ones, 0, 2), (1, layers - 1, ones_in, 0, layers + 1))
+    second = Layers((0, 2, twos, 0, 2), (2, layers - 2, twos_in, 0, layers - 1))
     moments[...] = moments_in[...]
     krylov_step(place, layers, modes, mass, zeroth, first, second, ones, twos, plan, moments, (inverse, counts))
     _, other = halves(place[0], half)
@@ -434,7 +408,7 @@
         copy.wait()
 
 
-def combine_kernel(modes, layers, cuts, place, parts, za, zb, zc, ones_in, twos_in, ones_right, twos_right,
+def combine_kernel(modes, layers, cuts, place, parts, za, zb, zc, ones_in, twos_in,
                    ones_left, twos_left, swap, out):
     core = place[0]
     half, depth = out.shape[2:]
@@ -460,8 +434,8 @@
         factors.append([jnp.broadcast_to(c, (8, depth)) for c in (c0, c1, c2)])
 
     zeroth = z0_layers(cuts, layers, za, zb, zc)
-    first = Layers((0, 1, ones_left, 1, 2), (1, layers - 2, ones_in, 0, layers - 2), (layers - 1, 1, ones_right, 0, 3))
-    second = Layers((0, 2, twos_left, 0, 2), (2, layers - 4, twos_in, 0, layers - 4), (layers - 2, 2, twos_right, 0, 3))
+    first = Layers((0, 1, ones_left, 1, 2), (1, layers - 1, ones_in, 0, layers + 1))
+    second = Layers((0, 2, twos_left, 0, 2), (2, layers - 2, twos_in, 0, layers - 1))
     total = swap.shape[0] // modes
     theirs = [
         Layers((0, layers, swap, 0, total)),
@@ -521,18 +495,26 @@
             name=name,
         )
 
-    operands = []
-    for x in (mode_shapes, density, filter_mass, passive):
-        operands += [pltpu.with_memory_space_constraint(x, pltpu.HBM), lax.ppermute(x, "gy", across)]
-    node, node_crossed = kernel(
+    stored = [pltpu.with_memory_space_constraint(x, pltpu.HBM) for x in (mode_shapes, density, filter_mass, passive)]
+    node, node_crossed, *own = kernel(
         "first_layer",
         first_kernel,
-        (planes(group + 2, half), planes(group + 2, half)),
-        [smem] + [anywhere] * 2,
-        [pltpu.SemaphoreType.DMA((4,))],
+        (
+            planes(group + 2, half),
+            planes(group + 2, half),
+            jax.ShapeDtypeStruct((group, layers, half, depth), f32),
+            planes(layers, half),
+            planes(layers, half),
+            jax.ShapeDtypeStruct(passive.shape, passive.dtype),
+        ),
+        [smem] + [anywhere] * 4,
+        [pltpu.SemaphoreType.DMA((8,))],
         4,
         1,
-    )(place, operands[0], operands[4])
+    )(place, *stored)
+    operands = []
+    for mine, x in zip(own, (mode_shapes, density, filter_mass, passive)):
+        operands += [mine, lax.ppermute(x, "gy", across)]
     straight = [(2 * i + c, 2 * i - 2 + c) for i in range(1, count) for c in (0, 1)]
     crossed = [(2 * i + c, 2 * i - 1 - c) for i in range(1, count) for c in (0, 1)]
     halo = lax.ppermute(node, ("gx", "gy"), straight)
@@ -548,13 +530,10 @@
             name,
             partial(energy_kernel, low, high, end),
             outs + (planes(2),) if end else outs,
-            [smem, smem] + [anywhere] * (8 + len(extra)),
+            [smem, smem] + [vmem] * (8 + 2 * end) + [anywhere] * (len(extra) - 2 * end),
             [
-                pltpu.VMEM((group, n + 1, width, depth), f32),
                 pltpu.VMEM((2, n, width, depth), f32),
-                pltpu.VMEM((n, width, depth), jnp.int32),
                 pltpu.VMEM((4, 12, width, depth), f32),
-                pltpu.SemaphoreType.DMA((8 + 4 * modes,)),
             ],
             12,
             n * 200,
@@ -566,26 +545,17 @@
     zc, mc, ghost_mass = energies("energies_last", cuts[1], layers, halo, halo_swap, mb)
     up = lax.ppermute(zc, "gx", upward)
 
-    tables = [pltpu.VMEM((layers, width, depth), f32)] * 2
+    tables = [pltpu.VMEM((layers + 2, width, depth), f32)] * 2
     sums = jax.ShapeDtypeStruct((6 * modes, 8, 128), f32)
     ones_in, twos_in, moments = kernel(
-        "krylov_inner",
-        partial(inner_kernel, modes, layers, cuts),
-        (planes(modes * (layers - 2)), planes(modes * (layers - 4)), sums),
-        [smem] + [vmem] * 6,
+        "krylov_main",
+        partial(main_kernel, modes, layers, cuts),
+        (planes(modes * (layers + 1)), planes(modes * (layers - 1)), sums),
+        [smem] + [vmem] * 8,
         tables,
         12,
         400,
-    )(place, za, zb, zc, ma, mb, mc)
-    ones_right, twos_right, moments = kernel(
-        "krylov_right",
-        partial(right_kernel, modes, layers, cuts),
-        (planes(3 * modes), planes(3 * modes), sums),
-        [smem] + [vmem] * 7,
-        tables,
-        12,
-        200,
-    )(place, zc, mc, down, ghost_mass, ones_in, twos_in, moments)
+    )(place, za, zb, zc, ma, mb, mc, down, ghost_mass)
     ones_left, twos_left, send, parts = kernel(
         "krylov_left",
         partial(left_kernel, modes, layers, cuts),
@@ -595,11 +565,11 @@
             planes(modes * 3 * layers, half),
             jax.ShapeDtypeStruct((2 * count, 8, 128), f32),
         ),
-        [smem] + [vmem] * 10,
-        tables + [pltpu.VMEM((6 * modes, 8, 128), f32), pltpu.SemaphoreType.DMA((7 * modes,))],
+        [smem] + [vmem] * 8,
+        tables + [pltpu.VMEM((6 * modes, 8, 128), f32), pltpu.SemaphoreType.DMA((5 * modes,))],
         12,
         200,
-    )(place, za, zb, zc, ma, up, ones_in, twos_in, ones_right, twos_right, moments)
+    )(place, za, zb, zc, ma, up, ones_in, twos_in, moments)
     swap_in = lax.ppermute(send, "gy", across)
     parts = lax.all_to_all(parts, ("gx", "gy"), 0, 0, tiled=True)
 
@@ -607,11 +577,11 @@
         "combine",
         partial(combine_kernel, modes, layers, cuts),
         jax.ShapeDtypeStruct((2 * modes, layers, half, depth), f32),
-        [smem] + [vmem] * 11,
+        [smem] + [vmem] * 9,
         [],
         12,
         100,
-    )(place, parts, za, zb, zc, ones_in, twos_in, ones_right, twos_right, ones_left, twos_left, swap_in)
+    )(place, parts, za, zb, zc, ones_in, twos_in, ones_left, twos_left, swap_in)
 
 
 def solution(mesh):

time: 49.6 us -> 46.6 us (0.940)
  Pallas kernels: 18.8 us -> 15.2 us
  waiting for transfers between devices: 3.74 us -> 6.7 us
  blocking collectives: 16.3 us -> 14.4 us
    pallas_call x3, Pallas kernels: 10.2 us -> 6.89 us  [energies(): kernel(name, partial(energy_kernel, low, high, end), outs + (planes(2),)...]
    all_to_all x1, blocking collectives: 16.3 us -> 14.4 us  [local(): parts = lax.all_to_all(parts, ('gx', 'gy'), 0, 0, tiled=True)]
    ppermute x1, waiting for transfers between devices: 0.81 us -> 2.57 us  [local(): halo_swap = lax.ppermute(node_crossed, ('gx', 'gy'), crossed)]
    ppermute x1, starting transfers between devices: 5.27 us -> 4.23 us  [local(): up = lax.ppermute(zc, 'gx', upward)]
    ppermute x1, waiting for transfers between devices: 0.01 us -> 0.83 us  [local(): halo = lax.ppermute(node, ('gx', 'gy'), straight)]
    ppermute x1, waiting for transfers between devices: 0.01 us -> 0.82 us  [local(): down = lax.ppermute(za, 'gx', downward)]
    ppermute x1, starting transfers between devices: 0.07 us -> 0.8 us  [local(): swap_in = lax.ppermute(send, 'gy', across)]
    pallas_call x2 -> x1, Pallas kernels: 3.21 us -> 2.52 us  [local(): kernel('krylov_main', partial(main_kernel, modes, layers, cuts), (planes(...]
  transfers between devices with their start and end apart: 9 -> 9, of which waited for: 3 -> 5; matrix products, arithmetic and copies ran while one was open for 0% -> 0% of each run, Pallas kernels for 30% -> 25%
where the time goes in v4:
time: 46.6 us; the launch traced here: 46.4 us
  Pallas kernels  15.2 us (33%)
  blocking collectives  14.4 us (31%)
  starting transfers between devices  9.92 us (21%)
  waiting for transfers between devices  6.7 us (14%)
    all_to_all x1, blocking collectives, local(): parts = lax.all_to_all(parts, ('gx', 'gy'), 0, 0, tiled=True)  14.4 us
    pallas_call x3, Pallas kernels, energies(): kernel(name, partial(energy_kernel, low, high, end), outs + (planes(2),)...  6.89 us
    ppermute x1, starting transfers between devices, local(): up = lax.ppermute(zc, 'gx', upward)  4.23 us
    ppermute x1, waiting for transfers between devices, local(): halo_swap = lax.ppermute(node_crossed, ('gx', 'gy'), crossed)  2.57 us
    pallas_call x1, Pallas kernels, local(): kernel('krylov_main', partial(main_kernel, modes, layers, cuts), (planes(...  2.52 us
    pallas_call x1, Pallas kernels, local(): kernel('first_layer', first_kernel, (planes(group + 2, half), planes(grou...  2.14 us
    ppermute x1, waiting for transfers between devices, local(): up = lax.ppermute(zc, 'gx', upward)  2.01 us
    pallas_call x1, Pallas kernels, local(): kernel('krylov_left', partial(left_kernel, modes, layers, cuts), (planes(...  1.93 us
  transfers between devices with their start and end apart: 9, of which 5 were waited for; matrix products, arithmetic and copies ran while one was open for 0% of the time, Pallas kernels for 25%

profile of v4, /device:TPU:0, one launch (start us, length us, event | category | flops | bytes accessed | tf_op | source)
XLA Modules:
  0.0 46.4 jit_solution(6058776727600949747)
XLA Ops:
  0.0 0.5 collective-permute-start
  0.5 0.1 collective-permute-start.1
  0.5 0.5 collective-permute-start.2
  1.0 0.1 collective-permute-start.3
  1.0 0.1 pad_add_fusion.place.refs_0_
  1.1 0.0 copy-start
  1.1 2.1 %first_layer.1 = (f32[11,16,256]{2,1,0:T(8,128)S(1)}, f32[11,16,256]{2,1,0:T(8,128)S(1)}, f32[9,8,16,256]{3,2,1,0:T(8,128)S(1)}, f32[8,16,256]{2,1,0:T(8,128)S(1...) custom-call(s32[3]{0:T(128)S(1)} %pad_add_fusion.place.refs_0_, f32[18,8,16,256]{3,2,1,0:T(8,128)} %modes.1, ...), custom_call_target="tpu_custom_call" | custom-call | flops 1048576 | bytes 1048576 | tf_op jit(solution)/shard_map/first_layer/pallas_call | solution.py:499
  3.2 1.3 %collective-permute-start.4 = (f32[11,16,256]{2,1,0:T(8,128)S(1)}, f32[11,16,256]{2,1,0:T(8,128)S(1)}, u32[]{:S(2)}, u32[]{:S(2)}) collective-permute-start(f32[11,16,256]{2,1,0:T(8,128)S(1)} %get-tuple-element.32), channel_id=1, source_target_pairs={{2,0},{3,1},{4,2},{5,3},{6,4},{7,5},{8,6},{9,7},{10,8},{11,9},{12,... | collective-permute-start | bytes 540680 | tf_op jit(solution)/shard_map/ppermute | solution.py:520
  4.5 0.5 %collective-permute-done.1.refs_5_ = f32[8,16,256]{2,1,0:T(8,128)S(1)} collective-permute-done((f32[8,16,256]{2,1,0:T(8,128)}, f32[8,16,256]{2,1,0:T(8,128)S(1)}, u32[]{:S(2)}, u32[]{:S(2)}) %collective-permute-start.1) | collective-permute-done | bytes 131104 | tf_op jit(solution)/shard_map/ppermute | solution.py:517
  5.0 1.3 %collective-permute-start.5 = (f32[11,16,256]{2,1,0:T(8,128)S(1)}, f32[11,16,256]{2,1,0:T(8,128)S(1)}, u32[]{:S(2)}, u32[]{:S(2)}) collective-permute-start(f32[11,16,256]{2,1,0:T(8,128)S(1)} %get-tuple-element.33), channel_id=1, source_target_pairs={{2,1},{3,0},{4,3},{5,2},{6,5},{7,4},{8,7},{9,6},{10,9},{11,8},{12,... | collective-permute-start | bytes 540680 | tf_op jit(solution)/shard_map/ppermute | solution.py:521
  6.3 0.0 collective-permute-done.2.refs_7_
  6.3 0.0 collective-permute-done.3.refs_9_
  6.3 0.0 collective-permute-done.refs_3_
  6.3 0.0 copy-done
  6.3 2.5 %energies_first.1 = (f32[9,32,256]{2,1,0:T(8,128)S(1)}, f32[3,32,256]{2,1,0:T(8,128)S(1)}) custom-call(s32[3]{0:T(128)S(1)} %pad_add_fusion.place.refs_0_, f32[6]{0:T(128)S(1)} %copy-done, f32[9,8,16,256]{3,2,1,0:T(8,128)S(1)} %get-tuple-element.25.refs_2_, f32[18,8,16,256]{3,2,1,0:T(8,128)S(1)} %collective-permute-done.refs_3_, ...), custom_call_target="tpu_custom_call" | custom-call | flops 629145600 | bytes 1048576 | tf_op jit(solution)/shard_map/energies_first/pallas_call | solution.py:529
  8.8 1.3 %collective-permute-start.7 = (f32[9,32,256]{2,1,0:T(8,128)S(1)}, f32[9,32,256]{2,1,0:T(8,128)S(1)}, u32[]{:S(2)}, u32[]{:S(2)}) collective-permute-start(f32[9,32,256]{2,1,0:T(8,128)S(1)} %get-tuple-element.29.za), channel_id=1, source_target_pairs={{2,0},{4,2},{6,4},{8,6},{10,8},{12,10},{14,12},{3,1},{5,3},{7,5},{... | collective-permute-start | bytes 884744 | tf_op jit(solution)/shard_map/ppermute | solution.py:543
  10.1 2.5 %energies_inner.1 = (f32[9,32,256]{2,1,0:T(8,128)S(1)}, f32[3,32,256]{2,1,0:T(8,128)S(1)}) custom-call(s32[3]{0:T(128)S(1)} %pad_add_fusion.place.refs_0_, f32[6]{0:T(128)S(1)} %copy-done, f32[9,8,16,256]{3,2,1,0:T(8,128)S(1)} %get-tuple-element.25.refs_2_, f32[18,8,16,256]{3,2,1,0:T(8,128)S(1)} %collective-permute-done.refs_3_, ...), custom_call_target="tpu_custom_call" | custom-call | flops 629145600 | bytes 1048576 | tf_op jit(solution)/shard_map/energies_inner/pallas_call | solution.py:529
  12.6 0.8 %collective-permute-done.4.refs_10_ = f32[11,16,256]{2,1,0:T(8,128)S(1)} collective-permute-done((f32[11,16,256]{2,1,0:T(8,128)S(1)}, f32[11,16,256]{2,1,0:T(8,128)S(1)}, u32[]{:S(2)}, u32[]{:S(2)}) %collective-permute-start.4) | collective-permute-done | bytes 180256 | tf_op jit(solution)/shard_map/ppermute | solution.py:520
  13.5 2.6 %collective-permute-done.5.refs_11_ = f32[11,16,256]{2,1,0:T(8,128)S(1)} collective-permute-done((f32[11,16,256]{2,1,0:T(8,128)S(1)}, f32[11,16,256]{2,1,0:T(8,128)S(1)}, u32[]{:S(2)}, u32[]{:S(2)}) %collective-permute-start.5) | collective-permute-done | bytes 180256 | tf_op jit(solution)/shard_map/ppermute | solution.py:521
  16.0 1.9 %energies_last.1 = (f32[7,32,256]{2,1,0:T(8,128)S(1)}, f32[2,32,256]{2,1,0:T(8,128)S(1)}, f32[2,32,256]{2,1,0:T(8,128)S(1)}) custom-call(s32[3]{0:T(128)S(1)} %pad_add_fusion.place.refs_0_, f32[6]{0:T(128)S(1)} %copy-done, f32[9,8,16,256]{3,2,1,0:T(8,128)S(1)} %get-tuple-element.25.refs_2_, f32[18,8,16,256]{3,2,1,0:T(8,128)S(1)} %collective-permute-done.refs_3_, ...), custom_call_target="tpu_custom_call" | custom-call | flops 419430400 | bytes 1048576 | tf_op jit(solution)/shard_map/energies_last/pallas_call | solution.py:529
  18.0 4.2 %collective-permute-start.6 = (f32[7,32,256]{2,1,0:T(8,128)S(1)}, f32[7,32,256]{2,1,0:T(8,128)S(1)}, u32[]{:S(2)}, u32[]{:S(2)}) collective-permute-start(f32[7,32,256]{2,1,0:T(8,128)S(1)} %get-tuple-element.35.zc), channel_id=1, source_target_pairs={{0,2},{2,4},{4,6},{6,8},{8,10},{10,12},{12,14},{1,3},{3,5},{5,7},{... | collective-permute-start | bytes 688136 | tf_op jit(solution)/shard_map/ppermute | solution.py:546
  22.2 0.8 %collective-permute-done.7.down = f32[9,32,256]{2,1,0:T(8,128)S(1)} collective-permute-done((f32[9,32,256]{2,1,0:T(8,128)S(1)}, f32[9,32,256]{2,1,0:T(8,128)S(1)}, u32[]{:S(2)}, u32[]{:S(2)}) %collective-permute-start.7) | collective-permute-done | bytes 294944 | tf_op jit(solution)/shard_map/ppermute | solution.py:543
  23.0 2.5 %krylov_main.1 = (f32[27,32,256]{2,1,0:T(8,128)S(1)}, f32[21,32,256]{2,1,0:T(8,128)S(1)}, f32[18,8,128]{2,1,0:T(8,128)S(1)}) custom-call(s32[3]{0:T(128)S(1)} %pad_add_fusion.place.refs_0_, f32[9,32,256]{2,1,0:T(8,128)S(1)} %get-tuple-element.29.za, f32[9,32,256]{2,1,0:T(8,128)S(1)} %get-tuple-element.31.zb, f32[7,32,256]{2,1,0:T(8,128)S(1)} %get-tuple-element.35.zc, ...), custom_call_target="tpu_custom_call" | custom-call | flops 419430400 | bytes 1048576 | tf_op jit(solution)/shard_map/krylov_main/pallas_call | solution.py:550
  25.5 2.0 %collective-permute-done.6.up = f32[7,32,256]{2,1,0:T(8,128)S(1)} collective-permute-done((f32[7,32,256]{2,1,0:T(8,128)S(1)}, f32[7,32,256]{2,1,0:T(8,128)S(1)}, u32[]{:S(2)}, u32[]{:S(2)}) %collective-permute-start.6) | collective-permute-done | bytes 229408 | tf_op jit(solution)/shard_map/ppermute | solution.py:546
  27.5 1.9 %krylov_left.1 = (f32[6,32,256]{2,1,0:T(8,128)S(1)}, f32[6,32,256]{2,1,0:T(8,128)S(1)}, f32[72,16,256]{2,1,0:T(8,128)S(1)}, f32[16,8,128]{2,1,0:T(8,128)S(1)}) custom-call(s32[3]{0:T(128)S(1)} %pad_add_fusion.place.refs_0_, f32[9,32,256]{2,1,0:T(8,128)S(1)} %get-tuple-element.29.za, f32[9,32,256]{2,1,0:T(8,128)S(1)} %get-tuple-element.31.zb, ...), custom_call_target="tpu_custom_call" | custom-call | flops 209715200 | bytes 1048576 | tf_op jit(solution)/shard_map/krylov_left/pallas_call | solution.py:559
  29.5 0.8 %collective-permute-start.8 = (f32[72,16,256]{2,1,0:T(8,128)S(1)}, f32[72,16,256]{2,1,0:T(8,128)S(1)}, u32[]{:S(2)}, u32[]{:S(2)}) collective-permute-start(f32[72,16,256]{2,1,0:T(8,128)S(1)} %get-tuple-element.44), channel_id=1, source_target_pairs={{0,1},{1,0},{2,3},{3,2},{4,5},{5,4},{6,7},{7,6},{8,9},{9,8},{10,11... | collective-permute-start | bytes 3538952 | tf_op jit(solution)/shard_map/ppermute | solution.py:573
  30.3 14.4 %all_to_all.5.parts = f32[16,8,128]{2,1,0:T(8,128)S(1)} all-to-all(f32[16,8,128]{2,1,0:T(8,128)S(1)} %get-tuple-element.41), channel_id=1, replica_groups=mesh['grp'=2,'gx'=8,'gy'=2] {'gx','gy'}, dimensions={0} | all-to-all | bytes 131072 | tf_op jit(solution)/shard_map/all_to_all | solution.py:574
  44.7 0.0 collective-permute-done.8.swap
  44.7 1.7 %combine.1 = f32[6,8,16,256]{3,2,1,0:T(8,128)} custom-call(s32[3]{0:T(128)S(1)} %pad_add_fusion.place.refs_0_, f32[16,8,128]{2,1,0:T(8,128)S(1)} %all_to_all.5.parts, f32[9,32,256]{2,1,0:T(8,128)S(1)} %get-tuple-element.29.za, f32[9,32,256]{2,1,0:T(8,128)S(1)} %get-tuple-element.31.zb, f32[7,32,256]{2,1,0:T(8,128)S(1)} %get-tuple-element.35.zc, ...), custom_call_target="tpu_custom_call" | custom-call | flops 104857600 | bytes 1048576 | tf_op jit(solution)/shard_map/combine/pallas_call | solution.py:576
Async XLA Ops:
  0.0 6.3 %collective-permute-start = (f32[18,8,16,256]{3,2,1,0:T(8,128)}, f32[18,8,16,256]{3,2,1,0:T(8,128)S(1)}, u32[]{:S(2)}, u32[]{:S(2)}) collective-permute-start(f32[18,8,16,256]{3,2,1,0:T(8,128)} %modes.1), channel_id=1, source_target_pairs={{0,1},{1,0},{2,3},{3,2},{4,5},{5,4},{6,7},{7,6},{8,9},{9,8},{10,11... | collective-permute-start | bytes 7077896 | tf_op jit(solution)/shard_map/ppermute | solution.py:517
  0.5 4.6 %collective-permute-start.1 = (f32[8,16,256]{2,1,0:T(8,128)}, f32[8,16,256]{2,1,0:T(8,128)S(1)}, u32[]{:S(2)}, u32[]{:S(2)}) collective-permute-start(f32[8,16,256]{2,1,0:T(8,128)} %density.1), channel_id=1, source_target_pairs={{0,1},{1,0},{2,3},{3,2},{4,5},{5,4},{6,7},{7,6},{8,9},{9,8},{10,11... | collective-permute-start | bytes 393224 | tf_op jit(solution)/shard_map/ppermute | solution.py:517
  0.5 5.8 %collective-permute-start.2 = (f32[8,16,256]{2,1,0:T(8,128)}, f32[8,16,256]{2,1,0:T(8,128)S(1)}, u32[]{:S(2)}, u32[]{:S(2)}) collective-permute-start(f32[8,16,256]{2,1,0:T(8,128)} %mass.1), channel_id=1, source_target_pairs={{0,1},{1,0},{2,3},{3,2},{4,5},{5,4},{6,7},{7,6},{8,9},{9,8},{10,11... | collective-permute-start | bytes 393224 | tf_op jit(solution)/shard_map/ppermute | solution.py:517
  1.0 5.3 %collective-permute-start.3 = (s32[8,16,256]{2,1,0:T(8,128)}, s32[8,16,256]{2,1,0:T(8,128)S(1)}, u32[]{:S(2)}, u32[]{:S(2)}) collective-permute-start(s32[8,16,256]{2,1,0:T(8,128)} %passive.1), channel_id=1, source_target_pairs={{0,1},{1,0},{2,3},{3,2},{4,5},{5,4},{6,7},{7,6},{8,9},{9,8},{10,11... | collective-permute-start | bytes 393224 | tf_op jit(solution)/shard_map/ppermute | solution.py:517
  1.1 5.2 %copy-start = (f32[6]{0:T(128)S(1)}, f32[6]{0:T(128)}, u32[]{:S(2)}) copy-start(f32[6]{0:T(128)} %refs_1_.5) | copy-start | bytes 76
  3.2 10.2 %collective-permute-start.4 = (f32[11,16,256]{2,1,0:T(8,128)S(1)}, f32[11,16,256]{2,1,0:T(8,128)S(1)}, u32[]{:S(2)}, u32[]{:S(2)}) collective-permute-start(f32[11,16,256]{2,1,0:T(8,128)S(1)} %get-tuple-element.32), channel_id=1, source_target_pairs={{2,0},{3,1},{4,2},{5,3},{6,4},{7,5},{8,6},{9,7},{10,8},{11,9},{12,... | collective-permute-start | bytes 540680 | tf_op jit(solution)/shard_map/ppermute | solution.py:520
  5.0 11.0 %collective-permute-start.5 = (f32[11,16,256]{2,1,0:T(8,128)S(1)}, f32[11,16,256]{2,1,0:T(8,128)S(1)}, u32[]{:S(2)}, u32[]{:S(2)}) collective-permute-start(f32[11,16,256]{2,1,0:T(8,128)S(1)} %get-tuple-element.33), channel_id=1, source_target_pairs={{2,1},{3,0},{4,3},{5,2},{6,5},{7,4},{8,7},{9,6},{10,9},{11,8},{12,... | collective-permute-start | bytes 540680 | tf_op jit(solution)/shard_map/ppermute | solution.py:521
  8.8 14.2 %collective-permute-start.7 = (f32[9,32,256]{2,1,0:T(8,128)S(1)}, f32[9,32,256]{2,1,0:T(8,128)S(1)}, u32[]{:S(2)}, u32[]{:S(2)}) collective-permute-start(f32[9,32,256]{2,1,0:T(8,128)S(1)} %get-tuple-element.29.za), channel_id=1, source_target_pairs={{2,0},{4,2},{6,4},{8,6},{10,8},{12,10},{14,12},{3,1},{5,3},{7,5},{... | collective-permute-start | bytes 884744 | tf_op jit(solution)/shard_map/ppermute | solution.py:543
  18.0 9.6 %collective-permute-start.6 = (f32[7,32,256]{2,1,0:T(8,128)S(1)}, f32[7,32,256]{2,1,0:T(8,128)S(1)}, u32[]{:S(2)}, u32[]{:S(2)}) collective-permute-start(f32[7,32,256]{2,1,0:T(8,128)S(1)} %get-tuple-element.35.zc), channel_id=1, source_target_pairs={{0,2},{2,4},{4,6},{6,8},{8,10},{10,12},{12,14},{1,3},{3,5},{5,7},{... | collective-permute-start | bytes 688136 | tf_op jit(solution)/shard_map/ppermute | solution.py:546
  29.5 15.2 %collective-permute-start.8 = (f32[72,16,256]{2,1,0:T(8,128)S(1)}, f32[72,16,256]{2,1,0:T(8,128)S(1)}, u32[]{:S(2)}, u32[]{:S(2)}) collective-permute-start(f32[72,16,256]{2,1,0:T(8,128)S(1)} %get-tuple-element.44), channel_id=1, source_target_pairs={{0,1},{1,0},{2,3},{3,2},{4,5},{5,4},{6,7},{7,6},{8,9},{9,8},{10,11... | collective-permute-start | bytes 3538952 | tf_op jit(solution)/shard_map/ppermute | solution.py:573

commit v5 on v4

--- a/solution.py
+++ b/solution.py
@@ -140,15 +140,15 @@
     return pl.multiple_of(core * half, half), pl.multiple_of((1 - core) * half, half)
 
 
-def first_kernel(place, modes, density, mass, passive, straight, crossed, own, own_density, own_mass, own_passive, sems):
+def first_kernel(place, modes, density, mass, passive, halo, own, own_density, own_mass, own_passive, sems):
     group = modes.shape[0] // 2
-    mine, theirs = pl.ds(place[0] * group, group), pl.ds((1 - place[0]) * group, group)
-    moves = [
-        (modes.at[mine, 0], straight.at[pl.ds(0, group)]),
-        (mass.at[pl.ds(0, 2)], straight.at[pl.ds(group, 2)]),
-        (modes.at[theirs, 0], crossed.at[pl.ds(0, group)]),
-        (mass.at[pl.ds(0, 2)], crossed.at[pl.ds(group, 2)]),
-        (modes.at[mine], own),
+    moves = []
+    for core in (0, 1):
+        at = core * (group + 2)
+        moves.append((modes.at[pl.ds(core * group, group), 0], halo.at[pl.ds(at, group)]))
+        moves.append((mass.at[pl.ds(0, 2)], halo.at[pl.ds(at + group, 2)]))
+    moves += [
+        (modes.at[pl.ds(place[0] * group, group)], own),
         (density, own_density),
         (mass, own_mass),
         (passive, own_passive),
@@ -163,7 +163,7 @@
 def energy_kernel(low, high, end, *refs):
     place, eig, modes, modes_swap, density, density_swap, mass, mass_swap, passive, passive_swap = refs[:10]
     if end:
-        halo, halo_swap = refs[10:12]
+        halo = refs[10]
         z_out, mass_out, ghost_mass, floats, sums = refs[-5:]
     else:
         z_out, mass_out, floats, sums = refs[-4:]
@@ -190,11 +190,11 @@
     if end:
         z_out[z_out.shape[0] - 1] = mass_out[count - 1]
         for i in (0, 1):
-            ghost_mass[i] = whole(halo[group + i], halo_swap[group + i])
+            ghost_mass[i] = jnp.concatenate([halo[group + i], halo[2 * group + 2 + i]], axis=0)
 
     def node(row, x):
         if x == layers:
-            return whole(halo[row], halo_swap[row])
+            return jnp.concatenate([halo[row], halo[group + 2 + row]], axis=0)
         return whole(modes[row, x], modes_swap[start + row, x])
 
     ring = sums.shape[0]
@@ -328,18 +328,16 @@
     lax.fori_loop(0, modes, one_mode, 0)
 
 
-def send_halves(target, core, half, modes, parts, sems):
+def send_halves(target, core, half, modes, parts, sems, used):
     _, other = halves(core, half)
     total = target.shape[0] // modes
     copies = []
     for mode in range(modes):
-        at = mode * total
-        for ref, offset, stride, count in parts:
+        for ref, offset, stride, count, at in parts:
             source = ref.at[pl.ds(mode * stride + offset, count), pl.ds(other, half), :]
-            copies.append(pltpu.make_async_copy(source, target.at[pl.ds(at, count)], sems.at[len(copies)]))
-            at += count
-    for copy in copies:
-        copy.start()
+            sem = sems.at[used + len(copies)]
+            copies.append(pltpu.make_async_copy(source, target.at[pl.ds(mode * total + at, count)], sem))
+            copies[-1].start()
     return copies
 
 
@@ -351,7 +349,8 @@
     return main, left
 
 
-def main_kernel(modes, layers, cuts, place, za, zb, zc, ma, mb, mc, down, ghost_mass, ones, twos, moments, inverse, counts):
+def main_kernel(modes, layers, cuts, place, za, zb, zc, ma, mb, mc, down, ghost_mass,
+                ones, twos, moments, send, inverse, counts, sems):
     plan = plans(layers)[0]
     zeroth = z0_layers(cuts, layers, za, zb, zc)
     zeroth.where.update(Layers((layers, DOWN, down, 0, DOWN)).where)
@@ -360,7 +359,15 @@
     first = Layers((1, layers + 1, ones, 0, layers + 1))
     second = Layers((2, layers - 1, twos, 0, layers - 1))
     moments[...] = jnp.zeros(moments.shape, jnp.float32)
+    a, b = cuts
+    half = za.shape[1] // 2
+    known = [(za, 0, a, a, 0), (zb, 0, b - a, b - a, a), (zc, 0, layers - b, layers - b, b)]
+    copies = send_halves(send, place[0], half, modes, known, sems, 0)
     krylov_step(place, layers, modes, mass, zeroth, first, second, ones, twos, plan, moments, (inverse, counts))
+    made = [(ones, 0, layers + 1, layers - 1, layers), (twos, 0, layers - 1, layers - 2, 2 * layers - 1)]
+    copies += send_halves(send, place[0], half, modes, made, sems, len(copies))
+    for copy in copies:
+        copy.wait()
 
 
 def z0_layers(cuts, layers, za, zb, zc):
@@ -373,20 +380,16 @@
     return Layers((0, a, ma, 0, 0), (a, b - a, mb, 0, 0), (b, layers - b, mc, 0, 0))
 
 
-def left_kernel(modes, layers, cuts, place, za, zb, zc, ma, up, ones_in, twos_in, moments_in,
-                ones, twos, send, parts, inverse, counts, moments, sems):
+def left_kernel(modes, layers, cuts, place, za, ma, up, ones_in, twos_in, moments_in, _,
+                ones, twos, send, parts, inverse, counts, moments):
     plan = plans(layers)[1]
-    half = za.shape[1] // 2
-    tail = layers - cuts[1]
-    pieces = [(za, 0, cuts[0], cuts[0]), (zb, 0, cuts[1] - cuts[0], cuts[1] - cuts[0]), (zc, 0, tail, tail)]
-    pieces += [(ones_in, 0, layers + 1, layers - 1), (twos_in, 0, layers - 1, layers - 2)]
-    copies = send_halves(send, place[0], half, modes, pieces, sems)
     zeroth = Layers((-UP, UP, up, 0, UP), (0, cuts[0], za, 0, cuts[0]))
     mass = Layers((-1, 1, up, UP * modes, 0), (0, cuts[0], ma, 0, 0))
     first = Layers((-1, 2, ones, 0, 2), (1, layers - 1, ones_in, 0, layers + 1))
     second = Layers((0, 2, twos, 0, 2), (2, layers - 2, twos_in, 0, layers - 1))
     moments[...] = moments_in[...]
     krylov_step(place, layers, modes, mass, zeroth, first, second, ones, twos, plan, moments, (inverse, counts))
+    half = za.shape[1] // 2
     _, other = halves(place[0], half)
     total = send.shape[0] // modes
     for mode in range(modes):
@@ -394,33 +397,31 @@
         send[at] = ones[2 * mode + 1, pl.ds(other, half), :]
         send[at + 1] = twos[2 * mode, pl.ds(other, half), :]
         send[at + 2] = twos[2 * mode + 1, pl.ds(other, half), :]
-    row = lax.broadcasted_iota(jnp.int32, (8, 128), 0)
-    lane = lax.broadcasted_iota(jnp.int32, (8, 128), 1)
-    block = jnp.zeros((8, 128), jnp.float32)
-    for mode in range(modes):
-        for k in range(6):
-            line = jnp.sum(moments[mode * 6 + k], axis=0, keepdims=True)
-            total = jnp.sum(line, axis=1, keepdims=True)
-            block = jnp.where((row == mode) & (lane == k), total, block)
+    lines = [jnp.sum(moments[i], axis=0, keepdims=True) for i in range(6 * modes)]
+    lines = jnp.concatenate(lines + [jnp.zeros((-len(lines) % 8, 128), jnp.float32)], axis=0)
+    totals = jnp.sum(lines, axis=1, keepdims=True)
+    row = lax.broadcasted_iota(jnp.int32, lines.shape, 0)
+    lane = lax.broadcasted_iota(jnp.int32, lines.shape, 1)
+    line = jnp.sum(jnp.where(row == lane, totals, 0.0), axis=0, keepdims=True)
+    block = jnp.broadcast_to(line, (8, 128))
     for i in range(parts.shape[0]):
         parts[i] = block
-    for copy in copies:
-        copy.wait()
 
 
 def combine_kernel(modes, layers, cuts, place, parts, za, zb, zc, ones_in, twos_in,
-                   ones_left, twos_left, swap, out):
+                   ones_left, twos_left, swap, out_hbm, out, sems):
     core = place[0]
     half, depth = out.shape[2:]
     mine, _ = halves(core, half)
     shape = (8, 128)
     lane = lax.broadcasted_iota(jnp.int32, shape, 1)
+    row = lax.broadcasted_iota(jnp.int32, shape, 0)
     factors = []
     for c in (0, 1):
         block = parts[c]
         for i in range(2 + c, parts.shape[0], 2):
             block = block + parts[i]
-        m = [jnp.sum(jnp.where(lane == k, block, 0.0), axis=1, keepdims=True) for k in range(6)]
+        m = [jnp.sum(jnp.where(lane == 6 * row + k, block, 0.0), axis=1, keepdims=True) for k in range(6)]
         one, two = m[2] / m[1], m[3] / m[1]
         pivot = m[3] - one * m[2]
         cross = m[4] - two * m[2]
@@ -443,6 +444,7 @@
         Layers((0, 2, swap, 3 * layers - 2, total), (2, layers - 2, swap, 2 * layers - 1, total)),
     ]
 
+    copies = []
     for slot in (0, 1):
         for mode in range(modes):
             target = slot * modes + mode
@@ -462,6 +464,11 @@
                 for x in range(layers):
                     planes = [field(mode, x) for field in theirs]
                     out[target, x] = a * planes[0] + b * planes[1] + c * planes[2]
+
+            copies.append(pltpu.make_async_copy(out.at[target], out_hbm.at[target], sems.at[target]))
+            copies[-1].start()
+    for copy in copies:
+        copy.wait()
 
 
 def local(mode_shapes, eigenvalues, density, filter_mass, passive):
@@ -483,12 +490,13 @@
     def planes(n, rows=width):
         return jax.ShapeDtypeStruct((n, rows, depth), f32)
 
-    def kernel(name, body, outs, in_specs, scratch, limit, work):
+    def kernel(name, body, outs, in_specs, scratch, limit, work, out_spec=vmem, aliases={}):
         return pl.pallas_call(
             body,
             out_shape=outs,
             in_specs=in_specs,
-            out_specs=jax.tree.map(lambda _: vmem, outs),
+            out_specs=jax.tree.map(lambda _: out_spec, outs),
+            input_output_aliases=aliases,
             scratch_shapes=scratch,
             compiler_params=pltpu.CompilerParams(vmem_limit_bytes=limit * 2**20),
             cost_estimate=pl.CostEstimate(flops=work * 2**20, bytes_accessed=2**20, transcendentals=0),
@@ -496,12 +504,11 @@
         )
 
     stored = [pltpu.with_memory_space_constraint(x, pltpu.HBM) for x in (mode_shapes, density, filter_mass, passive)]
-    node, node_crossed, *own = kernel(
+    halo, *own = kernel(
         "first_layer",
         first_kernel,
         (
-            planes(group + 2, half),
-            planes(group + 2, half),
+            planes(2 * group + 4, half),
             jax.ShapeDtypeStruct((group, layers, half, depth), f32),
             planes(layers, half),
             planes(layers, half),
@@ -515,10 +522,7 @@
     operands = []
     for mine, x in zip(own, (mode_shapes, density, filter_mass, passive)):
         operands += [mine, lax.ppermute(x, "gy", across)]
-    straight = [(2 * i + c, 2 * i - 2 + c) for i in range(1, count) for c in (0, 1)]
-    crossed = [(2 * i + c, 2 * i - 1 - c) for i in range(1, count) for c in (0, 1)]
-    halo = lax.ppermute(node, ("gx", "gy"), straight)
-    halo_swap = lax.ppermute(node_crossed, ("gx", "gy"), crossed)
+    halo = lax.ppermute(halo, "gx", downward)
 
     cuts = (DOWN, layers - UP)
 
@@ -530,7 +534,7 @@
             name,
             partial(energy_kernel, low, high, end),
             outs + (planes(2),) if end else outs,
-            [smem, smem] + [vmem] * (8 + 2 * end) + [anywhere] * (len(extra) - 2 * end),
+            [smem, smem] + [vmem] * (8 + end) + [anywhere] * (len(extra) - end),
             [
                 pltpu.VMEM((2, n, width, depth), f32),
                 pltpu.VMEM((4, 12, width, depth), f32),
@@ -542,17 +546,19 @@
     za, ma = energies("energies_first", 0, cuts[0])
     down = lax.ppermute(za, "gx", downward)
     zb, mb = energies("energies_inner", cuts[0], cuts[1], ma)
-    zc, mc, ghost_mass = energies("energies_last", cuts[1], layers, halo, halo_swap, mb)
+    halo, _ = lax.optimization_barrier((halo, mb))
+    halo = lax.all_to_all(halo, "gy", 0, 0, tiled=True)
+    zc, mc, ghost_mass = energies("energies_last", cuts[1], layers, halo, mb)
     up = lax.ppermute(zc, "gx", upward)
 
     tables = [pltpu.VMEM((layers + 2, width, depth), f32)] * 2
     sums = jax.ShapeDtypeStruct((6 * modes, 8, 128), f32)
-    ones_in, twos_in, moments = kernel(
+    ones_in, twos_in, moments, send = kernel(
         "krylov_main",
         partial(main_kernel, modes, layers, cuts),
-        (planes(modes * (layers + 1)), planes(modes * (layers - 1)), sums),
+        (planes(modes * (layers + 1)), planes(modes * (layers - 1)), sums, planes(modes * 3 * layers, half)),
         [smem] + [vmem] * 8,
-        tables,
+        tables + [pltpu.SemaphoreType.DMA((5 * modes,))],
         12,
         400,
     )(place, za, zb, zc, ma, mb, mc, down, ghost_mass)
@@ -565,11 +571,12 @@
             planes(modes * 3 * layers, half),
             jax.ShapeDtypeStruct((2 * count, 8, 128), f32),
         ),
-        [smem] + [vmem] * 8,
-        tables + [pltpu.VMEM((6 * modes, 8, 128), f32), pltpu.SemaphoreType.DMA((5 * modes,))],
+        [smem] + [vmem] * 7,
+        tables + [pltpu.VMEM((6 * modes, 8, 128), f32)],
         12,
         200,
-    )(place, za, zb, zc, ma, up, ones_in, twos_in, moments)
+        aliases={7: 2},
+    )(place, za, ma, up, ones_in, twos_in, moments, send)
     swap_in = lax.ppermute(send, "gy", across)
     parts = lax.all_to_all(parts, ("gx", "gy"), 0, 0, tiled=True)
 
@@ -578,9 +585,10 @@
         partial(combine_kernel, modes, layers, cuts),
         jax.ShapeDtypeStruct((2 * modes, layers, half, depth), f32),
         [smem] + [vmem] * 9,
-        [],
+        [pltpu.VMEM((2 * modes, layers, half, depth), f32), pltpu.SemaphoreType.DMA((2 * modes,))],
         12,
         100,
+        anywhere,
     )(place, parts, za, zb, zc, ones_in, twos_in, ones_left, twos_left, swap_in)
 
 

time: 46.6 us -> 48.2 us (1.034)
  blocking collectives: 14.4 us -> 16.7 us
  starting transfers between devices: 9.92 us -> 8.52 us
  waiting for transfers between devices: 6.7 us -> 7.53 us
    all_to_all x0 -> x1, blocking collectives: none -> 3.99 us  [local(): halo = lax.all_to_all(halo, 'gy', 0, 0, tiled=True)]
    all_to_all x1, blocking collectives: 14.4 us -> 12.7 us  [local(): parts = lax.all_to_all(parts, ('gx', 'gy'), 0, 0, tiled=True)]
    ppermute x2 -> x1, starting transfers between devices: 2.57 us -> 1.29 us  [local(): halo = lax.ppermute(halo, 'gx', downward)]
    ppermute x1, waiting for transfers between devices: 0.82 us -> 0.01 us  [local(): down = lax.ppermute(za, 'gx', downward)]
    ppermute x4, waiting for transfers between devices: 0.48 us -> 1.26 us  [local(): operands += [mine, lax.ppermute(x, 'gy', across)]]
    ppermute x2 -> x1, waiting for transfers between devices: 3.4 us -> 4.14 us  [local(): halo = lax.ppermute(halo, 'gx', downward)]
    ppermute x1, starting transfers between devices: 0.8 us -> 0.07 us  [local(): swap_in = lax.ppermute(send, 'gy', across)]
    ppermute x1, starting transfers between devices: 4.23 us -> 4.75 us  [local(): up = lax.ppermute(zc, 'gx', upward)]
  transfers between devices with their start and end apart: 9 -> 8, of which waited for: 5 -> 5; matrix products, arithmetic and copies ran while one was open for 0% -> 0% of each run, Pallas kernels for 25% -> 25%
where the time goes in v5:
time: 48.2 us; the launch traced here: 48 us
  blocking collectives  16.7 us (35%)
  Pallas kernels  15.1 us (31%)
  starting transfers between devices  8.52 us (18%)
  waiting for transfers between devices  7.53 us (16%)
    all_to_all x1, blocking collectives, local(): parts = lax.all_to_all(parts, ('gx', 'gy'), 0, 0, tiled=True)  12.7 us
    pallas_call x3, Pallas kernels, energies(): kernel(name, partial(energy_kernel, low, high, end), outs + (planes(2),)...  6.89 us
    ppermute x1, starting transfers between devices, local(): up = lax.ppermute(zc, 'gx', upward)  4.75 us
    ppermute x1, waiting for transfers between devices, local(): halo = lax.ppermute(halo, 'gx', downward)  4.14 us
    all_to_all x1, blocking collectives, local(): halo = lax.all_to_all(halo, 'gy', 0, 0, tiled=True)  3.99 us
    pallas_call x1, Pallas kernels, local(): kernel('krylov_main', partial(main_kernel, modes, layers, cuts), (planes(...  2.99 us
    pallas_call x1, Pallas kernels, local(): kernel('first_layer', first_kernel, (planes(2 * group + 4, half), jax.Sha...  2.14 us
    ppermute x1, waiting for transfers between devices, local(): up = lax.ppermute(zc, 'gx', upward)  2.13 us
  transfers between devices with their start and end apart: 8, of which 5 were waited for; matrix products, arithmetic and copies ran while one was open for 0% of the time, Pallas kernels for 25%

profile of v5, /device:TPU:0, one launch (start us, length us, event | category | flops | bytes accessed | tf_op | source)
XLA Modules:
  0.0 48.0 jit_solution(15890567706562828915)
XLA Ops:
  0.0 0.5 collective-permute-start
  0.5 0.1 pad_add_fusion.place.refs_0_
  0.5 0.0 copy-start.1
  0.5 0.0 copy-start.3
  0.5 2.1 %first_layer.1 = (f32[22,16,256]{2,1,0:T(8,128)S(1)}, f32[9,8,16,256]{3,2,1,0:T(8,128)S(1)}, f32[8,16,256]{2,1,0:T(8,128)S(1)}, f32[8,16,256]{2,1,0:T(8,128)S(1)}, s32[8,16,256]{2,1,0:T(8,128)S(1)}) custom-call(s32[3]{0:T(128)S(1)} %pad_add_fusion.place.refs_0_, f32[18,8,16,256]{3,2,1,0:T(8,128)} %modes.1, f32[8,16,256]{2,1,0:T(8,128)} %density.1, ...), custom_call_target="tpu_custom_call" | custom-call | flops 1048576 | bytes 1048576 | tf_op jit(solution)/shard_map/first_layer/pallas_call | solution.py:507
  2.7 1.3 %collective-permute-start.4 = (f32[22,16,256]{2,1,0:T(8,128)S(1)}, f32[22,16,256]{2,1,0:T(8,128)S(1)}, u32[]{:S(2)}, u32[]{:S(2)}) collective-permute-start(f32[22,16,256]{2,1,0:T(8,128)S(1)} %get-tuple-element.32), channel_id=1, source_target_pairs={{2,0},{4,2},{6,4},{8,6},{10,8},{12,10},{14,12},{3,1},{5,3},{7,5},{... | collective-permute-start | bytes 1081352 | tf_op jit(solution)/shard_map/ppermute | solution.py:525
  4.0 0.0 copy-done.1
  4.0 0.1 collective-permute-start.1
  4.1 0.0 copy-done.2
  4.1 0.5 collective-permute-start.2
  4.6 0.0 copy-done.3
  4.6 0.1 collective-permute-start.3
  4.7 0.7 %collective-permute-done.1.refs_5_ = f32[8,16,256]{2,1,0:T(8,128)S(1)} collective-permute-done((f32[8,16,256]{2,1,0:T(8,128)S(1)}, f32[8,16,256]{2,1,0:T(8,128)S(1)}, u32[]{:S(2)}, u32[]{:S(2)}) %collective-permute-start.1) | collective-permute-done | bytes 131104 | tf_op jit(solution)/shard_map/ppermute | solution.py:524
  5.4 0.2 collective-permute-done.2.refs_7_
  5.6 0.3 collective-permute-done.3.refs_9_
  5.9 0.0 collective-permute-done.refs_3_
  5.9 0.0 copy-done
  5.9 2.5 %energies_first.1 = (f32[9,32,256]{2,1,0:T(8,128)S(1)}, f32[3,32,256]{2,1,0:T(8,128)S(1)}) custom-call(s32[3]{0:T(128)S(1)} %pad_add_fusion.place.refs_0_, f32[6]{0:T(128)S(1)} %copy-done, f32[9,8,16,256]{3,2,1,0:T(8,128)S(1)} %get-tuple-element.26.refs_2_, f32[18,8,16,256]{3,2,1,0:T(8,128)S(1)} %collective-permute-done.refs_3_, ...), custom_call_target="tpu_custom_call" | custom-call | flops 629145600 | bytes 1048576 | tf_op jit(solution)/shard_map/energies_first/pallas_call | solution.py:533
  8.4 1.3 %collective-permute-start.6 = (f32[9,32,256]{2,1,0:T(8,128)S(1)}, f32[9,32,256]{2,1,0:T(8,128)S(1)}, u32[]{:S(2)}, u32[]{:S(2)}) collective-permute-start(f32[9,32,256]{2,1,0:T(8,128)S(1)} %get-tuple-element.30.za), channel_id=1, source_target_pairs={{2,0},{4,2},{6,4},{8,6},{10,8},{12,10},{14,12},{3,1},{5,3},{7,5},{... | collective-permute-start | bytes 884744 | tf_op jit(solution)/shard_map/ppermute | solution.py:547
  9.7 2.5 %energies_inner.1 = (f32[9,32,256]{2,1,0:T(8,128)S(1)}, f32[3,32,256]{2,1,0:T(8,128)S(1)}) custom-call(s32[3]{0:T(128)S(1)} %pad_add_fusion.place.refs_0_, f32[6]{0:T(128)S(1)} %copy-done, f32[9,8,16,256]{3,2,1,0:T(8,128)S(1)} %get-tuple-element.26.refs_2_, f32[18,8,16,256]{3,2,1,0:T(8,128)S(1)} %collective-permute-done.refs_3_, ...), custom_call_target="tpu_custom_call" | custom-call | flops 629145600 | bytes 1048576 | tf_op jit(solution)/shard_map/energies_inner/pallas_call | solution.py:533
  12.2 4.1 %collective-permute-done.4 = f32[22,16,256]{2,1,0:T(8,128)S(1)} collective-permute-done((f32[22,16,256]{2,1,0:T(8,128)S(1)}, f32[22,16,256]{2,1,0:T(8,128)S(1)}, u32[]{:S(2)}, u32[]{:S(2)}) %collective-permute-start.4) | collective-permute-done | bytes 360480 | tf_op jit(solution)/shard_map/ppermute | solution.py:525
  16.4 4.0 %all_to_all.10.refs_10_ = f32[22,16,256]{2,1,0:T(8,128)S(1)} all-to-all(f32[22,16,256]{2,1,0:T(8,128)S(1)} %collective-permute-done.4), channel_id=1, replica_groups=mesh['grp'=2,'gx'=8,'gy'=2] {'gy'}, dimensions={0} | all-to-all | bytes 720896 | tf_op jit(solution)/shard_map/all_to_all | solution.py:550
  20.4 1.9 %energies_last.1 = (f32[7,32,256]{2,1,0:T(8,128)S(1)}, f32[2,32,256]{2,1,0:T(8,128)S(1)}, f32[2,32,256]{2,1,0:T(8,128)S(1)}) custom-call(s32[3]{0:T(128)S(1)} %pad_add_fusion.place.refs_0_, f32[6]{0:T(128)S(1)} %copy-done, f32[9,8,16,256]{3,2,1,0:T(8,128)S(1)} %get-tuple-element.26.refs_2_, f32[18,8,16,256]{3,2,1,0:T(8,128)S(1)} %collective-permute-done.refs_3_, ...), custom_call_target="tpu_custom_call" | custom-call | flops 419430400 | bytes 1048576 | tf_op jit(solution)/shard_map/energies_last/pallas_call | solution.py:533
  22.3 4.8 %collective-permute-start.5 = (f32[7,32,256]{2,1,0:T(8,128)S(1)}, f32[7,32,256]{2,1,0:T(8,128)S(1)}, u32[]{:S(2)}, u32[]{:S(2)}) collective-permute-start(f32[7,32,256]{2,1,0:T(8,128)S(1)} %get-tuple-element.35.zc), channel_id=1, source_target_pairs={{0,2},{2,4},{4,6},{6,8},{8,10},{10,12},{12,14},{1,3},{3,5},{5,7},{... | collective-permute-start | bytes 688136 | tf_op jit(solution)/shard_map/ppermute | solution.py:552
  27.0 0.0 collective-permute-done.6.down
  27.0 3.0 %krylov_main.1 = (f32[27,32,256]{2,1,0:T(8,128)S(1)}, f32[21,32,256]{2,1,0:T(8,128)S(1)}, f32[18,8,128]{2,1,0:T(8,128)S(1)}, f32[72,16,256]{2,1,0:T(8,128)S(1)}) custom-call(s32[3]{0:T(128)S(1)} %pad_add_fusion.place.refs_0_, f32[9,32,256]{2,1,0:T(8,128)S(1)} %get-tuple-element.30.za, f32[9,32,256]{2,1,0:T(8,128)S(1)} %get-tuple-element.36.zb, ...), custom_call_target="tpu_custom_call" | custom-call | flops 419430400 | bytes 1048576 | tf_op jit(solution)/shard_map/krylov_main/pallas_call | solution.py:556
  30.0 2.1 %collective-permute-done.5.up = f32[7,32,256]{2,1,0:T(8,128)S(1)} collective-permute-done((f32[7,32,256]{2,1,0:T(8,128)S(1)}, f32[7,32,256]{2,1,0:T(8,128)S(1)}, u32[]{:S(2)}, u32[]{:S(2)}) %collective-permute-start.5) | collective-permute-done | bytes 229408 | tf_op jit(solution)/shard_map/ppermute | solution.py:552
  32.2 1.4 %krylov_left.1 = (f32[6,32,256]{2,1,0:T(8,128)S(1)}, f32[6,32,256]{2,1,0:T(8,128)S(1)}, f32[72,16,256]{2,1,0:T(8,128)S(1)}, f32[16,8,128]{2,1,0:T(8,128)S(1)}) custom-call(s32[3]{0:T(128)S(1)} %pad_add_fusion.place.refs_0_, f32[9,32,256]{2,1,0:T(8,128)S(1)} %get-tuple-element.30.za, ...), custom_call_target="tpu_custom_call", output_to_operand_aliasing={{2}: (7, {})} | custom-call | flops 209715200 | bytes 1048576 | tf_op jit(solution)/shard_map/krylov_left/pallas_call | solution.py:565
  33.6 0.1 collective-permute-start.7
  33.7 12.7 %all_to_all.11.parts = f32[16,8,128]{2,1,0:T(8,128)S(1)} all-to-all(f32[16,8,128]{2,1,0:T(8,128)S(1)} %get-tuple-element.43), channel_id=1, replica_groups=mesh['grp'=2,'gx'=8,'gy'=2] {'gx','gy'}, dimensions={0} | all-to-all | bytes 131072 | tf_op jit(solution)/shard_map/all_to_all | solution.py:581
  46.4 0.0 collective-permute-done.7.swap
  46.4 1.6 %combine.1 = f32[6,8,16,256]{3,2,1,0:T(8,128)} custom-call(s32[3]{0:T(128)S(1)} %pad_add_fusion.place.refs_0_, f32[16,8,128]{2,1,0:T(8,128)S(1)} %all_to_all.11.parts, f32[9,32,256]{2,1,0:T(8,128)S(1)} %get-tuple-element.30.za, f32[9,32,256]{2,1,0:T(8,128)S(1)} %get-tuple-element.36.zb, f32[7,32,256]{2,1,0:T(8,128)S(1)} %get-tuple-element.35.zc, ...), custom_call_target="tpu_custom_call" | custom-call | flops 104857600 | bytes 1048576 | tf_op jit(solution)/shard_map/combine/pallas_call | solution.py:583
  (2 shorter events, 0.0 us)
Async XLA Ops:
  0.0 5.9 %collective-permute-start = (f32[18,8,16,256]{3,2,1,0:T(8,128)}, f32[18,8,16,256]{3,2,1,0:T(8,128)S(1)}, u32[]{:S(2)}, u32[]{:S(2)}) collective-permute-start(f32[18,8,16,256]{3,2,1,0:T(8,128)} %modes.1), channel_id=1, source_target_pairs={{0,1},{1,0},{2,3},{3,2},{4,5},{5,4},{6,7},{7,6},{8,9},{9,8},{10,11... | collective-permute-start | bytes 7077896 | tf_op jit(solution)/shard_map/ppermute | solution.py:524
  0.5 3.5 %copy-start.1 = (f32[8,16,256]{2,1,0:T(8,128)S(1)}, f32[8,16,256]{2,1,0:T(8,128)}, u32[]{:S(2)}) copy-start(f32[8,16,256]{2,1,0:T(8,128)} %density.1) | copy-start | bytes 393220
  0.5 3.6 %copy-start.2 = (f32[8,16,256]{2,1,0:T(8,128)S(1)}, f32[8,16,256]{2,1,0:T(8,128)}, u32[]{:S(2)}) copy-start(f32[8,16,256]{2,1,0:T(8,128)} %mass.1) | copy-start | bytes 393220
  0.5 4.0 %copy-start.3 = (s32[8,16,256]{2,1,0:T(8,128)S(1)}, s32[8,16,256]{2,1,0:T(8,128)}, u32[]{:S(2)}) copy-start(s32[8,16,256]{2,1,0:T(8,128)} %passive.1) | copy-start | bytes 393220
  0.5 5.4 %copy-start = (f32[6]{0:T(128)S(1)}, f32[6]{0:T(128)}, u32[]{:S(2)}) copy-start(f32[6]{0:T(128)} %refs_1_.5) | copy-start | bytes 76
  2.7 13.7 %collective-permute-start.4 = (f32[22,16,256]{2,1,0:T(8,128)S(1)}, f32[22,16,256]{2,1,0:T(8,128)S(1)}, u32[]{:S(2)}, u32[]{:S(2)}) collective-permute-start(f32[22,16,256]{2,1,0:T(8,128)S(1)} %get-tuple-element.32), channel_id=1, source_target_pairs={{2,0},{4,2},{6,4},{8,6},{10,8},{12,10},{14,12},{3,1},{5,3},{7,5},{... | collective-permute-start | bytes 1081352 | tf_op jit(solution)/shard_map/ppermute | solution.py:525
  4.0 1.4 %collective-permute-start.1 = (f32[8,16,256]{2,1,0:T(8,128)S(1)}, f32[8,16,256]{2,1,0:T(8,128)S(1)}, u32[]{:S(2)}, u32[]{:S(2)}) collective-permute-start(f32[8,16,256]{2,1,0:T(8,128)S(1)} %copy-done.1), channel_id=1, source_target_pairs={{0,1},{1,0},{2,3},{3,2},{4,5},{5,4},{6,7},{7,6},{8,9},{9,8},{10,11... | collective-permute-start | bytes 393224 | tf_op jit(solution)/shard_map/ppermute | solution.py:524
  4.1 1.5 %collective-permute-start.2 = (f32[8,16,256]{2,1,0:T(8,128)S(1)}, f32[8,16,256]{2,1,0:T(8,128)S(1)}, u32[]{:S(2)}, u32[]{:S(2)}) collective-permute-start(f32[8,16,256]{2,1,0:T(8,128)S(1)} %copy-done.2), channel_id=1, source_target_pairs={{0,1},{1,0},{2,3},{3,2},{4,5},{5,4},{6,7},{7,6},{8,9},{9,8},{10,11... | collective-permute-start | bytes 393224 | tf_op jit(solution)/shard_map/ppermute | solution.py:524
  4.6 1.3 %collective-permute-start.3 = (s32[8,16,256]{2,1,0:T(8,128)S(1)}, s32[8,16,256]{2,1,0:T(8,128)S(1)}, u32[]{:S(2)}, u32[]{:S(2)}) collective-permute-start(s32[8,16,256]{2,1,0:T(8,128)S(1)} %copy-done.3), channel_id=1, source_target_pairs={{0,1},{1,0},{2,3},{3,2},{4,5},{5,4},{6,7},{7,6},{8,9},{9,8},{10,11... | collective-permute-start | bytes 393224 | tf_op jit(solution)/shard_map/ppermute | solution.py:524
  8.4 18.6 %collective-permute-start.6 = (f32[9,32,256]{2,1,0:T(8,128)S(1)}, f32[9,32,256]{2,1,0:T(8,128)S(1)}, u32[]{:S(2)}, u32[]{:S(2)}) collective-permute-start(f32[9,32,256]{2,1,0:T(8,128)S(1)} %get-tuple-element.30.za), channel_id=1, source_target_pairs={{2,0},{4,2},{6,4},{8,6},{10,8},{12,10},{14,12},{3,1},{5,3},{7,5},{... | collective-permute-start | bytes 884744 | tf_op jit(solution)/shard_map/ppermute | solution.py:547
  22.3 9.9 %collective-permute-start.5 = (f32[7,32,256]{2,1,0:T(8,128)S(1)}, f32[7,32,256]{2,1,0:T(8,128)S(1)}, u32[]{:S(2)}, u32[]{:S(2)}) collective-permute-start(f32[7,32,256]{2,1,0:T(8,128)S(1)} %get-tuple-element.35.zc), channel_id=1, source_target_pairs={{0,2},{2,4},{4,6},{6,8},{8,10},{10,12},{12,14},{1,3},{3,5},{5,7},{... | collective-permute-start | bytes 688136 | tf_op jit(solution)/shard_map/ppermute | solution.py:552
  33.6 12.8 %collective-permute-start.7 = (f32[72,16,256]{2,1,0:T(8,128)S(1)}, f32[72,16,256]{2,1,0:T(8,128)S(1)}, u32[]{:S(2)}, u32[]{:S(2)}) collective-permute-start(f32[72,16,256]{2,1,0:T(8,128)S(1)} %get-tuple-element.46), channel_id=1, source_target_pairs={{0,1},{1,0},{2,3},{3,2},{4,5},{5,4},{6,7},{7,6},{8,9},{9,8},{10,11... | collective-permute-start | bytes 3538952 | tf_op jit(solution)/shard_map/ppermute | solution.py:580

commit v6 on v5

--- a/solution.py
+++ b/solution.py
@@ -140,34 +140,33 @@
     return pl.multiple_of(core * half, half), pl.multiple_of((1 - core) * half, half)
 
 
-def first_kernel(place, modes, density, mass, passive, halo, own, own_density, own_mass, own_passive, sems):
+def first_kernel(place, modes, density, mass, passive, straight, crossed, fields, signed, flags, sems):
     group = modes.shape[0] // 2
-    moves = []
-    for core in (0, 1):
-        at = core * (group + 2)
-        moves.append((modes.at[pl.ds(core * group, group), 0], halo.at[pl.ds(at, group)]))
-        moves.append((mass.at[pl.ds(0, 2)], halo.at[pl.ds(at + group, 2)]))
-    moves += [
-        (modes.at[pl.ds(place[0] * group, group)], own),
-        (density, own_density),
-        (mass, own_mass),
-        (passive, own_passive),
-    ]
+    layers = density.shape[0]
+    moves = [(density, signed), (passive, flags), (mass, fields.at[pl.ds(layers, layers)])]
+    for target, core in ((straight, place[0]), (crossed, 1 - place[0])):
+        moves.append((modes.at[pl.ds(core * group, group), 0], target.at[pl.ds(0, group)]))
+        moves.append((mass.at[pl.ds(0, 2)], target.at[pl.ds(group, 2)]))
     copies = [pltpu.make_async_copy(*move, sems.at[i]) for i, move in enumerate(moves)]
     for copy in copies:
         copy.start()
-    for copy in copies:
+    for copy in copies[:2]:
         copy.wait()
+    for x in range(layers):
+        fields[x] = jnp.where(flags[x] == 0, signed[x], -signed[x])
+    for copy in copies[2:]:
+        copy.wait()
 
 
 def energy_kernel(low, high, end, *refs):
-    place, eig, modes, modes_swap, density, density_swap, mass, mass_swap, passive, passive_swap = refs[:10]
+    place, eig, modes, modes_swap, fields, fields_swap = refs[:6]
     if end:
-        halo = refs[10]
+        halo, halo_swap = refs[6:8]
         z_out, mass_out, ghost_mass, floats, sums = refs[-5:]
     else:
         z_out, mass_out, floats, sums = refs[-4:]
-    group, layers, half, depth = modes.shape
+    layers, half, depth = modes.shape[1:]
+    group = modes.shape[0] // 2
     width, count = 2 * half, high - low
     core, first, last = place[0], place[1], place[2]
     start = core * group
@@ -180,22 +179,22 @@
     missing = missing_plane((width, depth))
     for i in range(count):
         x = low + i
-        weight = whole(mass[x], mass_swap[x])
+        weight = whole(fields[layers + x], fields_swap[layers + x])
         mass_out[i] = weight
         inverse = 1.0 / (weight + RADIUS_SQ * neighbour_count(missing, x, layers, first, last))
-        design = (1 - whole(passive[x], passive_swap[x])).astype(jnp.float32) * inverse
-        rho = whole(density[x], density_swap[x])
+        rho = whole(fields[x], fields_swap[x])
+        design = jnp.where(rho > 0.0, inverse, 0.0)
         floats[0, i] = 3.0 * (1.0 - void_floor) * rho * rho * design
         floats[1, i] = design
     if end:
         z_out[z_out.shape[0] - 1] = mass_out[count - 1]
         for i in (0, 1):
-            ghost_mass[i] = jnp.concatenate([halo[group + i], halo[2 * group + 2 + i]], axis=0)
+            ghost_mass[i] = whole(halo[group + i], halo_swap[group + i])
 
     def node(row, x):
         if x == layers:
-            return jnp.concatenate([halo[row], halo[group + 2 + row]], axis=0)
-        return whole(modes[row, x], modes_swap[start + row, x])
+            return whole(halo[row], halo_swap[row])
+        return whole(modes[start + row, x], modes_swap[start + row, x])
 
     ring = sums.shape[0]
 
@@ -504,25 +503,25 @@
         )
 
     stored = [pltpu.with_memory_space_constraint(x, pltpu.HBM) for x in (mode_shapes, density, filter_mass, passive)]
-    halo, *own = kernel(
+    node, node_crossed, fields = kernel(
         "first_layer",
         first_kernel,
-        (
-            planes(2 * group + 4, half),
-            jax.ShapeDtypeStruct((group, layers, half, depth), f32),
-            planes(layers, half),
-            planes(layers, half),
-            jax.ShapeDtypeStruct(passive.shape, passive.dtype),
-        ),
+        (planes(group + 2, half), planes(group + 2, half), planes(2 * layers, half)),
         [smem] + [anywhere] * 4,
-        [pltpu.SemaphoreType.DMA((8,))],
+        [
+            pltpu.VMEM((layers, half, depth), f32),
+            pltpu.VMEM((layers, half, depth), jnp.int32),
+            pltpu.SemaphoreType.DMA((7,)),
+        ],
         4,
         1,
     )(place, *stored)
-    operands = []
-    for mine, x in zip(own, (mode_shapes, density, filter_mass, passive)):
-        operands += [mine, lax.ppermute(x, "gy", across)]
-    halo = lax.ppermute(halo, "gx", downward)
+    source, _ = lax.optimization_barrier((mode_shapes, node))
+    operands = [source, lax.ppermute(source, "gy", across), fields, lax.ppermute(fields, "gy", across)]
+    straight = [(2 * i + c, 2 * i - 2 + c) for i in range(1, count) for c in (0, 1)]
+    crossed = [(2 * i + c, 2 * i - 1 - c) for i in range(1, count) for c in (0, 1)]
+    halo = lax.ppermute(node, ("gx", "gy"), straight)
+    halo_swap = lax.ppermute(node_crossed, ("gx", "gy"), crossed)
 
     cuts = (DOWN, layers - UP)
 
@@ -534,7 +533,7 @@
             name,
             partial(energy_kernel, low, high, end),
             outs + (planes(2),) if end else outs,
-            [smem, smem] + [vmem] * (8 + end) + [anywhere] * (len(extra) - end),
+            [smem, smem] + [vmem] * (4 + 2 * end) + [anywhere] * (len(extra) - 2 * end),
             [
                 pltpu.VMEM((2, n, width, depth), f32),
                 pltpu.VMEM((4, 12, width, depth), f32),
@@ -546,9 +545,7 @@
     za, ma = energies("energies_first", 0, cuts[0])
     down = lax.ppermute(za, "gx", downward)
     zb, mb = energies("energies_inner", cuts[0], cuts[1], ma)
-    halo, _ = lax.optimization_barrier((halo, mb))
-    halo = lax.all_to_all(halo, "gy", 0, 0, tiled=True)
-    zc, mc, ghost_mass = energies("energies_last", cuts[1], layers, halo, mb)
+    zc, mc, ghost_mass = energies("energies_last", cuts[1], layers, halo, halo_swap, mb)
     up = lax.ppermute(zc, "gx", upward)
 
     tables = [pltpu.VMEM((layers + 2, width, depth), f32)] * 2

time: 48.2 us -> 45.1 us (0.936)
  blocking collectives: 16.7 us -> 13.9 us
  waiting for transfers between devices: 7.53 us -> 6.87 us
  starting transfers between devices: 8.52 us -> 9.1 us
    all_to_all x1 -> x0, blocking collectives: 3.99 us -> none  [local(): halo = lax.all_to_all(halo, 'gy', 0, 0, tiled=True)]
    all_to_all x1, blocking collectives: 12.7 us -> 13.9 us  [local(): parts = lax.all_to_all(parts, ('gx', 'gy'), 0, 0, tiled=True)]
    ppermute x5 -> x4, starting transfers between devices: 2.41 us -> 3.17 us  [the longest x1 1.29 us: local(): halo = lax.ppermute(node, ('gx', 'gy'), straight)]
    ppermute x5 -> x4, waiting for transfers between devices: 5.4 us -> 5.19 us  [the longest x1 3.31 us: local(): halo = lax.ppermute(node, ('gx', 'gy'), straight)]
  transfers between devices with their start and end apart: 8 -> 7, of which waited for: 5 -> 3; matrix products, arithmetic and copies ran while one was open for 0% -> 0% of each run, Pallas kernels for 25% -> 22%
where the time goes in v6:
time: 45.1 us; the launch traced here: 44.8 us
  Pallas kernels  14.8 us (33%)
  blocking collectives  13.9 us (31%)
  starting transfers between devices  9.1 us (20%)
  waiting for transfers between devices  6.87 us (15%)
    all_to_all x1, blocking collectives, local(): parts = lax.all_to_all(parts, ('gx', 'gy'), 0, 0, tiled=True)  13.9 us
    pallas_call x3, Pallas kernels, energies(): kernel(name, partial(energy_kernel, low, high, end), outs + (planes(2),)...  6.85 us
    ppermute x1, starting transfers between devices, local(): up = lax.ppermute(zc, 'gx', upward)  4.57 us
    ppermute x1, waiting for transfers between devices, local(): halo = lax.ppermute(node, ('gx', 'gy'), straight)  3.31 us
    pallas_call x1, Pallas kernels, local(): kernel('krylov_main', partial(main_kernel, modes, layers, cuts), (planes(...  2.97 us
    pallas_call x1, Pallas kernels, local(): kernel('first_layer', first_kernel, (planes(group + 2, half), planes(grou...  1.97 us
    ppermute x1, waiting for transfers between devices, local(): lax.ppermute(fields, 'gy', across)  1.87 us
    ppermute x1, waiting for transfers between devices, local(): up = lax.ppermute(zc, 'gx', upward)  1.67 us
  transfers between devices with their start and end apart: 7, of which 3 were waited for; matrix products, arithmetic and copies ran while one was open for 0% of the time, Pallas kernels for 22%

profile of v6, /device:TPU:0, one launch (start us, length us, event | category | flops | bytes accessed | tf_op | source)
XLA Modules:
  0.0 44.8 jit_solution(172936171597736855)
XLA Ops:
  0.0 0.1 pad_add_fusion.place.refs_0_
  0.1 0.0 copy-start
  0.1 0.0 copy-start.1
  0.1 2.0 %first_layer.1 = (f32[11,16,256]{2,1,0:T(8,128)S(1)}, f32[11,16,256]{2,1,0:T(8,128)S(1)}, f32[16,16,256]{2,1,0:T(8,128)S(1)}) custom-call(s32[3]{0:T(128)S(1)} %pad_add_fusion.place.refs_0_, f32[18,8,16,256]{3,2,1,0:T(8,128)} %refs_2_.2, f32[8,16,256]{2,1,0:T(8,128)} %density.1, f32[8,16,256]{2,1,0:T(8,128)} %mass.1, s32[8,16,256]{2,1,0:T(8,128)} %passive.1), custom_call_target="tpu_custom_call" | custom-call | flops 1048576 | bytes 1048576 | tf_op jit(solution)/shard_map/first_layer/pallas_call | solution.py:506
  2.1 0.0 copy-done
  2.1 0.5 %collective-permute-start = (f32[18,8,16,256]{3,2,1,0:T(8,128)S(1)}, f32[18,8,16,256]{3,2,1,0:T(8,128)S(1)}, u32[]{:S(2)}, u32[]{:S(2)}) collective-permute-start(f32[18,8,16,256]{3,2,1,0:T(8,128)S(1)} %copy-done), channel_id=1, source_target_pairs={{0,1},{1,0},{2,3},{3,2},{4,5},{5,4},{6,7},{7,6},{8,9},{9,8},{10,11... | collective-permute-start | bytes 7077896 | tf_op jit(solution)/shard_map/ppermute | solution.py:520
  2.6 0.1 collective-permute-start.1
  2.7 1.3 %collective-permute-start.3 = (f32[11,16,256]{2,1,0:T(8,128)S(1)}, f32[11,16,256]{2,1,0:T(8,128)S(1)}, u32[]{:S(2)}, u32[]{:S(2)}) collective-permute-start(f32[11,16,256]{2,1,0:T(8,128)S(1)} %get-tuple-element.29), channel_id=1, source_target_pairs={{2,1},{3,0},{4,3},{5,2},{6,5},{7,4},{8,7},{9,6},{10,9},{11,8},{12,... | collective-permute-start | bytes 540680 | tf_op jit(solution)/shard_map/ppermute | solution.py:524
  4.0 1.3 %collective-permute-start.2 = (f32[11,16,256]{2,1,0:T(8,128)S(1)}, f32[11,16,256]{2,1,0:T(8,128)S(1)}, u32[]{:S(2)}, u32[]{:S(2)}) collective-permute-start(f32[11,16,256]{2,1,0:T(8,128)S(1)} %get-tuple-element.24), channel_id=1, source_target_pairs={{2,0},{3,1},{4,2},{5,3},{6,4},{7,5},{8,6},{9,7},{10,8},{11,9},{12,... | collective-permute-start | bytes 540680 | tf_op jit(solution)/shard_map/ppermute | solution.py:523
  5.3 1.9 %collective-permute-done.1.refs_5_ = f32[16,16,256]{2,1,0:T(8,128)S(1)} collective-permute-done((f32[16,16,256]{2,1,0:T(8,128)S(1)}, f32[16,16,256]{2,1,0:T(8,128)S(1)}, u32[]{:S(2)}, u32[]{:S(2)}) %collective-permute-start.1) | collective-permute-done | bytes 262176 | tf_op jit(solution)/shard_map/ppermute | solution.py:520
  7.1 0.0 collective-permute-done.refs_3_
  7.1 0.0 copy-done.1
  7.1 2.5 %energies_first.1 = (f32[9,32,256]{2,1,0:T(8,128)S(1)}, f32[3,32,256]{2,1,0:T(8,128)S(1)}) custom-call(s32[3]{0:T(128)S(1)} %pad_add_fusion.place.refs_0_, f32[6]{0:T(128)S(1)} %copy-done.1, f32[18,8,16,256]{3,2,1,0:T(8,128)S(1)} %copy-done, f32[18,8,16,256]{3,2,1,0:T(8,128)S(1)} %collective-permute-done.refs_3_, ...), custom_call_target="tpu_custom_call" | custom-call | flops 629145600 | bytes 1048576 | tf_op jit(solution)/shard_map/energies_first/pallas_call | solution.py:532
  9.6 1.3 %collective-permute-start.5 = (f32[9,32,256]{2,1,0:T(8,128)S(1)}, f32[9,32,256]{2,1,0:T(8,128)S(1)}, u32[]{:S(2)}, u32[]{:S(2)}) collective-permute-start(f32[9,32,256]{2,1,0:T(8,128)S(1)} %get-tuple-element.27.za), channel_id=1, source_target_pairs={{2,0},{4,2},{6,4},{8,6},{10,8},{12,10},{14,12},{3,1},{5,3},{7,5},{... | collective-permute-start | bytes 884744 | tf_op jit(solution)/shard_map/ppermute | solution.py:546
  10.9 2.5 %energies_inner.1 = (f32[9,32,256]{2,1,0:T(8,128)S(1)}, f32[3,32,256]{2,1,0:T(8,128)S(1)}) custom-call(s32[3]{0:T(128)S(1)} %pad_add_fusion.place.refs_0_, f32[6]{0:T(128)S(1)} %copy-done.1, f32[18,8,16,256]{3,2,1,0:T(8,128)S(1)} %copy-done, f32[18,8,16,256]{3,2,1,0:T(8,128)S(1)} %collective-permute-done.refs_3_, ...), custom_call_target="tpu_custom_call" | custom-call | flops 629145600 | bytes 1048576 | tf_op jit(solution)/shard_map/energies_inner/pallas_call | solution.py:532
  13.4 0.0 collective-permute-done.3.refs_7_
  13.4 3.3 %collective-permute-done.2.refs_6_ = f32[11,16,256]{2,1,0:T(8,128)S(1)} collective-permute-done((f32[11,16,256]{2,1,0:T(8,128)S(1)}, f32[11,16,256]{2,1,0:T(8,128)S(1)}, u32[]{:S(2)}, u32[]{:S(2)}) %collective-permute-start.2) | collective-permute-done | bytes 180256 | tf_op jit(solution)/shard_map/ppermute | solution.py:523
  16.7 1.9 %energies_last.1 = (f32[7,32,256]{2,1,0:T(8,128)S(1)}, f32[2,32,256]{2,1,0:T(8,128)S(1)}, f32[2,32,256]{2,1,0:T(8,128)S(1)}) custom-call(s32[3]{0:T(128)S(1)} %pad_add_fusion.place.refs_0_, f32[6]{0:T(128)S(1)} %copy-done.1, f32[18,8,16,256]{3,2,1,0:T(8,128)S(1)} %copy-done, f32[18,8,16,256]{3,2,1,0:T(8,128)S(1)} %collective-permute-done.refs_3_, ...), custom_call_target="tpu_custom_call" | custom-call | flops 419430400 | bytes 1048576 | tf_op jit(solution)/shard_map/energies_last/pallas_call | solution.py:532
  18.6 4.6 %collective-permute-start.4 = (f32[7,32,256]{2,1,0:T(8,128)S(1)}, f32[7,32,256]{2,1,0:T(8,128)S(1)}, u32[]{:S(2)}, u32[]{:S(2)}) collective-permute-start(f32[7,32,256]{2,1,0:T(8,128)S(1)} %get-tuple-element.31.zc), channel_id=1, source_target_pairs={{0,2},{2,4},{4,6},{6,8},{8,10},{10,12},{12,14},{1,3},{3,5},{5,7},{... | collective-permute-start | bytes 688136 | tf_op jit(solution)/shard_map/ppermute | solution.py:549
  23.2 0.0 collective-permute-done.5.down
  23.2 3.0 %krylov_main.1 = (f32[27,32,256]{2,1,0:T(8,128)S(1)}, f32[21,32,256]{2,1,0:T(8,128)S(1)}, f32[18,8,128]{2,1,0:T(8,128)S(1)}, f32[72,16,256]{2,1,0:T(8,128)S(1)}) custom-call(s32[3]{0:T(128)S(1)} %pad_add_fusion.place.refs_0_, f32[9,32,256]{2,1,0:T(8,128)S(1)} %get-tuple-element.27.za, f32[9,32,256]{2,1,0:T(8,128)S(1)} %get-tuple-element.32.zb, ...), custom_call_target="tpu_custom_call" | custom-call | flops 419430400 | bytes 1048576 | tf_op jit(solution)/shard_map/krylov_main/pallas_call | solution.py:553
  26.2 1.7 %collective-permute-done.4.up = f32[7,32,256]{2,1,0:T(8,128)S(1)} collective-permute-done((f32[7,32,256]{2,1,0:T(8,128)S(1)}, f32[7,32,256]{2,1,0:T(8,128)S(1)}, u32[]{:S(2)}, u32[]{:S(2)}) %collective-permute-start.4) | collective-permute-done | bytes 229408 | tf_op jit(solution)/shard_map/ppermute | solution.py:549
  27.9 1.4 %krylov_left.1 = (f32[6,32,256]{2,1,0:T(8,128)S(1)}, f32[6,32,256]{2,1,0:T(8,128)S(1)}, f32[72,16,256]{2,1,0:T(8,128)S(1)}, f32[16,8,128]{2,1,0:T(8,128)S(1)}) custom-call(s32[3]{0:T(128)S(1)} %pad_add_fusion.place.refs_0_, f32[9,32,256]{2,1,0:T(8,128)S(1)} %get-tuple-element.27.za, ...), custom_call_target="tpu_custom_call", output_to_operand_aliasing={{2}: (7, {})} | custom-call | flops 209715200 | bytes 1048576 | tf_op jit(solution)/shard_map/krylov_left/pallas_call | solution.py:562
  29.3 0.1 collective-permute-start.6
  29.4 13.9 %all_to_all.5.parts = f32[16,8,128]{2,1,0:T(8,128)S(1)} all-to-all(f32[16,8,128]{2,1,0:T(8,128)S(1)} %get-tuple-element.39), channel_id=1, replica_groups=mesh['grp'=2,'gx'=8,'gy'=2] {'gx','gy'}, dimensions={0} | all-to-all | bytes 131072 | tf_op jit(solution)/shard_map/all_to_all | solution.py:578
  43.2 0.0 collective-permute-done.6.swap
  43.2 1.6 %combine.1 = f32[6,8,16,256]{3,2,1,0:T(8,128)} custom-call(s32[3]{0:T(128)S(1)} %pad_add_fusion.place.refs_0_, f32[16,8,128]{2,1,0:T(8,128)S(1)} %all_to_all.5.parts, f32[9,32,256]{2,1,0:T(8,128)S(1)} %get-tuple-element.27.za, f32[9,32,256]{2,1,0:T(8,128)S(1)} %get-tuple-element.32.zb, f32[7,32,256]{2,1,0:T(8,128)S(1)} %get-tuple-element.31.zc, ...), custom_call_target="tpu_custom_call" | custom-call | flops 104857600 | bytes 1048576 | tf_op jit(solution)/shard_map/combine/pallas_call | solution.py:580
Async XLA Ops:
  0.1 2.0 %copy-start = (f32[18,8,16,256]{3,2,1,0:T(8,128)S(1)}, f32[18,8,16,256]{3,2,1,0:T(8,128)}, u32[]{:S(2)}) copy-start(f32[18,8,16,256]{3,2,1,0:T(8,128)} %refs_2_.2) | copy-start | bytes 7077892
  0.1 7.1 %copy-start.1 = (f32[6]{0:T(128)S(1)}, f32[6]{0:T(128)}, u32[]{:S(2)}) copy-start(f32[6]{0:T(128)} %refs_1_.5) | copy-start | bytes 76
  2.1 5.1 %collective-permute-start = (f32[18,8,16,256]{3,2,1,0:T(8,128)S(1)}, f32[18,8,16,256]{3,2,1,0:T(8,128)S(1)}, u32[]{:S(2)}, u32[]{:S(2)}) collective-permute-start(f32[18,8,16,256]{3,2,1,0:T(8,128)S(1)} %copy-done), channel_id=1, source_target_pairs={{0,1},{1,0},{2,3},{3,2},{4,5},{5,4},{6,7},{7,6},{8,9},{9,8},{10,11... | collective-permute-start | bytes 7077896 | tf_op jit(solution)/shard_map/ppermute | solution.py:520
  2.6 4.5 %collective-permute-start.1 = (f32[16,16,256]{2,1,0:T(8,128)S(1)}, f32[16,16,256]{2,1,0:T(8,128)S(1)}, u32[]{:S(2)}, u32[]{:S(2)}) collective-permute-start(f32[16,16,256]{2,1,0:T(8,128)S(1)} %get-tuple-element.26.refs_4_), channel_id=1, source_target_pairs={{0,1},{1,0},{2,3},{3,2},{4,5},{5,4},{6,7},{7,6},{8,9},{9,8},{10,11... | collective-permute-start | bytes 786440 | tf_op jit(solution)/shard_map/ppermute | solution.py:520
  2.7 10.7 %collective-permute-start.3 = (f32[11,16,256]{2,1,0:T(8,128)S(1)}, f32[11,16,256]{2,1,0:T(8,128)S(1)}, u32[]{:S(2)}, u32[]{:S(2)}) collective-permute-start(f32[11,16,256]{2,1,0:T(8,128)S(1)} %get-tuple-element.29), channel_id=1, source_target_pairs={{2,1},{3,0},{4,3},{5,2},{6,5},{7,4},{8,7},{9,6},{10,9},{11,8},{12,... | collective-permute-start | bytes 540680 | tf_op jit(solution)/shard_map/ppermute | solution.py:524
  4.0 12.8 %collective-permute-start.2 = (f32[11,16,256]{2,1,0:T(8,128)S(1)}, f32[11,16,256]{2,1,0:T(8,128)S(1)}, u32[]{:S(2)}, u32[]{:S(2)}) collective-permute-start(f32[11,16,256]{2,1,0:T(8,128)S(1)} %get-tuple-element.24), channel_id=1, source_target_pairs={{2,0},{3,1},{4,2},{5,3},{6,4},{7,5},{8,6},{9,7},{10,8},{11,9},{12,... | collective-permute-start | bytes 540680 | tf_op jit(solution)/shard_map/ppermute | solution.py:523
  9.6 13.6 %collective-permute-start.5 = (f32[9,32,256]{2,1,0:T(8,128)S(1)}, f32[9,32,256]{2,1,0:T(8,128)S(1)}, u32[]{:S(2)}, u32[]{:S(2)}) collective-permute-start(f32[9,32,256]{2,1,0:T(8,128)S(1)} %get-tuple-element.27.za), channel_id=1, source_target_pairs={{2,0},{4,2},{6,4},{8,6},{10,8},{12,10},{14,12},{3,1},{5,3},{7,5},{... | collective-permute-start | bytes 884744 | tf_op jit(solution)/shard_map/ppermute | solution.py:546
  18.6 9.2 %collective-permute-start.4 = (f32[7,32,256]{2,1,0:T(8,128)S(1)}, f32[7,32,256]{2,1,0:T(8,128)S(1)}, u32[]{:S(2)}, u32[]{:S(2)}) collective-permute-start(f32[7,32,256]{2,1,0:T(8,128)S(1)} %get-tuple-element.31.zc), channel_id=1, source_target_pairs={{0,2},{2,4},{4,6},{6,8},{8,10},{10,12},{12,14},{1,3},{3,5},{5,7},{... | collective-permute-start | bytes 688136 | tf_op jit(solution)/shard_map/ppermute | solution.py:549
  29.3 13.9 %collective-permute-start.6 = (f32[72,16,256]{2,1,0:T(8,128)S(1)}, f32[72,16,256]{2,1,0:T(8,128)S(1)}, u32[]{:S(2)}, u32[]{:S(2)}) collective-permute-start(f32[72,16,256]{2,1,0:T(8,128)S(1)} %get-tuple-element.42), channel_id=1, source_target_pairs={{0,1},{1,0},{2,3},{3,2},{4,5},{5,4},{6,7},{7,6},{8,9},{9,8},{10,11... | collective-permute-start | bytes 3538952 | tf_op jit(solution)/shard_map/ppermute | solution.py:577

commit v7 on v6

--- a/solution.py
+++ b/solution.py
@@ -14,6 +14,7 @@
 RADIUS_SQ = RMIN * RMIN / 12.0
 DOWN = 3
 UP = 2
+ROUNDING = 2.0**-24
 
 
 void_floor = 0.001
@@ -101,18 +102,31 @@
             stiff = total * weight if stiff is None else stiff + total * weight
         inert[mass] = inert[mass] + total if mass in inert else total
     for weight, members in products:
-        total = entries[members[0][0]] * entries[members[0][1]]
-        for i, j in members[1:]:
-            total = total + entries[i] * entries[j]
+        a, b = members[0]
+        rest = [m for m in members[1:] if a in m]
+        if len(members) == 3 and rest:
+            (last,) = [m for m in members[1:] if a not in m]
+            other = rest[0][0] if rest[0][1] == a else rest[0][1]
+            total = entries[a] * (entries[b] + entries[other]) + entries[last[0]] * entries[last[1]]
+        else:
+            total = entries[a] * entries[b]
+            for i, j in members[1:]:
+                total = total + entries[i] * entries[j]
         stiff = stiff + weight * total
     return stiff, sum(total * mass for mass, total in inert.items())
 
 
 def shifted(value, step, dim):
-    size = value.shape[dim]
-    index = lax.broadcasted_iota(jnp.int32, value.shape, dim)
-    edge = size - 1 if step > 0 else 0
-    return jnp.where(index == edge, 0.0, pltpu.roll(value, (-step) % size, dim))
+    tile, axis = (8, 0) if dim == 0 else (128, 1)
+    count = value.shape[dim] // tile
+    parts = [lax.slice_in_dim(value, i * tile, (i + 1) * tile, axis=axis) for i in range(count)]
+    rolled = [pltpu.roll(part, (-step) % tile, axis) for part in parts]
+    edge = lax.broadcasted_iota(jnp.int32, parts[0].shape, axis) == (tile - 1 if step > 0 else 0)
+    result = []
+    for i, part in enumerate(rolled):
+        beyond = rolled[i + step] if 0 <= i + step < count else 0.0
+        result.append(jnp.where(edge, beyond, part))
+    return jnp.concatenate(result, axis=axis)
 
 
 def missing_plane(shape):
@@ -146,7 +160,7 @@
     moves = [(density, signed), (passive, flags), (mass, fields.at[pl.ds(layers, layers)])]
     for target, core in ((straight, place[0]), (crossed, 1 - place[0])):
         moves.append((modes.at[pl.ds(core * group, group), 0], target.at[pl.ds(0, group)]))
-        moves.append((mass.at[pl.ds(0, 2)], target.at[pl.ds(group, 2)]))
+    moves.append((mass.at[pl.ds(0, 2)], straight.at[pl.ds(group, 2)]))
     copies = [pltpu.make_async_copy(*move, sems.at[i]) for i, move in enumerate(moves)]
     for copy in copies:
         copy.start()
@@ -189,7 +203,7 @@
     if end:
         z_out[z_out.shape[0] - 1] = mass_out[count - 1]
         for i in (0, 1):
-            ghost_mass[i] = whole(halo[group + i], halo_swap[group + i])
+            ghost_mass[i] = halo[group + i]
 
     def node(row, x):
         if x == layers:
@@ -248,7 +262,7 @@
         return ref[mode * stride + offset]
 
 
-def krylov_step(place, layers, modes, mass, zeroth, first_in, second_in, first_out, second_out, plan, moments, scratch):
+def krylov_step(place, layers, modes, mass, zeroth, first_in, second_in, first_out, second_out, plan, moments, scratch, unroll=False):
     first, last = place[1], place[2]
     ones, twos, in_0, in_1, in_3, inner, ahead_of = plan
     width, depth = moments.shape[2], None
@@ -324,7 +338,11 @@
                 moments[mode * 6 + k] = moments[mode * 6 + k] + sums[k]
         return carry
 
-    lax.fori_loop(0, modes, one_mode, 0)
+    if unroll:
+        for mode in range(modes):
+            one_mode(mode, 0)
+    else:
+        lax.fori_loop(0, modes, one_mode, 0)
 
 
 def send_halves(target, core, half, modes, parts, sems, used):
@@ -348,13 +366,17 @@
     return main, left
 
 
-def main_kernel(modes, layers, cuts, place, za, zb, zc, ma, mb, mc, down, ghost_mass,
-                ones, twos, moments, send, inverse, counts, sems):
+def main_kernel(modes, layers, cuts, place, za, zb, zc, ma, mb, mc, down, ghost_mass, ghost_swap,
+                ones, twos, moments, send, inverse, counts, ghosts, sems):
     plan = plans(layers)[0]
     zeroth = z0_layers(cuts, layers, za, zb, zc)
     zeroth.where.update(Layers((layers, DOWN, down, 0, DOWN)).where)
     mass = mass_layers(cuts, layers, ma, mb, mc)
-    mass.where.update(Layers((layers, 2, ghost_mass, 0, 0)).where)
+    lower = place[0] == 0
+    for i in (0, 1):
+        own, other = ghost_mass[i], ghost_swap[i]
+        ghosts[i] = jnp.concatenate([jnp.where(lower, own, other), jnp.where(lower, other, own)], axis=0)
+    mass.where.update(Layers((layers, 2, ghosts, 0, 0)).where)
     first = Layers((1, layers + 1, ones, 0, layers + 1))
     second = Layers((2, layers - 1, twos, 0, layers - 1))
     moments[...] = jnp.zeros(moments.shape, jnp.float32)
@@ -387,7 +409,7 @@
     first = Layers((-1, 2, ones, 0, 2), (1, layers - 1, ones_in, 0, layers + 1))
     second = Layers((0, 2, twos, 0, 2), (2, layers - 2, twos_in, 0, layers - 1))
     moments[...] = moments_in[...]
-    krylov_step(place, layers, modes, mass, zeroth, first, second, ones, twos, plan, moments, (inverse, counts))
+    krylov_step(place, layers, modes, mass, zeroth, first, second, ones, twos, plan, moments, (inverse, counts), True)
     half = za.shape[1] // 2
     _, other = halves(place[0], half)
     total = send.shape[0] // modes
@@ -421,16 +443,18 @@
         for i in range(2 + c, parts.shape[0], 2):
             block = block + parts[i]
         m = [jnp.sum(jnp.where(lane == 6 * row + k, block, 0.0), axis=1, keepdims=True) for k in range(6)]
-        one, two = m[2] / m[1], m[3] / m[1]
-        pivot = m[3] - one * m[2]
+        inverse = 1.0 / m[1]
+        one, two = m[2] * inverse, m[3] * inverse
+        pivot = jnp.maximum(m[3] - one * m[2], ROUNDING * m[3])
         cross = m[4] - two * m[2]
-        slope = cross / pivot
-        rest = m[5] - two * m[3] - slope * cross
+        over = 1.0 / pivot
+        slope = cross * over
+        rest = jnp.maximum(m[5] - two * m[3] - slope * cross, ROUNDING * m[5])
         right_1 = m[1] - one * m[0]
         right_2 = m[2] - two * m[0] - slope * right_1
         c2 = right_2 / rest
-        c1 = (right_1 - cross * c2) / pivot
-        c0 = (m[0] - m[2] * c1 - m[3] * c2) / m[1]
+        c1 = (right_1 - cross * c2) * over
+        c0 = (m[0] - m[2] * c1 - m[3] * c2) * inverse
         factors.append([jnp.broadcast_to(c, (8, depth)) for c in (c0, c1, c2)])
 
     zeroth = z0_layers(cuts, layers, za, zb, zc)
@@ -444,28 +468,22 @@
     ]
 
     copies = []
-    for slot in (0, 1):
+    for is_own in (True, False):
+        start = (core if is_own else 1 - core) * modes
+        first_group = start == 0
+        chosen = [jnp.where(first_group, f, g) for f, g in zip(*factors)]
         for mode in range(modes):
-            target = slot * modes + mode
-            a, b, c = (f[mode : mode + 1] for f in factors[slot])
-
-            @pl.when(core == slot)
-            def _():
-                for x in range(layers):
-                    planes = []
-                    for field in (zeroth, first, second):
-                        ref, offset, stride = field.where[x]
-                        planes.append(ref[mode * stride + offset, pl.ds(mine, half), :])
-                    out[target, x] = a * planes[0] + b * planes[1] + c * planes[2]
-
-            @pl.when(core != slot)
-            def _():
-                for x in range(layers):
-                    planes = [field(mode, x) for field in theirs]
-                    out[target, x] = a * planes[0] + b * planes[1] + c * planes[2]
-
-            copies.append(pltpu.make_async_copy(out.at[target], out_hbm.at[target], sems.at[target]))
-            copies[-1].start()
+            a, b, c = (f[mode : mode + 1] for f in chosen)
+            for x in range(layers):
+                planes = []
+                for field in (zeroth, first, second) if is_own else theirs:
+                    ref, offset, stride = field.where[x]
+                    rows = pl.ds(mine, half) if is_own else slice(None)
+                    planes.append(ref[mode * stride + offset, rows, :])
+                out[start + mode, x] = a * planes[0] + b * planes[1] + c * planes[2]
+            copy = pltpu.make_async_copy(out.at[start + mode], out_hbm.at[start + mode], sems.at[len(copies)])
+            copy.start()
+            copies.append(copy)
     for copy in copies:
         copy.wait()
 
@@ -506,12 +524,12 @@
     node, node_crossed, fields = kernel(
         "first_layer",
         first_kernel,
-        (planes(group + 2, half), planes(group + 2, half), planes(2 * layers, half)),
+        (planes(group + 2, half), planes(group, half), planes(2 * layers, half)),
         [smem] + [anywhere] * 4,
         [
             pltpu.VMEM((layers, half, depth), f32),
             pltpu.VMEM((layers, half, depth), jnp.int32),
-            pltpu.SemaphoreType.DMA((7,)),
+            pltpu.SemaphoreType.DMA((6,)),
         ],
         4,
         1,
@@ -532,7 +550,7 @@
         return kernel(
             name,
             partial(energy_kernel, low, high, end),
-            outs + (planes(2),) if end else outs,
+            outs + (planes(2, half),) if end else outs,
             [smem, smem] + [vmem] * (4 + 2 * end) + [anywhere] * (len(extra) - 2 * end),
             [
                 pltpu.VMEM((2, n, width, depth), f32),
@@ -547,6 +565,7 @@
     zb, mb = energies("energies_inner", cuts[0], cuts[1], ma)
     zc, mc, ghost_mass = energies("energies_last", cuts[1], layers, halo, halo_swap, mb)
     up = lax.ppermute(zc, "gx", upward)
+    ghost_swap = lax.ppermute(ghost_mass, "gy", across)
 
     tables = [pltpu.VMEM((layers + 2, width, depth), f32)] * 2
     sums = jax.ShapeDtypeStruct((6 * modes, 8, 128), f32)
@@ -554,11 +573,11 @@
         "krylov_main",
         partial(main_kernel, modes, layers, cuts),
         (planes(modes * (layers + 1)), planes(modes * (layers - 1)), sums, planes(modes * 3 * layers, half)),
-        [smem] + [vmem] * 8,
-        tables + [pltpu.SemaphoreType.DMA((5 * modes,))],
+        [smem] + [vmem] * 9,
+        tables + [pltpu.VMEM((2, width, depth), f32), pltpu.SemaphoreType.DMA((5 * modes,))],
         12,
         400,
-    )(place, za, zb, zc, ma, mb, mc, down, ghost_mass)
+    )(place, za, zb, zc, ma, mb, mc, down, ghost_mass, ghost_swap)
     ones_left, twos_left, send, parts = kernel(
         "krylov_left",
         partial(left_kernel, modes, layers, cuts),

time: 45.1 us -> 44.8 us (level)
  blocking collectives: 13.9 us -> 14.9 us
  waiting for transfers between devices: 6.87 us -> 6 us
  Pallas kernels: 14.8 us -> 14.1 us
    ppermute x1, waiting for transfers between devices: 3.31 us -> 0.01 us  [local(): halo = lax.ppermute(node, ('gx', 'gy'), straight)]
    ppermute x1, waiting for transfers between devices: 0.01 us -> 1.69 us  [local(): halo_swap = lax.ppermute(node_crossed, ('gx', 'gy'), crossed)]
    all_to_all x1, blocking collectives: 13.9 us -> 14.9 us  [local(): parts = lax.all_to_all(parts, ('gx', 'gy'), 0, 0, tiled=True)]
    ppermute x0 -> x1, waiting for transfers between devices: none -> 0.86 us  [local(): ghost_swap = lax.ppermute(ghost_mass, 'gy', across)]
    ppermute x0 -> x1, starting transfers between devices: none -> 0.58 us  [local(): ghost_swap = lax.ppermute(ghost_mass, 'gy', across)]
  transfers between devices with their start and end apart: 7 -> 8, of which waited for: 3 -> 4; matrix products, arithmetic and copies ran while one was open for 0% -> 0% of each run, Pallas kernels for 22% -> 21%
where the time goes in v7:
time: 44.8 us; the launch traced here: 44.6 us
  blocking collectives  14.9 us (33%)
  Pallas kernels  14.1 us (31%)
  starting transfers between devices  9.34 us (21%)
  waiting for transfers between devices  6 us (13%)
    all_to_all x1, blocking collectives, local(): parts = lax.all_to_all(parts, ('gx', 'gy'), 0, 0, tiled=True)  14.9 us
    pallas_call x3, Pallas kernels, energies(): kernel(name, partial(energy_kernel, low, high, end), outs + (planes(2, ha...  6.6 us
    ppermute x1, starting transfers between devices, local(): up = lax.ppermute(zc, 'gx', upward)  4.23 us
    pallas_call x1, Pallas kernels, local(): kernel('krylov_main', partial(main_kernel, modes, layers, cuts), (planes(...  2.84 us
    pallas_call x1, Pallas kernels, local(): kernel('first_layer', first_kernel, (planes(group + 2, half), planes(grou...  1.95 us
    ppermute x1, waiting for transfers between devices, local(): lax.ppermute(fields, 'gy', across)  1.87 us
    ppermute x1, waiting for transfers between devices, local(): halo_swap = lax.ppermute(node_crossed, ('gx', 'gy'), crossed)  1.69 us
    pallas_call x1, Pallas kernels, local(): kernel('combine', partial(combine_kernel, modes, layers, cuts), jax.Shape...  1.61 us
  transfers between devices with their start and end apart: 8, of which 4 were waited for; matrix products, arithmetic and copies ran while one was open for 0% of the time, Pallas kernels for 21%

profile of v7, /device:TPU:0, one launch (start us, length us, event | category | flops | bytes accessed | tf_op | source)
XLA Modules:
  0.0 44.6 jit_solution(6551086075553435095)
XLA Ops:
  0.0 0.1 pad_add_fusion.place.refs_0_
  0.1 0.0 copy-start
  0.1 0.0 copy-start.1
  0.1 1.9 %first_layer.1 = (f32[11,16,256]{2,1,0:T(8,128)S(1)}, f32[9,16,256]{2,1,0:T(8,128)S(1)}, f32[16,16,256]{2,1,0:T(8,128)S(1)}) custom-call(s32[3]{0:T(128)S(1)} %pad_add_fusion.place.refs_0_, f32[18,8,16,256]{3,2,1,0:T(8,128)} %refs_2_.2, f32[8,16,256]{2,1,0:T(8,128)} %density.1, f32[8,16,256]{2,1,0:T(8,128)} %mass.1, s32[8,16,256]{2,1,0:T(8,128)} %passive.1), custom_call_target="tpu_custom_call" | custom-call | flops 1048576 | bytes 1048576 | tf_op jit(solution)/shard_map/first_layer/pallas_call | solution.py:524
  2.0 0.0 copy-done
  2.0 0.5 %collective-permute-start = (f32[18,8,16,256]{3,2,1,0:T(8,128)S(1)}, f32[18,8,16,256]{3,2,1,0:T(8,128)S(1)}, u32[]{:S(2)}, u32[]{:S(2)}) collective-permute-start(f32[18,8,16,256]{3,2,1,0:T(8,128)S(1)} %copy-done), channel_id=1, source_target_pairs={{0,1},{1,0},{2,3},{3,2},{4,5},{5,4},{6,7},{7,6},{8,9},{9,8},{10,11... | collective-permute-start | bytes 7077896 | tf_op jit(solution)/shard_map/ppermute | solution.py:538
  2.6 0.1 collective-permute-start.1
  2.6 1.3 %collective-permute-start.2 = (f32[11,16,256]{2,1,0:T(8,128)S(1)}, f32[11,16,256]{2,1,0:T(8,128)S(1)}, u32[]{:S(2)}, u32[]{:S(2)}) collective-permute-start(f32[11,16,256]{2,1,0:T(8,128)S(1)} %get-tuple-element.24), channel_id=1, source_target_pairs={{2,0},{3,1},{4,2},{5,3},{6,4},{7,5},{8,6},{9,7},{10,8},{11,9},{12,... | collective-permute-start | bytes 540680 | tf_op jit(solution)/shard_map/ppermute | solution.py:541
  3.9 1.3 %collective-permute-start.3 = (f32[9,16,256]{2,1,0:T(8,128)S(1)}, f32[9,16,256]{2,1,0:T(8,128)S(1)}, u32[]{:S(2)}, u32[]{:S(2)}) collective-permute-start(f32[9,16,256]{2,1,0:T(8,128)S(1)} %get-tuple-element.29), channel_id=1, source_target_pairs={{2,1},{3,0},{4,3},{5,2},{6,5},{7,4},{8,7},{9,6},{10,9},{11,8},{12,... | collective-permute-start | bytes 442376 | tf_op jit(solution)/shard_map/ppermute | solution.py:542
  5.2 1.9 %collective-permute-done.1.refs_5_ = f32[16,16,256]{2,1,0:T(8,128)S(1)} collective-permute-done((f32[16,16,256]{2,1,0:T(8,128)S(1)}, f32[16,16,256]{2,1,0:T(8,128)S(1)}, u32[]{:S(2)}, u32[]{:S(2)}) %collective-permute-start.1) | collective-permute-done | bytes 262176 | tf_op jit(solution)/shard_map/ppermute | solution.py:538
  7.1 0.0 collective-permute-done.refs_3_
  7.1 0.0 copy-done.1
  7.1 2.4 %energies_first.1 = (f32[9,32,256]{2,1,0:T(8,128)S(1)}, f32[3,32,256]{2,1,0:T(8,128)S(1)}) custom-call(s32[3]{0:T(128)S(1)} %pad_add_fusion.place.refs_0_, f32[6]{0:T(128)S(1)} %copy-done.1, f32[18,8,16,256]{3,2,1,0:T(8,128)S(1)} %copy-done, f32[18,8,16,256]{3,2,1,0:T(8,128)S(1)} %collective-permute-done.refs_3_, ...), custom_call_target="tpu_custom_call" | custom-call | flops 629145600 | bytes 1048576 | tf_op jit(solution)/shard_map/energies_first/pallas_call | solution.py:550
  9.5 1.3 %collective-permute-start.5 = (f32[9,32,256]{2,1,0:T(8,128)S(1)}, f32[9,32,256]{2,1,0:T(8,128)S(1)}, u32[]{:S(2)}, u32[]{:S(2)}) collective-permute-start(f32[9,32,256]{2,1,0:T(8,128)S(1)} %get-tuple-element.27.za), channel_id=1, source_target_pairs={{2,0},{4,2},{6,4},{8,6},{10,8},{12,10},{14,12},{3,1},{5,3},{7,5},{... | collective-permute-start | bytes 884744 | tf_op jit(solution)/shard_map/ppermute | solution.py:564
  10.8 2.4 %energies_inner.1 = (f32[9,32,256]{2,1,0:T(8,128)S(1)}, f32[3,32,256]{2,1,0:T(8,128)S(1)}) custom-call(s32[3]{0:T(128)S(1)} %pad_add_fusion.place.refs_0_, f32[6]{0:T(128)S(1)} %copy-done.1, f32[18,8,16,256]{3,2,1,0:T(8,128)S(1)} %copy-done, f32[18,8,16,256]{3,2,1,0:T(8,128)S(1)} %collective-permute-done.refs_3_, ...), custom_call_target="tpu_custom_call" | custom-call | flops 629145600 | bytes 1048576 | tf_op jit(solution)/shard_map/energies_inner/pallas_call | solution.py:550
  13.2 1.7 %collective-permute-done.3.refs_7_ = f32[9,16,256]{2,1,0:T(8,128)S(1)} collective-permute-done((f32[9,16,256]{2,1,0:T(8,128)S(1)}, f32[9,16,256]{2,1,0:T(8,128)S(1)}, u32[]{:S(2)}, u32[]{:S(2)}) %collective-permute-start.3) | collective-permute-done | bytes 147488 | tf_op jit(solution)/shard_map/ppermute | solution.py:542
  14.9 0.0 collective-permute-done.2.refs_6_
  14.9 1.8 %energies_last.1 = (f32[7,32,256]{2,1,0:T(8,128)S(1)}, f32[2,32,256]{2,1,0:T(8,128)S(1)}, f32[2,16,256]{2,1,0:T(8,128)S(1)}) custom-call(s32[3]{0:T(128)S(1)} %pad_add_fusion.place.refs_0_, f32[6]{0:T(128)S(1)} %copy-done.1, f32[18,8,16,256]{3,2,1,0:T(8,128)S(1)} %copy-done, f32[18,8,16,256]{3,2,1,0:T(8,128)S(1)} %collective-permute-done.refs_3_, ...), custom_call_target="tpu_custom_call" | custom-call | flops 419430400 | bytes 1048576 | tf_op jit(solution)/shard_map/energies_last/pallas_call | solution.py:550
  16.7 4.2 %collective-permute-start.4 = (f32[7,32,256]{2,1,0:T(8,128)S(1)}, f32[7,32,256]{2,1,0:T(8,128)S(1)}, u32[]{:S(2)}, u32[]{:S(2)}) collective-permute-start(f32[7,32,256]{2,1,0:T(8,128)S(1)} %get-tuple-element.31.zc), channel_id=1, source_target_pairs={{0,2},{2,4},{4,6},{6,8},{8,10},{10,12},{12,14},{1,3},{3,5},{5,7},{... | collective-permute-start | bytes 688136 | tf_op jit(solution)/shard_map/ppermute | solution.py:567
  21.0 0.6 %collective-permute-start.6 = (f32[2,16,256]{2,1,0:T(8,128)S(1)}, f32[2,16,256]{2,1,0:T(8,128)S(1)}, u32[]{:S(2)}, u32[]{:S(2)}) collective-permute-start(f32[2,16,256]{2,1,0:T(8,128)S(1)} %get-tuple-element.34.ghost_mass), channel_id=1, source_target_pairs={{0,1},{1,0},{2,3},{3,2},{4,5},{5,4},{6,7},{7,6},{8,9},{9,8},{10,11... | collective-permute-start | bytes 98312 | tf_op jit(solution)/shard_map/ppermute | solution.py:568
  21.5 0.9 %collective-permute-done.6.ghost_swap = f32[2,16,256]{2,1,0:T(8,128)S(1)} collective-permute-done((f32[2,16,256]{2,1,0:T(8,128)S(1)}, f32[2,16,256]{2,1,0:T(8,128)S(1)}, u32[]{:S(2)}, u32[]{:S(2)}) %collective-permute-start.6) | collective-permute-done | bytes 32800 | tf_op jit(solution)/shard_map/ppermute | solution.py:568
  22.4 0.0 collective-permute-done.5.down
  22.4 2.8 %krylov_main.1 = (f32[27,32,256]{2,1,0:T(8,128)S(1)}, f32[21,32,256]{2,1,0:T(8,128)S(1)}, f32[18,8,128]{2,1,0:T(8,128)S(1)}, f32[72,16,256]{2,1,0:T(8,128)S(1)}) custom-call(s32[3]{0:T(128)S(1)} %pad_add_fusion.place.refs_0_, f32[9,32,256]{2,1,0:T(8,128)S(1)} %get-tuple-element.27.za, f32[9,32,256]{2,1,0:T(8,128)S(1)} %get-tuple-element.32.zb, ...), custom_call_target="tpu_custom_call" | custom-call | flops 419430400 | bytes 1048576 | tf_op jit(solution)/shard_map/krylov_main/pallas_call | solution.py:572
  25.2 1.6 %collective-permute-done.4.up = f32[7,32,256]{2,1,0:T(8,128)S(1)} collective-permute-done((f32[7,32,256]{2,1,0:T(8,128)S(1)}, f32[7,32,256]{2,1,0:T(8,128)S(1)}, u32[]{:S(2)}, u32[]{:S(2)}) %collective-permute-start.4) | collective-permute-done | bytes 229408 | tf_op jit(solution)/shard_map/ppermute | solution.py:567
  26.8 1.2 %krylov_left.1 = (f32[6,32,256]{2,1,0:T(8,128)S(1)}, f32[6,32,256]{2,1,0:T(8,128)S(1)}, f32[72,16,256]{2,1,0:T(8,128)S(1)}, f32[16,8,128]{2,1,0:T(8,128)S(1)}) custom-call(s32[3]{0:T(128)S(1)} %pad_add_fusion.place.refs_0_, f32[9,32,256]{2,1,0:T(8,128)S(1)} %get-tuple-element.27.za, ...), custom_call_target="tpu_custom_call", output_to_operand_aliasing={{2}: (7, {})} | custom-call | flops 209715200 | bytes 1048576 | tf_op jit(solution)/shard_map/krylov_left/pallas_call | solution.py:581
  28.0 0.1 collective-permute-start.7
  28.0 14.9 %all_to_all.5.parts = f32[16,8,128]{2,1,0:T(8,128)S(1)} all-to-all(f32[16,8,128]{2,1,0:T(8,128)S(1)} %get-tuple-element.39), channel_id=1, replica_groups=mesh['grp'=2,'gx'=8,'gy'=2] {'gx','gy'}, dimensions={0} | all-to-all | bytes 131072 | tf_op jit(solution)/shard_map/all_to_all | solution.py:597
  42.9 0.0 collective-permute-done.7.swap
  42.9 1.6 %combine.1 = f32[6,8,16,256]{3,2,1,0:T(8,128)} custom-call(s32[3]{0:T(128)S(1)} %pad_add_fusion.place.refs_0_, f32[16,8,128]{2,1,0:T(8,128)S(1)} %all_to_all.5.parts, f32[9,32,256]{2,1,0:T(8,128)S(1)} %get-tuple-element.27.za, f32[9,32,256]{2,1,0:T(8,128)S(1)} %get-tuple-element.32.zb, f32[7,32,256]{2,1,0:T(8,128)S(1)} %get-tuple-element.31.zc, ...), custom_call_target="tpu_custom_call" | custom-call | flops 104857600 | bytes 1048576 | tf_op jit(solution)/shard_map/combine/pallas_call | solution.py:599
Async XLA Ops:
  0.1 2.0 %copy-start = (f32[18,8,16,256]{3,2,1,0:T(8,128)S(1)}, f32[18,8,16,256]{3,2,1,0:T(8,128)}, u32[]{:S(2)}) copy-start(f32[18,8,16,256]{3,2,1,0:T(8,128)} %refs_2_.2) | copy-start | bytes 7077892
  0.1 7.0 %copy-start.1 = (f32[6]{0:T(128)S(1)}, f32[6]{0:T(128)}, u32[]{:S(2)}) copy-start(f32[6]{0:T(128)} %refs_1_.5) | copy-start | bytes 76
  2.0 5.1 %collective-permute-start = (f32[18,8,16,256]{3,2,1,0:T(8,128)S(1)}, f32[18,8,16,256]{3,2,1,0:T(8,128)S(1)}, u32[]{:S(2)}, u32[]{:S(2)}) collective-permute-start(f32[18,8,16,256]{3,2,1,0:T(8,128)S(1)} %copy-done), channel_id=1, source_target_pairs={{0,1},{1,0},{2,3},{3,2},{4,5},{5,4},{6,7},{7,6},{8,9},{9,8},{10,11... | collective-permute-start | bytes 7077896 | tf_op jit(solution)/shard_map/ppermute | solution.py:538
  2.6 4.5 %collective-permute-start.1 = (f32[16,16,256]{2,1,0:T(8,128)S(1)}, f32[16,16,256]{2,1,0:T(8,128)S(1)}, u32[]{:S(2)}, u32[]{:S(2)}) collective-permute-start(f32[16,16,256]{2,1,0:T(8,128)S(1)} %get-tuple-element.26.refs_4_), channel_id=1, source_target_pairs={{0,1},{1,0},{2,3},{3,2},{4,5},{5,4},{6,7},{7,6},{8,9},{9,8},{10,11... | collective-permute-start | bytes 786440 | tf_op jit(solution)/shard_map/ppermute | solution.py:538
  2.6 12.2 %collective-permute-start.2 = (f32[11,16,256]{2,1,0:T(8,128)S(1)}, f32[11,16,256]{2,1,0:T(8,128)S(1)}, u32[]{:S(2)}, u32[]{:S(2)}) collective-permute-start(f32[11,16,256]{2,1,0:T(8,128)S(1)} %get-tuple-element.24), channel_id=1, source_target_pairs={{2,0},{3,1},{4,2},{5,3},{6,4},{7,5},{8,6},{9,7},{10,8},{11,9},{12,... | collective-permute-start | bytes 540680 | tf_op jit(solution)/shard_map/ppermute | solution.py:541
  3.9 10.9 %collective-permute-start.3 = (f32[9,16,256]{2,1,0:T(8,128)S(1)}, f32[9,16,256]{2,1,0:T(8,128)S(1)}, u32[]{:S(2)}, u32[]{:S(2)}) collective-permute-start(f32[9,16,256]{2,1,0:T(8,128)S(1)} %get-tuple-element.29), channel_id=1, source_target_pairs={{2,1},{3,0},{4,3},{5,2},{6,5},{7,4},{8,7},{9,6},{10,9},{11,8},{12,... | collective-permute-start | bytes 442376 | tf_op jit(solution)/shard_map/ppermute | solution.py:542
  9.5 12.9 %collective-permute-start.5 = (f32[9,32,256]{2,1,0:T(8,128)S(1)}, f32[9,32,256]{2,1,0:T(8,128)S(1)}, u32[]{:S(2)}, u32[]{:S(2)}) collective-permute-start(f32[9,32,256]{2,1,0:T(8,128)S(1)} %get-tuple-element.27.za), channel_id=1, source_target_pairs={{2,0},{4,2},{6,4},{8,6},{10,8},{12,10},{14,12},{3,1},{5,3},{7,5},{... | collective-permute-start | bytes 884744 | tf_op jit(solution)/shard_map/ppermute | solution.py:564
  16.7 10.1 %collective-permute-start.4 = (f32[7,32,256]{2,1,0:T(8,128)S(1)}, f32[7,32,256]{2,1,0:T(8,128)S(1)}, u32[]{:S(2)}, u32[]{:S(2)}) collective-permute-start(f32[7,32,256]{2,1,0:T(8,128)S(1)} %get-tuple-element.31.zc), channel_id=1, source_target_pairs={{0,2},{2,4},{4,6},{6,8},{8,10},{10,12},{12,14},{1,3},{3,5},{5,7},{... | collective-permute-start | bytes 688136 | tf_op jit(solution)/shard_map/ppermute | solution.py:567
  21.0 1.4 %collective-permute-start.6 = (f32[2,16,256]{2,1,0:T(8,128)S(1)}, f32[2,16,256]{2,1,0:T(8,128)S(1)}, u32[]{:S(2)}, u32[]{:S(2)}) collective-permute-start(f32[2,16,256]{2,1,0:T(8,128)S(1)} %get-tuple-element.34.ghost_mass), channel_id=1, source_target_pairs={{0,1},{1,0},{2,3},{3,2},{4,5},{5,4},{6,7},{7,6},{8,9},{9,8},{10,11... | collective-permute-start | bytes 98312 | tf_op jit(solution)/shard_map/ppermute | solution.py:568
  28.0 15.0 %collective-permute-start.7 = (f32[72,16,256]{2,1,0:T(8,128)S(1)}, f32[72,16,256]{2,1,0:T(8,128)S(1)}, u32[]{:S(2)}, u32[]{:S(2)}) collective-permute-start(f32[72,16,256]{2,1,0:T(8,128)S(1)} %get-tuple-element.42), channel_id=1, source_target_pairs={{0,1},{1,0},{2,3},{3,2},{4,5},{5,4},{6,7},{7,6},{8,9},{9,8},{10,11... | collective-permute-start | bytes 3538952 | tf_op jit(solution)/shard_map/ppermute | solution.py:596

commit v8 on v7

--- a/solution.py
+++ b/solution.py
@@ -150,17 +150,24 @@
     return count
 
 
+def position():
+    at = lax.axis_index("gx")
+    return lax.axis_index("gy"), at == 0, at == lax.axis_size("gx") - 1
+
+
 def halves(core, half):
     return pl.multiple_of(core * half, half), pl.multiple_of((1 - core) * half, half)
 
 
-def first_kernel(place, modes, density, mass, passive, straight, crossed, fields, signed, flags, sems):
+def first_kernel(modes, density, mass, passive, straight, crossed, fields, own, signed, flags, sems):
     group = modes.shape[0] // 2
     layers = density.shape[0]
+    here, _, _ = position()
     moves = [(density, signed), (passive, flags), (mass, fields.at[pl.ds(layers, layers)])]
-    for target, core in ((straight, place[0]), (crossed, 1 - place[0])):
+    for target, core in ((straight, here), (crossed, 1 - here)):
         moves.append((modes.at[pl.ds(core * group, group), 0], target.at[pl.ds(0, group)]))
     moves.append((mass.at[pl.ds(0, 2)], straight.at[pl.ds(group, 2)]))
+    moves.append((modes.at[pl.ds(here * group, group)], own))
     copies = [pltpu.make_async_copy(*move, sems.at[i]) for i, move in enumerate(moves)]
     for copy in copies:
         copy.start()
@@ -173,16 +180,15 @@
 
 
 def energy_kernel(low, high, end, *refs):
-    place, eig, modes, modes_swap, fields, fields_swap = refs[:6]
+    eig, modes, modes_swap, fields, fields_swap = refs[:5]
     if end:
-        halo, halo_swap = refs[6:8]
+        halo, halo_swap = refs[5:7]
         z_out, mass_out, ghost_mass, floats, sums = refs[-5:]
     else:
         z_out, mass_out, floats, sums = refs[-4:]
-    layers, half, depth = modes.shape[1:]
-    group = modes.shape[0] // 2
+    group, layers, half, depth = modes.shape
     width, count = 2 * half, high - low
-    core, first, last = place[0], place[1], place[2]
+    core, first, last = position()
     start = core * group
     lower = core == 0
 
@@ -208,7 +214,7 @@
     def node(row, x):
         if x == layers:
             return whole(halo[row], halo_swap[row])
-        return whole(modes[start + row, x], modes_swap[start + row, x])
+        return whole(modes[row, x], modes_swap[start + row, x])
 
     ring = sums.shape[0]
 
@@ -240,7 +246,11 @@
                 z_out[(mode * count + i,) + span] = result
 
     total = group // 3 * (count + 1)
-    values = [eig[core * (group // 3) + mode] for mode in range(group // 3)]
+    each = group // 3
+    values = []
+    for mode in range(each):
+        value = jnp.where(lower, eig[:, mode : mode + 1], eig[:, each + mode : each + mode + 1])
+        values.append(jnp.broadcast_to(value, (8, 128)))
     transform(0)
     transform(1)
     for step in range(total):
@@ -262,8 +272,8 @@
         return ref[mode * stride + offset]
 
 
-def krylov_step(place, layers, modes, mass, zeroth, first_in, second_in, first_out, second_out, plan, moments, scratch, unroll=False):
-    first, last = place[1], place[2]
+def krylov_step(layers, modes, mass, zeroth, first_in, second_in, first_out, second_out, plan, moments, scratch, unroll=False):
+    _, first, last = position()
     ones, twos, in_0, in_1, in_3, inner, ahead_of = plan
     width, depth = moments.shape[2], None
     inverse, count_of = scratch
@@ -366,13 +376,14 @@
     return main, left
 
 
-def main_kernel(modes, layers, cuts, place, za, zb, zc, ma, mb, mc, down, ghost_mass, ghost_swap,
+def main_kernel(modes, layers, cuts, za, zb, zc, ma, mb, mc, down, ghost_mass, ghost_swap,
                 ones, twos, moments, send, inverse, counts, ghosts, sems):
     plan = plans(layers)[0]
     zeroth = z0_layers(cuts, layers, za, zb, zc)
     zeroth.where.update(Layers((layers, DOWN, down, 0, DOWN)).where)
     mass = mass_layers(cuts, layers, ma, mb, mc)
-    lower = place[0] == 0
+    core, _, _ = position()
+    lower = core == 0
     for i in (0, 1):
         own, other = ghost_mass[i], ghost_swap[i]
         ghosts[i] = jnp.concatenate([jnp.where(lower, own, other), jnp.where(lower, other, own)], axis=0)
@@ -383,10 +394,10 @@
     a, b = cuts
     half = za.shape[1] // 2
     known = [(za, 0, a, a, 0), (zb, 0, b - a, b - a, a), (zc, 0, layers - b, layers - b, b)]
-    copies = send_halves(send, place[0], half, modes, known, sems, 0)
-    krylov_step(place, layers, modes, mass, zeroth, first, second, ones, twos, plan, moments, (inverse, counts))
+    copies = send_halves(send, core, half, modes, known, sems, 0)
+    krylov_step(layers, modes, mass, zeroth, first, second, ones, twos, plan, moments, (inverse, counts))
     made = [(ones, 0, layers + 1, layers - 1, layers), (twos, 0, layers - 1, layers - 2, 2 * layers - 1)]
-    copies += send_halves(send, place[0], half, modes, made, sems, len(copies))
+    copies += send_halves(send, core, half, modes, made, sems, len(copies))
     for copy in copies:
         copy.wait()
 
@@ -401,7 +412,7 @@
     return Layers((0, a, ma, 0, 0), (a, b - a, mb, 0, 0), (b, layers - b, mc, 0, 0))
 
 
-def left_kernel(modes, layers, cuts, place, za, ma, up, ones_in, twos_in, moments_in, _,
+def left_kernel(modes, layers, cuts, za, ma, up, ones_in, twos_in, moments_in, _,
                 ones, twos, send, parts, inverse, counts, moments):
     plan = plans(layers)[1]
     zeroth = Layers((-UP, UP, up, 0, UP), (0, cuts[0], za, 0, cuts[0]))
@@ -409,53 +420,54 @@
     first = Layers((-1, 2, ones, 0, 2), (1, layers - 1, ones_in, 0, layers + 1))
     second = Layers((0, 2, twos, 0, 2), (2, layers - 2, twos_in, 0, layers - 1))
     moments[...] = moments_in[...]
-    krylov_step(place, layers, modes, mass, zeroth, first, second, ones, twos, plan, moments, (inverse, counts), True)
+    krylov_step(layers, modes, mass, zeroth, first, second, ones, twos, plan, moments, (inverse, counts), True)
     half = za.shape[1] // 2
-    _, other = halves(place[0], half)
+    core, _, _ = position()
+    _, other = halves(core, half)
     total = send.shape[0] // modes
     for mode in range(modes):
         at = (mode + 1) * total - 3
         send[at] = ones[2 * mode + 1, pl.ds(other, half), :]
         send[at + 1] = twos[2 * mode, pl.ds(other, half), :]
         send[at + 2] = twos[2 * mode + 1, pl.ds(other, half), :]
-    lines = [jnp.sum(moments[i], axis=0, keepdims=True) for i in range(6 * modes)]
-    lines = jnp.concatenate(lines + [jnp.zeros((-len(lines) % 8, 128), jnp.float32)], axis=0)
-    totals = jnp.sum(lines, axis=1, keepdims=True)
-    row = lax.broadcasted_iota(jnp.int32, lines.shape, 0)
-    lane = lax.broadcasted_iota(jnp.int32, lines.shape, 1)
-    line = jnp.sum(jnp.where(row == lane, totals, 0.0), axis=0, keepdims=True)
-    block = jnp.broadcast_to(line, (8, 128))
+    row = lax.broadcasted_iota(jnp.int32, (8, 128), 0)
+    lane = lax.broadcasted_iota(jnp.int32, (8, 128), 1)
+    rows = []
+    for mode in range(modes):
+        lines = [jnp.sum(moments[6 * mode + k], axis=0, keepdims=True) for k in range(6)]
+        totals = jnp.sum(jnp.concatenate(lines + [jnp.zeros((2, 128), jnp.float32)], axis=0), axis=1, keepdims=True)
+        rows.append(jnp.sum(jnp.where(row == lane, totals, 0.0), axis=0, keepdims=True))
+    block = jnp.concatenate(rows + [jnp.zeros((8 - modes, 128), jnp.float32)], axis=0)
     for i in range(parts.shape[0]):
         parts[i] = block
 
 
-def combine_kernel(modes, layers, cuts, place, parts, za, zb, zc, ones_in, twos_in,
+def combine_kernel(modes, layers, cuts, parts, za, zb, zc, ones_in, twos_in,
                    ones_left, twos_left, swap, out_hbm, out, sems):
-    core = place[0]
+    core, _, _ = position()
     half, depth = out.shape[2:]
     mine, _ = halves(core, half)
-    shape = (8, 128)
-    lane = lax.broadcasted_iota(jnp.int32, shape, 1)
-    row = lax.broadcasted_iota(jnp.int32, shape, 0)
-    factors = []
+    blocks = []
     for c in (0, 1):
         block = parts[c]
         for i in range(2 + c, parts.shape[0], 2):
             block = block + parts[i]
-        m = [jnp.sum(jnp.where(lane == 6 * row + k, block, 0.0), axis=1, keepdims=True) for k in range(6)]
-        inverse = 1.0 / m[1]
-        one, two = m[2] * inverse, m[3] * inverse
-        pivot = jnp.maximum(m[3] - one * m[2], ROUNDING * m[3])
-        cross = m[4] - two * m[2]
-        over = 1.0 / pivot
-        slope = cross * over
-        rest = jnp.maximum(m[5] - two * m[3] - slope * cross, ROUNDING * m[5])
-        right_1 = m[1] - one * m[0]
-        right_2 = m[2] - two * m[0] - slope * right_1
-        c2 = right_2 / rest
-        c1 = (right_1 - cross * c2) * over
-        c0 = (m[0] - m[2] * c1 - m[3] * c2) * inverse
-        factors.append([jnp.broadcast_to(c, (8, depth)) for c in (c0, c1, c2)])
+        blocks.append(block)
+    both = jnp.concatenate(blocks, axis=0)
+    m = [jnp.broadcast_to(both[:, k : k + 1], both.shape) for k in range(6)]
+    inverse = 1.0 / m[1]
+    one, two = m[2] * inverse, m[3] * inverse
+    pivot = jnp.maximum(m[3] - one * m[2], ROUNDING * m[3])
+    cross = m[4] - two * m[2]
+    over = 1.0 / pivot
+    slope = cross * over
+    rest = jnp.maximum(m[5] - two * m[3] - slope * cross, ROUNDING * m[5])
+    right_1 = m[1] - one * m[0]
+    right_2 = m[2] - two * m[0] - slope * right_1
+    c2 = right_2 / rest
+    c1 = (right_1 - cross * c2) * over
+    c0 = (m[0] - m[2] * c1 - m[3] * c2) * inverse
+    wide = [jnp.concatenate([c] * (depth // 128), axis=1) for c in (c0, c1, c2)]
 
     zeroth = z0_layers(cuts, layers, za, zb, zc)
     first = Layers((0, 1, ones_left, 1, 2), (1, layers - 1, ones_in, 0, layers + 1))
@@ -471,7 +483,7 @@
     for is_own in (True, False):
         start = (core if is_own else 1 - core) * modes
         first_group = start == 0
-        chosen = [jnp.where(first_group, f, g) for f, g in zip(*factors)]
+        chosen = [jnp.where(first_group, c[:8], c[8:]) for c in wide]
         for mode in range(modes):
             a, b, c = (f[mode : mode + 1] for f in chosen)
             for x in range(layers):
@@ -494,13 +506,10 @@
     group = mode_shapes.shape[0] // 2
     modes = group // 3
     width = 2 * half
-    core, at = lax.axis_index("gy"), lax.axis_index("gx")
     count = lax.axis_size("gx")
-    place = jnp.stack([core, (at == 0).astype(jnp.int32), (at == count - 1).astype(jnp.int32)]).astype(jnp.int32)
     across = [(0, 1), (1, 0)]
     downward = [(i, i - 1) for i in range(1, count)]
     upward = [(i, i + 1) for i in range(count - 1)]
-    smem = pl.BlockSpec(memory_space=pltpu.SMEM)
     vmem = pl.BlockSpec(memory_space=pltpu.VMEM)
     anywhere = pl.BlockSpec(memory_space=pl.ANY)
 
@@ -521,21 +530,25 @@
         )
 
     stored = [pltpu.with_memory_space_constraint(x, pltpu.HBM) for x in (mode_shapes, density, filter_mass, passive)]
-    node, node_crossed, fields = kernel(
+    node, node_crossed, fields, own = kernel(
         "first_layer",
         first_kernel,
-        (planes(group + 2, half), planes(group, half), planes(2 * layers, half)),
-        [smem] + [anywhere] * 4,
+        (
+            planes(group + 2, half),
+            planes(group, half),
+            planes(2 * layers, half),
+            jax.ShapeDtypeStruct((group, layers, half, depth), f32),
+        ),
+        [anywhere] * 4,
         [
             pltpu.VMEM((layers, half, depth), f32),
             pltpu.VMEM((layers, half, depth), jnp.int32),
-            pltpu.SemaphoreType.DMA((6,)),
+            pltpu.SemaphoreType.DMA((7,)),
         ],
         4,
         1,
-    )(place, *stored)
-    source, _ = lax.optimization_barrier((mode_shapes, node))
-    operands = [source, lax.ppermute(source, "gy", across), fields, lax.ppermute(fields, "gy", across)]
+    )(*stored)
+    operands = [own, lax.ppermute(mode_shapes, "gy", across), fields, lax.ppermute(fields, "gy", across)]
     straight = [(2 * i + c, 2 * i - 2 + c) for i in range(1, count) for c in (0, 1)]
     crossed = [(2 * i + c, 2 * i - 1 - c) for i in range(1, count) for c in (0, 1)]
     halo = lax.ppermute(node, ("gx", "gy"), straight)
@@ -551,14 +564,14 @@
             name,
             partial(energy_kernel, low, high, end),
             outs + (planes(2, half),) if end else outs,
-            [smem, smem] + [vmem] * (4 + 2 * end) + [anywhere] * (len(extra) - 2 * end),
+            [vmem] * (5 + 2 * end) + [anywhere] * (len(extra) - 2 * end),
             [
                 pltpu.VMEM((2, n, width, depth), f32),
                 pltpu.VMEM((4, 12, width, depth), f32),
             ],
             12,
             n * 200,
-        )(place, eigenvalues, *operands, *extra)
+        )(eigenvalues[None], *operands, *extra)
 
     za, ma = energies("energies_first", 0, cuts[0])
     down = lax.ppermute(za, "gx", downward)
@@ -573,11 +586,11 @@
         "krylov_main",
         partial(main_kernel, modes, layers, cuts),
         (planes(modes * (layers + 1)), planes(modes * (layers - 1)), sums, planes(modes * 3 * layers, half)),
-        [smem] + [vmem] * 9,
+        [vmem] * 9,
         tables + [pltpu.VMEM((2, width, depth), f32), pltpu.SemaphoreType.DMA((5 * modes,))],
         12,
         400,
-    )(place, za, zb, zc, ma, mb, mc, down, ghost_mass, ghost_swap)
+    )(za, zb, zc, ma, mb, mc, down, ghost_mass, ghost_swap)
     ones_left, twos_left, send, parts = kernel(
         "krylov_left",
         partial(left_kernel, modes, layers, cuts),
@@ -587,12 +600,12 @@
             planes(modes * 3 * layers, half),
             jax.ShapeDtypeStruct((2 * count, 8, 128), f32),
         ),
-        [smem] + [vmem] * 7,
+        [vmem] * 7,
         tables + [pltpu.VMEM((6 * modes, 8, 128), f32)],
         12,
         200,
-        aliases={7: 2},
-    )(place, za, ma, up, ones_in, twos_in, moments, send)
+        aliases={6: 2},
+    )(za, ma, up, ones_in, twos_in, moments, send)
     swap_in = lax.ppermute(send, "gy", across)
     parts = lax.all_to_all(parts, ("gx", "gy"), 0, 0, tiled=True)
 
@@ -600,12 +613,12 @@
         "combine",
         partial(combine_kernel, modes, layers, cuts),
         jax.ShapeDtypeStruct((2 * modes, layers, half, depth), f32),
-        [smem] + [vmem] * 9,
+        [vmem] * 9,
         [pltpu.VMEM((2 * modes, layers, half, depth), f32), pltpu.SemaphoreType.DMA((2 * modes,))],
         12,
         100,
         anywhere,
-    )(place, parts, za, zb, zc, ones_in, twos_in, ones_left, twos_left, swap_in)
+    )(parts, za, zb, zc, ones_in, twos_in, ones_left, twos_left, swap_in)
 
 
 def solution(mesh):

time: 44.8 us -> 41.8 us (0.933)
  Pallas kernels: 14.1 us -> 10.7 us
  blocking collectives: 14.9 us -> 13.3 us
  waiting for transfers between devices: 6 us -> 7.18 us
  starting transfers between devices: 9.34 us -> 10.4 us
    ppermute x1, waiting for transfers between devices: 1.69 us -> 4.38 us  [local(): halo_swap = lax.ppermute(node_crossed, ('gx', 'gy'), crossed)]
    ppermute x1, waiting for transfers between devices: 1.87 us -> 0.15 us  [local(): lax.ppermute(fields, 'gy', across)]
    all_to_all x1, blocking collectives: 14.9 us -> 13.3 us  [local(): parts = lax.all_to_all(parts, ('gx', 'gy'), 0, 0, tiled=True)]
    pallas_call x3, Pallas kernels: 6.6 us -> 5 us  [energies(): kernel(name, partial(energy_kernel, low, high, end), outs + (planes(2, ha...]
    ppermute x1, starting transfers between devices: 0.58 us -> 1.37 us  [local(): ghost_swap = lax.ppermute(ghost_mass, 'gy', across)]
    pallas_call x1, Pallas kernels: 2.84 us -> 2.31 us  [local(): kernel('krylov_main', partial(main_kernel, modes, layers, cuts), (planes(...]
    pallas_call x1, Pallas kernels: 1.15 us -> 0.63 us  [local(): kernel('krylov_left', partial(left_kernel, modes, layers, cuts), (planes(...]
    pallas_call x1, Pallas kernels: 1.61 us -> 1.09 us  [local(): kernel('combine', partial(combine_kernel, modes, layers, cuts), jax.Shape...]
  transfers between devices with their start and end apart: 8 -> 8, of which waited for: 4 -> 4; matrix products, arithmetic and copies ran while one was open for 0% -> 0% of each run, Pallas kernels for 21% -> 22%
where the time goes in v8:
time: 41.8 us; the launch traced here: 41.6 us
  blocking collectives  13.3 us (32%)
  Pallas kernels  10.7 us (26%)
  starting transfers between devices  10.4 us (25%)
  waiting for transfers between devices  7.18 us (17%)
    all_to_all x1, blocking collectives, local(): parts = lax.all_to_all(parts, ('gx', 'gy'), 0, 0, tiled=True)  13.3 us
    pallas_call x3, Pallas kernels, energies(): kernel(name, partial(energy_kernel, low, high, end), outs + (planes(2, ha...  5 us
    ppermute x1, waiting for transfers between devices, local(): halo_swap = lax.ppermute(node_crossed, ('gx', 'gy'), crossed)  4.38 us
    ppermute x1, starting transfers between devices, local(): up = lax.ppermute(zc, 'gx', upward)  4.23 us
    pallas_call x1, Pallas kernels, local(): kernel('krylov_main', partial(main_kernel, modes, layers, cuts), (planes(...  2.31 us
    ppermute x1, waiting for transfers between devices, local(): up = lax.ppermute(zc, 'gx', upward)  1.78 us
    pallas_call x1, Pallas kernels, local(): kernel('first_layer', first_kernel, (planes(group + 2, half), planes(grou...  1.67 us
    ppermute x1, starting transfers between devices, local(): ghost_swap = lax.ppermute(ghost_mass, 'gy', across)  1.37 us
  transfers between devices with their start and end apart: 8, of which 4 were waited for; matrix products, arithmetic and copies ran while one was open for 0% of the time, Pallas kernels for 22%

profile of v8, /device:TPU:0, one launch (start us, length us, event | category | flops | bytes accessed | tf_op | source)
XLA Modules:
  0.0 41.6 jit_solution(7124613111551421587)
XLA Ops:
  0.0 0.0 copy-start
  0.0 0.5 %collective-permute-start = (f32[18,8,16,256]{3,2,1,0:T(8,128)}, f32[18,8,16,256]{3,2,1,0:T(8,128)S(1)}, u32[]{:S(2)}, u32[]{:S(2)}) collective-permute-start(f32[18,8,16,256]{3,2,1,0:T(8,128)} %modes.1), channel_id=1, source_target_pairs={{0,1},{1,0},{2,3},{3,2},{4,5},{5,4},{6,7},{7,6},{8,9},{9,8},{10,11... | collective-permute-start | bytes 7077896 | tf_op jit(solution)/shard_map/ppermute | solution.py:551
  0.5 1.7 %first_layer.1 = (f32[11,16,256]{2,1,0:T(8,128)S(1)}, f32[9,16,256]{2,1,0:T(8,128)S(1)}, f32[16,16,256]{2,1,0:T(8,128)S(1)}, f32[9,8,16,256]{3,2,1,0:T(8,128)S(1)}) custom-call(f32[18,8,16,256]{3,2,1,0:T(8,128)} %modes.1, f32[8,16,256]{2,1,0:T(8,128)} %density.1, f32[8,16,256]{2,1,0:T(8,128)} %mass.1, s32[8,16,256]{2,1,0:T(8,128)} %passive.1), custom_call_target="tpu_custom_call" | custom-call | flops 1048576 | bytes 1048576 | tf_op jit(solution)/shard_map/first_layer/pallas_call | solution.py:533
  2.1 0.1 collective-permute-start.1
  2.3 1.3 %collective-permute-start.2 = (f32[11,16,256]{2,1,0:T(8,128)S(1)}, f32[11,16,256]{2,1,0:T(8,128)S(1)}, u32[]{:S(2)}, u32[]{:S(2)}) collective-permute-start(f32[11,16,256]{2,1,0:T(8,128)S(1)} %get-tuple-element.28), channel_id=1, source_target_pairs={{2,0},{3,1},{4,2},{5,3},{6,4},{7,5},{8,6},{9,7},{10,8},{11,9},{12,... | collective-permute-start | bytes 540680 | tf_op jit(solution)/shard_map/ppermute | solution.py:554
  3.5 1.3 %collective-permute-start.3 = (f32[9,16,256]{2,1,0:T(8,128)S(1)}, f32[9,16,256]{2,1,0:T(8,128)S(1)}, u32[]{:S(2)}, u32[]{:S(2)}) collective-permute-start(f32[9,16,256]{2,1,0:T(8,128)S(1)} %get-tuple-element.29), channel_id=1, source_target_pairs={{2,1},{3,0},{4,3},{5,2},{6,5},{7,4},{8,7},{9,6},{10,9},{11,8},{12,... | collective-permute-start | bytes 442376 | tf_op jit(solution)/shard_map/ppermute | solution.py:555
  4.8 0.1 collective-permute-done.1.refs_4_
  5.0 0.0 collective-permute-done.refs_2_
  5.0 0.0 copy-done
  5.0 1.9 %energies_first.1 = (f32[9,32,256]{2,1,0:T(8,128)S(1)}, f32[3,32,256]{2,1,0:T(8,128)S(1)}) custom-call(f32[1,6]{1,0:T(1,128)S(1)} %bitcast.1, f32[9,8,16,256]{3,2,1,0:T(8,128)S(1)} %get-tuple-element.24.refs_1_, f32[18,8,16,256]{3,2,1,0:T(8,128)S(1)} %collective-permute-done.refs_2_, f32[16,16,256]{2,1,0:T(8,128)S(1)} %get-tuple-element.25.refs_3_, ...), custom_call_target="tpu_custom_call" | custom-call | flops 629145600 | bytes 1048576 | tf_op jit(solution)/shard_map/energies_first/pallas_call | solution.py:563
  6.9 1.3 %collective-permute-start.5 = (f32[9,32,256]{2,1,0:T(8,128)S(1)}, f32[9,32,256]{2,1,0:T(8,128)S(1)}, u32[]{:S(2)}, u32[]{:S(2)}) collective-permute-start(f32[9,32,256]{2,1,0:T(8,128)S(1)} %get-tuple-element.26.za), channel_id=1, source_target_pairs={{2,0},{4,2},{6,4},{8,6},{10,8},{12,10},{14,12},{3,1},{5,3},{7,5},{... | collective-permute-start | bytes 884744 | tf_op jit(solution)/shard_map/ppermute | solution.py:577
  8.2 1.8 %energies_inner.1 = (f32[9,32,256]{2,1,0:T(8,128)S(1)}, f32[3,32,256]{2,1,0:T(8,128)S(1)}) custom-call(f32[1,6]{1,0:T(1,128)S(1)} %bitcast.2, f32[9,8,16,256]{3,2,1,0:T(8,128)S(1)} %get-tuple-element.24.refs_1_, f32[18,8,16,256]{3,2,1,0:T(8,128)S(1)} %collective-permute-done.refs_2_, f32[16,16,256]{2,1,0:T(8,128)S(1)} %get-tuple-element.25.refs_3_, ...), custom_call_target="tpu_custom_call" | custom-call | flops 629145600 | bytes 1048576 | tf_op jit(solution)/shard_map/energies_inner/pallas_call | solution.py:563
  10.0 4.4 %collective-permute-done.3.refs_6_ = f32[9,16,256]{2,1,0:T(8,128)S(1)} collective-permute-done((f32[9,16,256]{2,1,0:T(8,128)S(1)}, f32[9,16,256]{2,1,0:T(8,128)S(1)}, u32[]{:S(2)}, u32[]{:S(2)}) %collective-permute-start.3) | collective-permute-done | bytes 147488 | tf_op jit(solution)/shard_map/ppermute | solution.py:555
  14.4 0.0 collective-permute-done.2.refs_5_
  14.4 1.3 %energies_last.1 = (f32[7,32,256]{2,1,0:T(8,128)S(1)}, f32[2,32,256]{2,1,0:T(8,128)S(1)}, f32[2,16,256]{2,1,0:T(8,128)S(1)}) custom-call(f32[1,6]{1,0:T(1,128)S(1)} %bitcast.3, f32[9,8,16,256]{3,2,1,0:T(8,128)S(1)} %get-tuple-element.24.refs_1_, f32[18,8,16,256]{3,2,1,0:T(8,128)S(1)} %collective-permute-done.refs_2_, ...), custom_call_target="tpu_custom_call" | custom-call | flops 419430400 | bytes 1048576 | tf_op jit(solution)/shard_map/energies_last/pallas_call | solution.py:563
  15.7 4.2 %collective-permute-start.4 = (f32[7,32,256]{2,1,0:T(8,128)S(1)}, f32[7,32,256]{2,1,0:T(8,128)S(1)}, u32[]{:S(2)}, u32[]{:S(2)}) collective-permute-start(f32[7,32,256]{2,1,0:T(8,128)S(1)} %get-tuple-element.31.zc), channel_id=1, source_target_pairs={{0,2},{2,4},{4,6},{6,8},{8,10},{10,12},{12,14},{1,3},{3,5},{5,7},{... | collective-permute-start | bytes 688136 | tf_op jit(solution)/shard_map/ppermute | solution.py:580
  19.9 1.4 %collective-permute-start.6 = (f32[2,16,256]{2,1,0:T(8,128)S(1)}, f32[2,16,256]{2,1,0:T(8,128)S(1)}, u32[]{:S(2)}, u32[]{:S(2)}) collective-permute-start(f32[2,16,256]{2,1,0:T(8,128)S(1)} %get-tuple-element.34.ghost_mass), channel_id=1, source_target_pairs={{0,1},{1,0},{2,3},{3,2},{4,5},{5,4},{6,7},{7,6},{8,9},{9,8},{10,11... | collective-permute-start | bytes 98312 | tf_op jit(solution)/shard_map/ppermute | solution.py:581
  21.3 0.9 %collective-permute-done.6.ghost_swap = f32[2,16,256]{2,1,0:T(8,128)S(1)} collective-permute-done((f32[2,16,256]{2,1,0:T(8,128)S(1)}, f32[2,16,256]{2,1,0:T(8,128)S(1)}, u32[]{:S(2)}, u32[]{:S(2)}) %collective-permute-start.6) | collective-permute-done | bytes 32800 | tf_op jit(solution)/shard_map/ppermute | solution.py:581
  22.2 0.0 collective-permute-done.5.down
  22.2 2.3 %krylov_main.1 = (f32[27,32,256]{2,1,0:T(8,128)S(1)}, f32[21,32,256]{2,1,0:T(8,128)S(1)}, f32[18,8,128]{2,1,0:T(8,128)S(1)}, f32[72,16,256]{2,1,0:T(8,128)S(1)}) custom-call(f32[9,32,256]{2,1,0:T(8,128)S(1)} %get-tuple-element.26.za, f32[9,32,256]{2,1,0:T(8,128)S(1)} %get-tuple-element.32.zb, f32[7,32,256]{2,1,0:T(8,128)S(1)} %get-tuple-element.31.zc, ...), custom_call_target="tpu_custom_call" | custom-call | flops 419430400 | bytes 1048576 | tf_op jit(solution)/shard_map/krylov_main/pallas_call | solution.py:585
  24.5 1.8 %collective-permute-done.4.up = f32[7,32,256]{2,1,0:T(8,128)S(1)} collective-permute-done((f32[7,32,256]{2,1,0:T(8,128)S(1)}, f32[7,32,256]{2,1,0:T(8,128)S(1)}, u32[]{:S(2)}, u32[]{:S(2)}) %collective-permute-start.4) | collective-permute-done | bytes 229408 | tf_op jit(solution)/shard_map/ppermute | solution.py:580
  26.3 0.6 %krylov_left.1 = (f32[6,32,256]{2,1,0:T(8,128)S(1)}, f32[6,32,256]{2,1,0:T(8,128)S(1)}, f32[72,16,256]{2,1,0:T(8,128)S(1)}, f32[16,8,128]{2,1,0:T(8,128)S(1)}) custom-call(f32[9,32,256]{2,1,0:T(8,128)S(1)} %get-tuple-element.26.za, f32[3,32,256]{2,1,0:T(8,128)S(1)} %get-tuple-element.27.refs_5_.ma, ...), custom_call_target="tpu_custom_call", output_to_operand_aliasing={{2}: (6, {})} | custom-call | flops 209715200 | bytes 1048576 | tf_op jit(solution)/shard_map/krylov_left/pallas_call | solution.py:594
  26.9 0.4 collective-permute-start.7
  27.3 13.3 %all_to_all.5.parts = f32[16,8,128]{2,1,0:T(8,128)S(1)} all-to-all(f32[16,8,128]{2,1,0:T(8,128)S(1)} %get-tuple-element.39), channel_id=1, replica_groups=mesh['grp'=2,'gx'=8,'gy'=2] {'gx','gy'}, dimensions={0} | all-to-all | bytes 131072 | tf_op jit(solution)/shard_map/all_to_all | solution.py:610
  40.5 0.0 collective-permute-done.7.swap
  40.5 1.1 %combine.1 = f32[6,8,16,256]{3,2,1,0:T(8,128)} custom-call(f32[16,8,128]{2,1,0:T(8,128)S(1)} %all_to_all.5.parts, f32[9,32,256]{2,1,0:T(8,128)S(1)} %get-tuple-element.26.za, f32[9,32,256]{2,1,0:T(8,128)S(1)} %get-tuple-element.32.zb, f32[7,32,256]{2,1,0:T(8,128)S(1)} %get-tuple-element.31.zc, f32[27,32,256]{2,1,0:T(8,128)S(1)} %get-tuple-element.35.ones_in, ...), custom_call_target="tpu_custom_call" | custom-call | flops 104857600 | bytes 1048576 | tf_op jit(solution)/shard_map/combine/pallas_call | solution.py:612
Async XLA Ops:
  0.0 5.0 %copy-start = (f32[6]{0:T(128)S(1)}, f32[6]{0:T(128)}, u32[]{:S(2)}) copy-start(f32[6]{0:T(128)} %param.6) | copy-start | bytes 76
  0.0 5.0 %collective-permute-start = (f32[18,8,16,256]{3,2,1,0:T(8,128)}, f32[18,8,16,256]{3,2,1,0:T(8,128)S(1)}, u32[]{:S(2)}, u32[]{:S(2)}) collective-permute-start(f32[18,8,16,256]{3,2,1,0:T(8,128)} %modes.1), channel_id=1, source_target_pairs={{0,1},{1,0},{2,3},{3,2},{4,5},{5,4},{6,7},{7,6},{8,9},{9,8},{10,11... | collective-permute-start | bytes 7077896 | tf_op jit(solution)/shard_map/ppermute | solution.py:551
  2.1 2.9 %collective-permute-start.1 = (f32[16,16,256]{2,1,0:T(8,128)S(1)}, f32[16,16,256]{2,1,0:T(8,128)S(1)}, u32[]{:S(2)}, u32[]{:S(2)}) collective-permute-start(f32[16,16,256]{2,1,0:T(8,128)S(1)} %get-tuple-element.25.refs_3_), channel_id=1, source_target_pairs={{0,1},{1,0},{2,3},{3,2},{4,5},{5,4},{6,7},{7,6},{8,9},{9,8},{10,11... | collective-permute-start | bytes 786440 | tf_op jit(solution)/shard_map/ppermute | solution.py:551
  2.3 12.1 %collective-permute-start.2 = (f32[11,16,256]{2,1,0:T(8,128)S(1)}, f32[11,16,256]{2,1,0:T(8,128)S(1)}, u32[]{:S(2)}, u32[]{:S(2)}) collective-permute-start(f32[11,16,256]{2,1,0:T(8,128)S(1)} %get-tuple-element.28), channel_id=1, source_target_pairs={{2,0},{3,1},{4,2},{5,3},{6,4},{7,5},{8,6},{9,7},{10,8},{11,9},{12,... | collective-permute-start | bytes 540680 | tf_op jit(solution)/shard_map/ppermute | solution.py:554
  3.5 10.8 %collective-permute-start.3 = (f32[9,16,256]{2,1,0:T(8,128)S(1)}, f32[9,16,256]{2,1,0:T(8,128)S(1)}, u32[]{:S(2)}, u32[]{:S(2)}) collective-permute-start(f32[9,16,256]{2,1,0:T(8,128)S(1)} %get-tuple-element.29), channel_id=1, source_target_pairs={{2,1},{3,0},{4,3},{5,2},{6,5},{7,4},{8,7},{9,6},{10,9},{11,8},{12,... | collective-permute-start | bytes 442376 | tf_op jit(solution)/shard_map/ppermute | solution.py:555
  6.9 15.3 %collective-permute-start.5 = (f32[9,32,256]{2,1,0:T(8,128)S(1)}, f32[9,32,256]{2,1,0:T(8,128)S(1)}, u32[]{:S(2)}, u32[]{:S(2)}) collective-permute-start(f32[9,32,256]{2,1,0:T(8,128)S(1)} %get-tuple-element.26.za), channel_id=1, source_target_pairs={{2,0},{4,2},{6,4},{8,6},{10,8},{12,10},{14,12},{3,1},{5,3},{7,5},{... | collective-permute-start | bytes 884744 | tf_op jit(solution)/shard_map/ppermute | solution.py:577
  15.7 10.6 %collective-permute-start.4 = (f32[7,32,256]{2,1,0:T(8,128)S(1)}, f32[7,32,256]{2,1,0:T(8,128)S(1)}, u32[]{:S(2)}, u32[]{:S(2)}) collective-permute-start(f32[7,32,256]{2,1,0:T(8,128)S(1)} %get-tuple-element.31.zc), channel_id=1, source_target_pairs={{0,2},{2,4},{4,6},{6,8},{8,10},{10,12},{12,14},{1,3},{3,5},{5,7},{... | collective-permute-start | bytes 688136 | tf_op jit(solution)/shard_map/ppermute | solution.py:580
  19.9 2.2 %collective-permute-start.6 = (f32[2,16,256]{2,1,0:T(8,128)S(1)}, f32[2,16,256]{2,1,0:T(8,128)S(1)}, u32[]{:S(2)}, u32[]{:S(2)}) collective-permute-start(f32[2,16,256]{2,1,0:T(8,128)S(1)} %get-tuple-element.34.ghost_mass), channel_id=1, source_target_pairs={{0,1},{1,0},{2,3},{3,2},{4,5},{5,4},{6,7},{7,6},{8,9},{9,8},{10,11... | collective-permute-start | bytes 98312 | tf_op jit(solution)/shard_map/ppermute | solution.py:581
  26.9 13.6 %collective-permute-start.7 = (f32[72,16,256]{2,1,0:T(8,128)S(1)}, f32[72,16,256]{2,1,0:T(8,128)S(1)}, u32[]{:S(2)}, u32[]{:S(2)}) collective-permute-start(f32[72,16,256]{2,1,0:T(8,128)S(1)} %get-tuple-element.42), channel_id=1, source_target_pairs={{0,1},{1,0},{2,3},{3,2},{4,5},{5,4},{6,7},{7,6},{8,9},{9,8},{10,11... | collective-permute-start | bytes 3538952 | tf_op jit(solution)/shard_map/ppermute | solution.py:609

commit v9 on v8

--- a/solution.py
+++ b/solution.py
@@ -159,7 +159,7 @@
     return pl.multiple_of(core * half, half), pl.multiple_of((1 - core) * half, half)
 
 
-def first_kernel(modes, density, mass, passive, straight, crossed, fields, own, signed, flags, sems):
+def first_kernel(modes, density, mass, passive, straight, crossed, fields, signed, flags, sems):
     group = modes.shape[0] // 2
     layers = density.shape[0]
     here, _, _ = position()
@@ -167,7 +167,6 @@
     for target, core in ((straight, here), (crossed, 1 - here)):
         moves.append((modes.at[pl.ds(core * group, group), 0], target.at[pl.ds(0, group)]))
     moves.append((mass.at[pl.ds(0, 2)], straight.at[pl.ds(group, 2)]))
-    moves.append((modes.at[pl.ds(here * group, group)], own))
     copies = [pltpu.make_async_copy(*move, sems.at[i]) for i, move in enumerate(moves)]
     for copy in copies:
         copy.start()
@@ -186,7 +185,8 @@
         z_out, mass_out, ghost_mass, floats, sums = refs[-5:]
     else:
         z_out, mass_out, floats, sums = refs[-4:]
-    group, layers, half, depth = modes.shape
+    layers, half, depth = modes.shape[1:]
+    group = modes.shape[0] // 2
     width, count = 2 * half, high - low
     core, first, last = position()
     start = core * group
@@ -214,7 +214,7 @@
     def node(row, x):
         if x == layers:
             return whole(halo[row], halo_swap[row])
-        return whole(modes[row, x], modes_swap[start + row, x])
+        return whole(modes[start + row, x], modes_swap[start + row, x])
 
     ring = sums.shape[0]
 
@@ -530,25 +530,20 @@
         )
 
     stored = [pltpu.with_memory_space_constraint(x, pltpu.HBM) for x in (mode_shapes, density, filter_mass, passive)]
-    node, node_crossed, fields, own = kernel(
+    node, node_crossed, fields = kernel(
         "first_layer",
         first_kernel,
-        (
-            planes(group + 2, half),
-            planes(group, half),
-            planes(2 * layers, half),
-            jax.ShapeDtypeStruct((group, layers, half, depth), f32),
-        ),
+        (planes(group + 2, half), planes(group, half), planes(2 * layers, half)),
         [anywhere] * 4,
         [
             pltpu.VMEM((layers, half, depth), f32),
             pltpu.VMEM((layers, half, depth), jnp.int32),
-            pltpu.SemaphoreType.DMA((7,)),
+            pltpu.SemaphoreType.DMA((6,)),
         ],
         4,
         1,
     )(*stored)
-    operands = [own, lax.ppermute(mode_shapes, "gy", across), fields, lax.ppermute(fields, "gy", across)]
+    operands = [mode_shapes, lax.ppermute(mode_shapes, "gy", across), fields, lax.ppermute(fields, "gy", across)]
     straight = [(2 * i + c, 2 * i - 2 + c) for i in range(1, count) for c in (0, 1)]
     crossed = [(2 * i + c, 2 * i - 1 - c) for i in range(1, count) for c in (0, 1)]
     halo = lax.ppermute(node, ("gx", "gy"), straight)

time: 41.8 us -> 41.4 us (level)
  transfers between devices with their start and end apart: 8 -> 8, of which waited for: 4 -> 4; matrix products, arithmetic and copies ran while one was open for 0% -> 0% of each run, Pallas kernels for 22% -> 21%
where the time goes in v9:
time: 41.4 us; the launch traced here: 41.2 us
  blocking collectives  13.1 us (32%)
  Pallas kernels  10.5 us (25%)
  starting transfers between devices  10.3 us (25%)
  waiting for transfers between devices  7.23 us (17%)
    all_to_all x1, blocking collectives, local(): parts = lax.all_to_all(parts, ('gx', 'gy'), 0, 0, tiled=True)  13.1 us
    pallas_call x3, Pallas kernels, energies(): kernel(name, partial(energy_kernel, low, high, end), outs + (planes(2, ha...  4.98 us
    ppermute x1, starting transfers between devices, local(): up = lax.ppermute(zc, 'gx', upward)  4.23 us
    ppermute x1, waiting for transfers between devices, local(): halo_swap = lax.ppermute(node_crossed, ('gx', 'gy'), crossed)  4.18 us
    pallas_call x1, Pallas kernels, local(): kernel('krylov_main', partial(main_kernel, modes, layers, cuts), (planes(...  2.33 us
    ppermute x1, waiting for transfers between devices, local(): up = lax.ppermute(zc, 'gx', upward)  1.77 us
    pallas_call x1, Pallas kernels, local(): kernel('first_layer', first_kernel, (planes(group + 2, half), planes(grou...  1.44 us
    ppermute x1, starting transfers between devices, local(): halo = lax.ppermute(node, ('gx', 'gy'), straight)  1.29 us
  transfers between devices with their start and end apart: 8, of which 4 were waited for; matrix products, arithmetic and copies ran while one was open for 0% of the time, Pallas kernels for 21%

profile of v9, /device:TPU:0, one launch (start us, length us, event | category | flops | bytes accessed | tf_op | source)
XLA Modules:
  0.0 41.2 jit_solution(3176386880709034767)
XLA Ops:
  0.0 0.0 copy-start
  0.0 0.0 copy-start.1
  0.0 0.5 %collective-permute-start = (f32[18,8,16,256]{3,2,1,0:T(8,128)}, f32[18,8,16,256]{3,2,1,0:T(8,128)S(1)}, u32[]{:S(2)}, u32[]{:S(2)}) collective-permute-start(f32[18,8,16,256]{3,2,1,0:T(8,128)} %refs_1_.5), channel_id=1, source_target_pairs={{0,1},{1,0},{2,3},{3,2},{4,5},{5,4},{6,7},{7,6},{8,9},{9,8},{10,11... | collective-permute-start | bytes 7077896 | tf_op jit(solution)/shard_map/ppermute | solution.py:546
  0.5 1.4 %first_layer.1 = (f32[11,16,256]{2,1,0:T(8,128)S(1)}, f32[9,16,256]{2,1,0:T(8,128)S(1)}, f32[16,16,256]{2,1,0:T(8,128)S(1)}) custom-call(f32[18,8,16,256]{3,2,1,0:T(8,128)} %refs_1_.5, f32[8,16,256]{2,1,0:T(8,128)} %density.1, f32[8,16,256]{2,1,0:T(8,128)} %mass.1, s32[8,16,256]{2,1,0:T(8,128)} %passive.1), custom_call_target="tpu_custom_call" | custom-call | flops 1048576 | bytes 1048576 | tf_op jit(solution)/shard_map/first_layer/pallas_call | solution.py:533
  1.9 0.1 collective-permute-start.1
  2.0 1.3 %collective-permute-start.2 = (f32[11,16,256]{2,1,0:T(8,128)S(1)}, f32[11,16,256]{2,1,0:T(8,128)S(1)}, u32[]{:S(2)}, u32[]{:S(2)}) collective-permute-start(f32[11,16,256]{2,1,0:T(8,128)S(1)} %get-tuple-element.26), channel_id=1, source_target_pairs={{2,0},{3,1},{4,2},{5,3},{6,4},{7,5},{8,6},{9,7},{10,8},{11,9},{12,... | collective-permute-start | bytes 540680 | tf_op jit(solution)/shard_map/ppermute | solution.py:549
  3.3 1.3 %collective-permute-start.3 = (f32[9,16,256]{2,1,0:T(8,128)S(1)}, f32[9,16,256]{2,1,0:T(8,128)S(1)}, u32[]{:S(2)}, u32[]{:S(2)}) collective-permute-start(f32[9,16,256]{2,1,0:T(8,128)S(1)} %get-tuple-element.27), channel_id=1, source_target_pairs={{2,1},{3,0},{4,3},{5,2},{6,5},{7,4},{8,7},{9,6},{10,9},{11,8},{12,... | collective-permute-start | bytes 442376 | tf_op jit(solution)/shard_map/ppermute | solution.py:550
  4.6 0.4 collective-permute-done.1.refs_4_
  5.0 0.0 collective-permute-done.refs_2_
  5.0 0.0 copy-done
  5.0 0.0 copy-done.1
  5.0 1.9 %energies_first.1 = (f32[9,32,256]{2,1,0:T(8,128)S(1)}, f32[3,32,256]{2,1,0:T(8,128)S(1)}) custom-call(f32[1,6]{1,0:T(1,128)S(1)} %bitcast.1, f32[18,8,16,256]{3,2,1,0:T(8,128)S(1)} %copy-done, f32[18,8,16,256]{3,2,1,0:T(8,128)S(1)} %collective-permute-done.refs_2_, f32[16,16,256]{2,1,0:T(8,128)S(1)} %get-tuple-element.23.refs_3_, ...), custom_call_target="tpu_custom_call" | custom-call | flops 629145600 | bytes 1048576 | tf_op jit(solution)/shard_map/energies_first/pallas_call | solution.py:558
  6.9 1.3 %collective-permute-start.5 = (f32[9,32,256]{2,1,0:T(8,128)S(1)}, f32[9,32,256]{2,1,0:T(8,128)S(1)}, u32[]{:S(2)}, u32[]{:S(2)}) collective-permute-start(f32[9,32,256]{2,1,0:T(8,128)S(1)} %get-tuple-element.24.za), channel_id=1, source_target_pairs={{2,0},{4,2},{6,4},{8,6},{10,8},{12,10},{14,12},{3,1},{5,3},{7,5},{... | collective-permute-start | bytes 884744 | tf_op jit(solution)/shard_map/ppermute | solution.py:572
  8.2 1.8 %energies_inner.1 = (f32[9,32,256]{2,1,0:T(8,128)S(1)}, f32[3,32,256]{2,1,0:T(8,128)S(1)}) custom-call(f32[1,6]{1,0:T(1,128)S(1)} %bitcast.2, f32[18,8,16,256]{3,2,1,0:T(8,128)S(1)} %copy-done, f32[18,8,16,256]{3,2,1,0:T(8,128)S(1)} %collective-permute-done.refs_2_, f32[16,16,256]{2,1,0:T(8,128)S(1)} %get-tuple-element.23.refs_3_, ...), custom_call_target="tpu_custom_call" | custom-call | flops 629145600 | bytes 1048576 | tf_op jit(solution)/shard_map/energies_inner/pallas_call | solution.py:558
  10.0 4.2 %collective-permute-done.3.refs_6_ = f32[9,16,256]{2,1,0:T(8,128)S(1)} collective-permute-done((f32[9,16,256]{2,1,0:T(8,128)S(1)}, f32[9,16,256]{2,1,0:T(8,128)S(1)}, u32[]{:S(2)}, u32[]{:S(2)}) %collective-permute-start.3) | collective-permute-done | bytes 147488 | tf_op jit(solution)/shard_map/ppermute | solution.py:550
  14.2 0.0 collective-permute-done.2.refs_5_
  14.2 1.3 %energies_last.1 = (f32[7,32,256]{2,1,0:T(8,128)S(1)}, f32[2,32,256]{2,1,0:T(8,128)S(1)}, f32[2,16,256]{2,1,0:T(8,128)S(1)}) custom-call(f32[1,6]{1,0:T(1,128)S(1)} %bitcast.3, f32[18,8,16,256]{3,2,1,0:T(8,128)S(1)} %copy-done, f32[18,8,16,256]{3,2,1,0:T(8,128)S(1)} %collective-permute-done.refs_2_, f32[16,16,256]{2,1,0:T(8,128)S(1)} %get-tuple-element.23.refs_3_, ...), custom_call_target="tpu_custom_call" | custom-call | flops 419430400 | bytes 1048576 | tf_op jit(solution)/shard_map/energies_last/pallas_call | solution.py:558
  15.5 4.2 %collective-permute-start.4 = (f32[7,32,256]{2,1,0:T(8,128)S(1)}, f32[7,32,256]{2,1,0:T(8,128)S(1)}, u32[]{:S(2)}, u32[]{:S(2)}) collective-permute-start(f32[7,32,256]{2,1,0:T(8,128)S(1)} %get-tuple-element.29.zc), channel_id=1, source_target_pairs={{0,2},{2,4},{4,6},{6,8},{8,10},{10,12},{12,14},{1,3},{3,5},{5,7},{... | collective-permute-start | bytes 688136 | tf_op jit(solution)/shard_map/ppermute | solution.py:575
  19.7 1.3 %collective-permute-start.6 = (f32[2,16,256]{2,1,0:T(8,128)S(1)}, f32[2,16,256]{2,1,0:T(8,128)S(1)}, u32[]{:S(2)}, u32[]{:S(2)}) collective-permute-start(f32[2,16,256]{2,1,0:T(8,128)S(1)} %get-tuple-element.32.ghost_mass), channel_id=1, source_target_pairs={{0,1},{1,0},{2,3},{3,2},{4,5},{5,4},{6,7},{7,6},{8,9},{9,8},{10,11... | collective-permute-start | bytes 98312 | tf_op jit(solution)/shard_map/ppermute | solution.py:576
  21.0 0.9 %collective-permute-done.6.ghost_swap = f32[2,16,256]{2,1,0:T(8,128)S(1)} collective-permute-done((f32[2,16,256]{2,1,0:T(8,128)S(1)}, f32[2,16,256]{2,1,0:T(8,128)S(1)}, u32[]{:S(2)}, u32[]{:S(2)}) %collective-permute-start.6) | collective-permute-done | bytes 32800 | tf_op jit(solution)/shard_map/ppermute | solution.py:576
  21.9 0.0 collective-permute-done.5.down
  21.9 2.3 %krylov_main.1 = (f32[27,32,256]{2,1,0:T(8,128)S(1)}, f32[21,32,256]{2,1,0:T(8,128)S(1)}, f32[18,8,128]{2,1,0:T(8,128)S(1)}, f32[72,16,256]{2,1,0:T(8,128)S(1)}) custom-call(f32[9,32,256]{2,1,0:T(8,128)S(1)} %get-tuple-element.24.za, f32[9,32,256]{2,1,0:T(8,128)S(1)} %get-tuple-element.30.zb, f32[7,32,256]{2,1,0:T(8,128)S(1)} %get-tuple-element.29.zc, ...), custom_call_target="tpu_custom_call" | custom-call | flops 419430400 | bytes 1048576 | tf_op jit(solution)/shard_map/krylov_main/pallas_call | solution.py:580
  24.2 1.8 %collective-permute-done.4.up = f32[7,32,256]{2,1,0:T(8,128)S(1)} collective-permute-done((f32[7,32,256]{2,1,0:T(8,128)S(1)}, f32[7,32,256]{2,1,0:T(8,128)S(1)}, u32[]{:S(2)}, u32[]{:S(2)}) %collective-permute-start.4) | collective-permute-done | bytes 229408 | tf_op jit(solution)/shard_map/ppermute | solution.py:575
  26.0 0.6 %krylov_left.1 = (f32[6,32,256]{2,1,0:T(8,128)S(1)}, f32[6,32,256]{2,1,0:T(8,128)S(1)}, f32[72,16,256]{2,1,0:T(8,128)S(1)}, f32[16,8,128]{2,1,0:T(8,128)S(1)}) custom-call(f32[9,32,256]{2,1,0:T(8,128)S(1)} %get-tuple-element.24.za, f32[3,32,256]{2,1,0:T(8,128)S(1)} %get-tuple-element.25.refs_5_.ma, ...), custom_call_target="tpu_custom_call", output_to_operand_aliasing={{2}: (6, {})} | custom-call | flops 209715200 | bytes 1048576 | tf_op jit(solution)/shard_map/krylov_left/pallas_call | solution.py:589
  26.6 0.4 collective-permute-start.7
  27.0 13.1 %all_to_all.5.parts = f32[16,8,128]{2,1,0:T(8,128)S(1)} all-to-all(f32[16,8,128]{2,1,0:T(8,128)S(1)} %get-tuple-element.37), channel_id=1, replica_groups=mesh['grp'=2,'gx'=8,'gy'=2] {'gx','gy'}, dimensions={0} | all-to-all | bytes 131072 | tf_op jit(solution)/shard_map/all_to_all | solution.py:605
  40.1 0.0 collective-permute-done.7.swap
  40.1 1.1 %combine.1 = f32[6,8,16,256]{3,2,1,0:T(8,128)} custom-call(f32[16,8,128]{2,1,0:T(8,128)S(1)} %all_to_all.5.parts, f32[9,32,256]{2,1,0:T(8,128)S(1)} %get-tuple-element.24.za, f32[9,32,256]{2,1,0:T(8,128)S(1)} %get-tuple-element.30.zb, f32[7,32,256]{2,1,0:T(8,128)S(1)} %get-tuple-element.29.zc, f32[27,32,256]{2,1,0:T(8,128)S(1)} %get-tuple-element.33.ones_in, ...), custom_call_target="tpu_custom_call" | custom-call | flops 104857600 | bytes 1048576 | tf_op jit(solution)/shard_map/combine/pallas_call | solution.py:607
Async XLA Ops:
  0.0 5.0 %copy-start = (f32[18,8,16,256]{3,2,1,0:T(8,128)S(1)}, f32[18,8,16,256]{3,2,1,0:T(8,128)}, u32[]{:S(2)}) copy-start(f32[18,8,16,256]{3,2,1,0:T(8,128)} %refs_1_.5) | copy-start | bytes 7077892
  0.0 5.0 %copy-start.1 = (f32[6]{0:T(128)S(1)}, f32[6]{0:T(128)}, u32[]{:S(2)}) copy-start(f32[6]{0:T(128)} %param.6) | copy-start | bytes 76
  0.0 5.0 %collective-permute-start = (f32[18,8,16,256]{3,2,1,0:T(8,128)}, f32[18,8,16,256]{3,2,1,0:T(8,128)S(1)}, u32[]{:S(2)}, u32[]{:S(2)}) collective-permute-start(f32[18,8,16,256]{3,2,1,0:T(8,128)} %refs_1_.5), channel_id=1, source_target_pairs={{0,1},{1,0},{2,3},{3,2},{4,5},{5,4},{6,7},{7,6},{8,9},{9,8},{10,11... | collective-permute-start | bytes 7077896 | tf_op jit(solution)/shard_map/ppermute | solution.py:546
  1.9 3.1 %collective-permute-start.1 = (f32[16,16,256]{2,1,0:T(8,128)S(1)}, f32[16,16,256]{2,1,0:T(8,128)S(1)}, u32[]{:S(2)}, u32[]{:S(2)}) collective-permute-start(f32[16,16,256]{2,1,0:T(8,128)S(1)} %get-tuple-element.23.refs_3_), channel_id=1, source_target_pairs={{0,1},{1,0},{2,3},{3,2},{4,5},{5,4},{6,7},{7,6},{8,9},{9,8},{10,11... | collective-permute-start | bytes 786440 | tf_op jit(solution)/shard_map/ppermute | solution.py:546
  2.0 12.2 %collective-permute-start.2 = (f32[11,16,256]{2,1,0:T(8,128)S(1)}, f32[11,16,256]{2,1,0:T(8,128)S(1)}, u32[]{:S(2)}, u32[]{:S(2)}) collective-permute-start(f32[11,16,256]{2,1,0:T(8,128)S(1)} %get-tuple-element.26), channel_id=1, source_target_pairs={{2,0},{3,1},{4,2},{5,3},{6,4},{7,5},{8,6},{9,7},{10,8},{11,9},{12,... | collective-permute-start | bytes 540680 | tf_op jit(solution)/shard_map/ppermute | solution.py:549
  3.3 10.9 %collective-permute-start.3 = (f32[9,16,256]{2,1,0:T(8,128)S(1)}, f32[9,16,256]{2,1,0:T(8,128)S(1)}, u32[]{:S(2)}, u32[]{:S(2)}) collective-permute-start(f32[9,16,256]{2,1,0:T(8,128)S(1)} %get-tuple-element.27), channel_id=1, source_target_pairs={{2,1},{3,0},{4,3},{5,2},{6,5},{7,4},{8,7},{9,6},{10,9},{11,8},{12,... | collective-permute-start | bytes 442376 | tf_op jit(solution)/shard_map/ppermute | solution.py:550
  6.9 15.0 %collective-permute-start.5 = (f32[9,32,256]{2,1,0:T(8,128)S(1)}, f32[9,32,256]{2,1,0:T(8,128)S(1)}, u32[]{:S(2)}, u32[]{:S(2)}) collective-permute-start(f32[9,32,256]{2,1,0:T(8,128)S(1)} %get-tuple-element.24.za), channel_id=1, source_target_pairs={{2,0},{4,2},{6,4},{8,6},{10,8},{12,10},{14,12},{3,1},{5,3},{7,5},{... | collective-permute-start | bytes 884744 | tf_op jit(solution)/shard_map/ppermute | solution.py:572
  15.5 10.5 %collective-permute-start.4 = (f32[7,32,256]{2,1,0:T(8,128)S(1)}, f32[7,32,256]{2,1,0:T(8,128)S(1)}, u32[]{:S(2)}, u32[]{:S(2)}) collective-permute-start(f32[7,32,256]{2,1,0:T(8,128)S(1)} %get-tuple-element.29.zc), channel_id=1, source_target_pairs={{0,2},{2,4},{4,6},{6,8},{8,10},{10,12},{12,14},{1,3},{3,5},{5,7},{... | collective-permute-start | bytes 688136 | tf_op jit(solution)/shard_map/ppermute | solution.py:575
  19.7 2.1 %collective-permute-start.6 = (f32[2,16,256]{2,1,0:T(8,128)S(1)}, f32[2,16,256]{2,1,0:T(8,128)S(1)}, u32[]{:S(2)}, u32[]{:S(2)}) collective-permute-start(f32[2,16,256]{2,1,0:T(8,128)S(1)} %get-tuple-element.32.ghost_mass), channel_id=1, source_target_pairs={{0,1},{1,0},{2,3},{3,2},{4,5},{5,4},{6,7},{7,6},{8,9},{9,8},{10,11... | collective-permute-start | bytes 98312 | tf_op jit(solution)/shard_map/ppermute | solution.py:576
  26.6 13.5 %collective-permute-start.7 = (f32[72,16,256]{2,1,0:T(8,128)S(1)}, f32[72,16,256]{2,1,0:T(8,128)S(1)}, u32[]{:S(2)}, u32[]{:S(2)}) collective-permute-start(f32[72,16,256]{2,1,0:T(8,128)S(1)} %get-tuple-element.40), channel_id=1, source_target_pairs={{0,1},{1,0},{2,3},{3,2},{4,5},{5,4},{6,7},{7,6},{8,9},{9,8},{10,11... | collective-permute-start | bytes 3538952 | tf_op jit(solution)/shard_map/ppermute | solution.py:604
